TPU v7x, 32 devices: a whole 2x2x4 slice. The times are simulated.
32 devices in a mesh: slide: 4 (over x, core), tile: 8 (over z, y).
Axes of the slice: x: 2, y: 2, z: 4, core: 2. Of those that a mesh axis runs over, the one named last changes fastest.
Arguments:
- features: bfloat16 [4, 512, 16, 16, 128], P('slide', 'tile'), may hold values from -6 to 6
- tissue_count: int32 [4, 8], P('slide', 'tile'), may hold values from 0 to 64, as said below
- neighbors: int32 [4, 512, 8], P('slide', 'tile'), may hold values from -1 to 511, as said below
- worker_perm: int32 [4, 8], P('slide'), may hold values from 0 to 7, each once within a row
- rotation: int32 [4], P('slide'), may hold values from 0 to 255
- kernel: bfloat16 [9, 128], replicated, may hold values from -2 to 2
- gain: float32 [128], replicated, may hold values from 0.1 to 1.9
- w_in: bfloat16 [128, 512], replicated, may hold values from -0.5 to 0.5
- w_out: bfloat16 [512, 128], replicated, may hold values from -0.25 to 0.25
- cotangent: float32 [4, 256, 128], P('slide', 'tile'), may hold values from -0.3 to 0.3
Outputs:
- embed: float32 [4, 256, 128], P('slide', 'tile')
- grad_kernel: float32 [9, 128], replicated
- grad_gain: float32 [128], replicated
- grad_in: float32 [128, 512], replicated
- grad_out: float32 [512, 128], replicated
Inputs may be any that keep to these rules, and one draw needn't show every extreme that they name: `tissue_count`: in each group the counts sum to 256. `neighbors`: each entry is -1 or the slot number q * 64 + j of a tissue slot (j below tissue_count of q) of an owner q equal to the slot's own owner or next to it in the same group; slots at or past their owner's count have -1 everywhere.
All inputs are finite; a program needn't handle non-finite values.
Results may differ from a plain program's by a relative error of at most 0.00065.
Values may be sent and summed in bfloat16 or wider, within the bound.
No kernel may reach another device: no remote copies, remote signals or barrier semaphores. Data moves between devices by JAX's collectives and lax.ppermute only.
A program may use at most 64 MiB of HBM per device.

v0:
```python
import math

import jax
import jax.numpy as jnp
from jax import lax
from jax.sharding import PartitionSpec as P


def with_halo(cells, sides, width):
    for axis, dim in sides:
        count = lax.axis_size(axis)
        ends = count - 1
        head = lax.slice_in_dim(cells, 0, width, axis=dim)
        tail = lax.slice_in_dim(cells, cells.shape[dim] - width, cells.shape[dim], axis=dim)
        cells = jnp.concatenate(
            [
                lax.ppermute(tail, axis, [(i, (i + 1) % count) for i in range(ends)]),
                cells,
                lax.ppermute(head, axis, [((i + 1) % count, i) for i in range(ends)]),
            ],
            axis=dim,
        )
    return cells


def border_rows(tiles):
    return jnp.stack([tiles[:, 0], tiles[:, -1], tiles[:, :, 0], tiles[:, :, -1]], axis=1)


def assemble(center, borders, index):
    side = center.shape[1]

    def pick(column, which):
        chosen = index[:, column]
        rows = jnp.take(borders[:, which], jnp.maximum(chosen, 0), axis=0)
        return jnp.where((chosen >= 0)[:, None, None], rows, jnp.zeros_like(rows))

    upper = pick(0, 1)
    lower = pick(1, 0)
    left_col = pick(2, 3)
    right_col = pick(3, 2)
    upper_left = pick(4, 1)[:, side - 1]
    upper_right = pick(5, 1)[:, 0]
    lower_left = pick(6, 0)[:, side - 1]
    lower_right = pick(7, 0)[:, 0]
    top = jnp.concatenate([upper_left[:, None], upper, upper_right[:, None]], axis=1)
    bottom = jnp.concatenate([lower_left[:, None], lower, lower_right[:, None]], axis=1)
    middle = jnp.concatenate([left_col[:, :, None], center, right_col[:, :, None]], axis=2)
    return jnp.concatenate([top[:, None], middle, bottom[:, None]], axis=1)


def gelu_value(before):
    return 0.5 * before * (1.0 + lax.erf(before * 0.7071067811865476))


def gelu_slope(before):
    return (
        0.5 * (1.0 + lax.erf(before * 0.7071067811865476))
        + before * jnp.exp(-0.5 * before * before) * 0.3989422804014327
    )


def block_section(padded, cot_rows, kernel, gain, w_in, w_out):
    count = padded.shape[0]
    side = padded.shape[1] - 2
    chans = padded.shape[3]
    pixels = side * side
    kernel_wide = kernel.astype(jnp.float32)
    shifted = [
        padded[:, row : row + side, col : col + side, :] for row in range(3) for col in range(3)
    ]
    depth = shifted[0].astype(jnp.float32) * kernel_wide[0]
    for offset in range(1, 9):
        depth = depth + shifted[offset].astype(jnp.float32) * kernel_wide[offset]
    depth = depth.reshape(count * pixels, chans)
    channel_mean = jnp.mean(depth, axis=1, keepdims=True)
    centered = depth - channel_mean
    inverse = lax.rsqrt(jnp.mean(centered * centered, axis=1, keepdims=True) + 1e-06)
    unit_values = centered * inverse
    normed = (unit_values * gain).astype(jnp.bfloat16)
    before = jnp.dot(normed, w_in, preferred_element_type=jnp.float32)
    hidden = before.shape[1]
    activated = gelu_value(before).astype(jnp.bfloat16)
    projected = jnp.dot(activated, w_out, preferred_element_type=jnp.float32)
    center = (
        padded[:, 1 : side + 1, 1 : side + 1, :].astype(jnp.float32).reshape(count * pixels, chans)
    )
    embed = jnp.mean((center + projected).reshape(count, pixels, chans), axis=1)
    grad_embed = cot_rows / pixels
    act_sum = jnp.sum(activated.reshape(count, pixels, hidden).astype(jnp.float32), axis=1)
    grad_out = jnp.dot(act_sum.T, grad_embed, precision=lax.Precision.HIGHEST)
    grad_act = jnp.dot(grad_embed, w_out.astype(jnp.float32).T, precision=lax.Precision.HIGHEST)
    grad_before = (grad_act[:, None, :] * gelu_slope(before).reshape(count, pixels, hidden)).astype(
        jnp.bfloat16
    )
    grad_before = grad_before.reshape(count * pixels, hidden)
    grad_in = jnp.dot(normed.T, grad_before, preferred_element_type=jnp.float32)
    grad_normed = jnp.dot(grad_before, w_in.T, preferred_element_type=jnp.float32)
    grad_gain = jnp.sum(grad_normed * unit_values, axis=0)
    grad_unit = grad_normed * gain
    grad_depth = inverse * (
        grad_unit
        - jnp.mean(grad_unit, axis=1, keepdims=True)
        - unit_values * jnp.mean(grad_unit * unit_values, axis=1, keepdims=True)
    )
    grad_depth = grad_depth.reshape(count, side, side, chans)
    grad_kernel = jnp.stack(
        [
            jnp.sum(grad_depth * shifted[offset].astype(jnp.float32), axis=(0, 1, 2))
            for offset in range(9)
        ]
    )
    return (embed, (grad_kernel, grad_gain, grad_in, grad_out))


def run_blocks(padded, cot_rows, kernel, gain, w_in, w_out, size):
    count = padded.shape[0]
    group = math.gcd(count, size)
    chans = padded.shape[3]
    hidden = w_in.shape[1]
    stacked = padded.reshape((count // group, group) + padded.shape[1:])
    cot_stack = cot_rows.reshape(count // group, group, cot_rows.shape[1])
    initial = (
        jnp.zeros((9, chans), jnp.float32),
        jnp.zeros((chans,), jnp.float32),
        jnp.zeros((chans, hidden), jnp.float32),
        jnp.zeros((hidden, chans), jnp.float32),
    )

    def advance(carry, item):
        embed, grads = block_section(item[0], item[1], kernel, gain, w_in, w_out)
        return (jax.tree.map(lambda left, right: left + right, carry, grads), embed)

    totals, embeds = lax.scan(advance, initial, (stacked, cot_stack))
    return (embeds.reshape(count, chans), totals)


def local(
    features, tissue_count, neighbors, worker_perm, rotation, kernel, gain, w_in, w_out, cotangent
):
    owned = features[0]
    slot_count = owned.shape[0]
    side = owned.shape[1]
    chans = owned.shape[3]
    links = neighbors[0]
    dealing = worker_perm[0]
    turned = rotation[0]
    cot_rows = cotangent[0]
    work_slots = cot_rows.shape[0]
    peers = lax.axis_size("tile")
    own_index = lax.axis_index("tile")
    per_peer = (slot_count + peers - 1) // peers
    group_total = peers * work_slots
    peer_ids = jnp.arange(peers, dtype=jnp.int32)
    rank_ids = jnp.arange(per_peer, dtype=jnp.int32)
    counts_all = lax.all_gather(tissue_count[0], "tile", axis=0, tiled=True)
    group_start = jnp.cumsum(counts_all, dtype=jnp.int32) - counts_all
    own_start = jnp.sum(jnp.where(peer_ids == own_index, group_start, 0))
    own_count = tissue_count[0][0]
    inverse_perm = jnp.sum(
        jnp.where(dealing[None, :] == peer_ids[:, None], peer_ids[None, :], 0), axis=1
    )
    strips = border_rows(owned)
    widened = with_halo(strips, (("tile", 0),), slot_count)
    local_links = jnp.where(links >= 0, links - (own_index - 1) * slot_count, -1)
    padded = assemble(owned, widened, local_links)
    first_slot = jnp.mod(inverse_perm - own_start - turned, peers)
    send_slot = first_slot[:, None] + rank_ids[None, :] * peers
    send_valid = (send_slot < own_count).reshape(-1)
    send_index = jnp.minimum(send_slot, slot_count - 1).reshape(-1)
    own_residue = jnp.sum(jnp.where(peer_ids == own_index, inverse_perm, 0))
    from_slot = (
        jnp.mod(own_residue - group_start - turned, peers)[:, None] + rank_ids[None, :] * peers
    )
    from_valid = from_slot < counts_all[:, None]
    arrival_rank = jnp.mod(group_start[:, None] + from_slot + turned, group_total)
    destination = jnp.where(from_valid, arrival_rank // peers, -1).reshape(-1)
    bucket_ids = jnp.arange(peers * per_peer, dtype=jnp.int32)
    placement = jnp.sum(
        jnp.where(
            destination[None, :] == jnp.arange(work_slots, dtype=jnp.int32)[:, None],
            bucket_ids[None, :],
            0,
        ),
        axis=1,
    )
    outgoing = jnp.where(
        send_valid[:, None, None, None], padded[send_index], jnp.zeros((), jnp.bfloat16)
    )
    outgoing = outgoing.reshape(peers, per_peer, side + 2, side + 2, chans)
    arrived = lax.all_to_all(outgoing, "tile", split_axis=0, concat_axis=0, tiled=True)
    arrived = arrived.reshape(peers * per_peer, side + 2, side + 2, chans)
    embed, grads = run_blocks(arrived[placement], cot_rows, kernel, gain, w_in, w_out, 4)
    summed = lax.psum((grads[0], grads[1], grads[2], grads[3]), ("slide", "tile"))
    return (embed[None], summed[0], summed[1], summed[2], summed[3])


def solution(mesh):
    placed = (
        P("slide", "tile", None, None, None),
        P("slide", "tile"),
        P("slide", "tile", None),
        P("slide", None),
        P("slide"),
        P(),
        P(),
        P(),
        P(),
        P("slide", "tile", None),
    )
    return jax.shard_map(
        local,
        mesh=mesh,
        in_specs=placed,
        out_specs=(P("slide", "tile", None), P(), P(), P(), P()),
        check_vma=False,
    )
```

profile of v0, /device:TPU:0, one launch (start us, length us, event | category | flops | bytes accessed | tf_op | source)
XLA Modules:
  0.0 463.3 jit_solution(10784026200840917766)
XLA Ops:
  7.2 3.3 copy.48
  10.5 1.1 fusion.46
  12.5 4.9 %collective-permute-start = (bf16[64,4,16,128]{3,2,0,1:T(8,128)(2,1)S(1)}, bf16[64,4,16,128]{3,2,0,1:T(8,128)(2,1)S(1)}, u32[]{:S(2)}, u32[]{:S(2)}) collective-permute-start(bf16[64,4,16,128]{3,2,0,1:T(8,128)(2,1)S(1)} %pad_maximum_fusion.2), channel_id=1, source_target_pairs={{0,1},{1,2},{2,3},{3,4},{4,5},{5,6},{6,7},{8,9},{9,10},{10,11},{11... | collective-permute-start | bytes 3145736 | tf_op jit(solution)/shard_map/ppermute | solution.py:17
  17.4 1.3 collective-permute-start.1
  20.8 50.8 %all-reduce = s32[8]{0:T(128)S(1)} all-reduce(s32[8]{0:T(128)S(1)} %bitcast_dynamic-update-slice_fusion.1), channel_id=2, replica_groups=mesh['slide'=4,'tile'=8] {'tile'}, use_global_device_ids=true, to_apply=%add | all-reduce | flops 8 | bytes 64 | tf_op jit(solution)/shard_map/all_gather | solution.py:156
  75.5 1.7 pad_maximum_fusion.1
  77.7 1.3 gather_fusion.2
  79.0 1.3 gather_fusion.4
  81.6 1.3 broadcast_select_fusion.5
  85.4 1.3 gather_fusion.9
  86.7 1.2 broadcast_select_fusion.1
  88.0 1.2 maximum_bitcast_fusion.1
  91.3 8.1 %pad_maximum_fusion = bf16[64,18,18,128]{3,1,0,2:T(8,128)(2,1)} fusion(bf16[64,1,18,128]{3,1,0,2:T(2,128)(2,1)S(1)} %copy.43, bf16[64,16,1,128]{3,1,0,2:T(8,128)(2,1)S(1)} %get-tuple-element.228, bf16[64,16,16,128]{3,1,0,2:T(8,128)(2,1)} %bitcast.232, bf16[64,16,1,128]{3,1,0,2:T(8,128)(2,1)S(1)} %get-tuple-element.229, bf16[64,1,18,128]{3,1,0,2:T(2,128)(2,1)S(1)} %copy.42), kind=kLoop, calls=%fused_computation.94 | loop fusion | flops 26542080 | bytes 10616832 | tf_op jit(solution)/shard_map/concatenate | solution.py:49
  99.4 7.7 %gather_fusion = bf16[64,18,18,128]{3,1,2,0:T(8,128)(2,1)} fusion(bf16[64,18,18,128]{3,1,0,2:T(8,128)(2,1)} %pad_maximum_fusion, s32[1024]{0:T(1024)S(1)} %pad_clamp_fusion.1), kind=kCustom, calls=%fused_computation.8 | custom fusion | bytes 10617088 | tf_op jit(solution)/shard_map/gather | solution.py:188
  107.1 6.4 %copy_select_fusion = bf16[8,8,18,18,128]{4,1,3,2,0:T(8,128)(2,1)} fusion(bf16[8,8,18,18,128]{4,2,3,1,0:T(8,128)(2,1)} %bitcast.229, pred[8,8]{1,0:T(8,128)(4,1)S(1)} %get-tuple-element.225), kind=kLoop, calls=%fused_computation.95 | loop fusion | flops 2654208 | bytes 10616896 | tf_op jit(solution)/shard_map/jit(_where)/select_n | solution.py:187
  113.5 4.8 %all-to-all-start = ((bf16[8,8,18,18,128]{4,1,3,2,0:T(8,128)(2,1)}), bf16[8,8,18,18,128]{4,1,3,2,0:T(8,128)(2,1)}, u32[]{:S(2)}, u32[]{:S(2)}) async-start(bf16[8,8,18,18,128]{4,1,3,2,0:T(8,128)(2,1)} %copy_select_fusion), calls=%async_computation | async-start | bytes 10616832 | tf_op jit(solution)/shard_map/all_to_all | solution.py:191
  118.7 115.4 %all-to-all-done = bf16[8,8,18,18,128]{4,1,3,2,0:T(8,128)(2,1)} async-done(((bf16[8,8,18,18,128]{4,1,3,2,0:T(8,128)(2,1)}), bf16[8,8,18,18,128]{4,1,3,2,0:T(8,128)(2,1)}, u32[]{:S(2)}, u32[]{:S(2)}) %all-to-all-start) | async-done | bytes 5308448 | tf_op jit(solution)/shard_map/all_to_all | solution.py:191
  234.1 6.7 %copy.45 = bf16[8,8,18,18,128]{4,3,2,1,0:T(8,128)(2,1)} copy(bf16[8,8,18,18,128]{4,1,3,2,0:T(8,128)(2,1)} %all-to-all-done) | data formatting | bytes 10616832 | tf_op jit(solution)/shard_map/all_to_all | solution.py:191
  240.8 5.9 %gather_fusion.1 = bf16[32,18,18,128]{3,2,1,0:T(8,128)(2,1)} fusion(bf16[64,18,18,128]{3,2,1,0:T(8,128)(2,1)} %bitcast.233, s32[1024]{0:T(1024)S(1)} %pad_clamp_fusion), kind=kCustom, calls=%fused_computation.9 | custom fusion | bytes 5308544 | tf_op jit(solution)/shard_map/gather | solution.py:193
  246.7 78.2 %while.19 = (s32[]{:T(128)}, f32[9,128]{1,0:T(8,128)S(1)}, f32[128]{0:T(128)S(1)}, f32[128,512]{1,0:T(8,128)S(1)}, f32[512,128]{1,0:T(8,128)S(1)}, /*index=5*/f3...) while((s32[]{:T(128)}, f32[9,128]{1,0:T(8,128)S(1)}, ...), condition=%wide.region_22.24_spmd.clone, body=%wide.region_5.23_spmd.clone.sunk | while | flops 562694528 | bytes 22358420 | solution.py:134
  250.1 1.2 fusion.88
  253.0 1.3 convolution_add_fusion.6
  255.4 1.1 fusion.89
  259.9 1.2 fusion.88
  262.8 1.3 convolution_add_fusion.6
  265.1 1.1 fusion.89
  269.7 1.2 fusion.88
  272.5 1.3 convolution_add_fusion.6
  274.9 1.1 fusion.89
  279.4 1.2 fusion.88
  282.3 1.3 convolution_add_fusion.6
  284.7 1.1 fusion.89
  289.2 1.2 fusion.88
  292.1 1.3 convolution_add_fusion.6
  294.4 1.1 fusion.89
  299.0 1.2 fusion.88
  301.8 1.3 convolution_add_fusion.6
  304.2 1.1 fusion.89
  308.8 1.2 fusion.88
  311.6 1.3 convolution_add_fusion.6
  314.0 1.1 fusion.89
  318.5 1.2 fusion.88
  321.4 1.3 convolution_add_fusion.6
  323.8 1.1 fusion.89
  325.7 38.3 %all-reduce.1 = (f32[9,128]{1,0:T(8,128)}, f32[128]{0:T(128)}) all-reduce(f32[9,128]{1,0:T(8,128)S(1)} %get-tuple-element.73, f32[128]{0:T(128)S(1)} %get-tuple-element.74), channel_id=1, replica_groups=mesh['slide'=4,'tile'=8] {'slide','tile'}, use_global_device_ids=true, to_apply=%region_23.25 | all-reduce | flops 1280 | bytes 10240 | tf_op jit(solution)/shard_map/psum | solution.py:194
  364.0 89.1 %all-reduce.5.cloned.1.call-done = (f32[128,512]{1,0:T(8,128)}, f32[512,128]{1,0:T(8,128)}) async-done(((f32[128,512]{1,0:T(8,128)}, f32[512,128]{1,0:T(8,128)}), (f32[128,512]{1,0:T(8,128)}, f32[512,128]{1,0:T(8,128)})) %all-reduce.5.cloned.1.call-update) | async-done | bytes 524304 | tf_op jit(solution)/shard_map/psum | solution.py:194
  453.2 1.7 copy.73
  454.8 1.7 copy.74
  (244 shorter events, 61.5 us)
Async XLA Ops:
  10.4 2.1 copy-start
  10.4 8.3 %copy-start.7 = (s32[1,64,8]{1,2,0:T(8,128)S(1)}, s32[1,64,8]{1,2,0:T(8,128)}, u32[]{:S(2)}) copy-start(s32[1,64,8]{1,2,0:T(8,128)} %param.16) | copy-start | bytes 6148
  10.5 9.1 %copy-start.9 = (u32[32]{0:T(128)S(1)}, u32[32]{0:T(128)}, u32[]{:S(2)}) copy-start(u32[32]{0:T(128)} %constant.130) | copy-start | bytes 388
  10.5 61.3 %copy-start.8 = (s32[1,8]{1,0:T(1,128)S(1)}, s32[1,8]{1,0:T(1,128)}, u32[]{:S(2)}) copy-start(s32[1,8]{1,0:T(1,128)} %param.17) | copy-start | bytes 100
  12.5 62.9 %collective-permute-start = (bf16[64,4,16,128]{3,2,0,1:T(8,128)(2,1)S(1)}, bf16[64,4,16,128]{3,2,0,1:T(8,128)(2,1)S(1)}, u32[]{:S(2)}, u32[]{:S(2)}) collective-permute-start(bf16[64,4,16,128]{3,2,0,1:T(8,128)(2,1)S(1)} %pad_maximum_fusion.2), channel_id=1, source_target_pairs={{0,1},{1,2},{2,3},{3,4},{4,5},{5,6},{6,7},{8,9},{9,10},{10,11},{11... | collective-permute-start | bytes 3145736 | tf_op jit(solution)/shard_map/ppermute | solution.py:17
  17.4 58.0 %collective-permute-start.1 = (bf16[64,4,16,128]{3,2,0,1:T(8,128)(2,1)S(1)}, bf16[64,4,16,128]{3,2,0,1:T(8,128)(2,1)}, u32[]{:S(2)}, u32[]{:S(2)}) collective-permute-start(bf16[64,4,16,128]{3,2,0,1:T(8,128)(2,1)S(1)} %pad_maximum_fusion.2), channel_id=1, source_target_pairs={{1,0},{2,1},{3,2},{4,3},{5,4},{6,5},{7,6},{9,8},{10,9},{11,10},{12... | collective-permute-start | bytes 3145736 | tf_op jit(solution)/shard_map/ppermute | solution.py:19
  113.5 120.7 %all-to-all-start = ((bf16[8,8,18,18,128]{4,1,3,2,0:T(8,128)(2,1)}), bf16[8,8,18,18,128]{4,1,3,2,0:T(8,128)(2,1)}, u32[]{:S(2)}, u32[]{:S(2)}) async-start(bf16[8,8,18,18,128]{4,1,3,2,0:T(8,128)(2,1)} %copy_select_fusion), calls=%async_computation | async-start | bytes 10616832 | tf_op jit(solution)/shard_map/all_to_all | solution.py:191
  118.3 334.9 %all-reduce.5.cloned.1.call-start = ((), (), s32[]{:S(2)}) async-start(), calls=%async_computation.1 | async-start | bytes 1048576 | tf_op jit(solution)/shard_map/psum | solution.py:194
  240.8 5.9 %copy-start.1 = (bf16[128,512]{1,0:T(8,128)(2,1)S(1)}, bf16[128,512]{1,0:T(8,128)(2,1)}, u32[]{:S(2)}) copy-start(bf16[128,512]{1,0:T(8,128)(2,1)} %param.21) | copy-start | bytes 393220
  240.8 5.9 %copy-start.2 = (bf16[512,128]{1,0:T(8,128)(2,1)S(1)}, bf16[512,128]{1,0:T(8,128)(2,1)}, u32[]{:S(2)}) copy-start(bf16[512,128]{1,0:T(8,128)(2,1)} %param.22) | copy-start | bytes 393220
  240.8 5.9 %copy-start.5 = (f32[128]{0:T(128)S(1)}, f32[128]{0:T(128)}, u32[]{:S(2)}) copy-start(f32[128]{0:T(128)} %param.20) | copy-start | bytes 1540
  240.8 5.9 %copy-start.6 = (bf16[9,128]{1,0:T(8,128)(2,1)S(1)}, bf16[9,128]{1,0:T(8,128)(2,1)}, u32[]{:S(2)}) copy-start(bf16[9,128]{1,0:T(8,128)(2,1)} %param.19) | copy-start | bytes 6916
  324.9 0.7 copy-start.3
  324.9 0.8 copy-start.4
Sparse Core Ops, SparseCore 0:
  325.8 127.2 all-reduce.4
where the time goes:
time: 465 us; the launch traced here: 463 us
  waiting for transfers between devices  205 us (44%)
  blocking collectives  89.1 us (19%)
  other arithmetic  53 us (11%)
  local copies, waits for them, and re-layouts  49.9 us (11%)
  matrix products  39.2 us (8%)
  between operations  15.8 us (3%)
  starting transfers between devices  11.1 us (2%)
    all_to_all x1, waiting for transfers between devices, local(): lax.all_to_all(outgoing, 'tile', split_axis=0, concat_axis=0, tiled=True)  115 us
    psum x1, waiting for transfers between devices, local(): lax.psum((grads[0], grads[1], grads[2], grads[3]), ('slide', 'tile'))  89.1 us
    all_gather x1, blocking collectives, local(): counts_all = lax.all_gather(tissue_count[0], 'tile', axis=0, tiled=True)  50.8 us
    psum x1, blocking collectives, local(): lax.psum((grads[0], grads[1], grads[2], grads[3]), ('slide', 'tile'))  38.3 us
    dot_general x8, matrix products, block_section(): grad_out = jnp.dot(act_sum.T, grad_embed, precision=lax.Precision.HIGHEST)  10.7 us
    dot_general x8, matrix products, block_section(): before = jnp.dot(normed, w_in, preferred_element_type=jnp.float32)  9.62 us
  transfers between devices with their start and end apart: 4, of which 2 were waited for; matrix products, arithmetic and copies ran while one was open for 1% of the time, Pallas kernels for 0%

commit v1 on v0

v1 whole, which is shorter than its diff:
```python
import functools

import jax
import jax.numpy as jnp
from jax import lax
from jax.experimental import pallas as pl
from jax.experimental.pallas import tpu as pltpu
from jax.sharding import PartitionSpec as P

HIGHEST = lax.Precision.HIGHEST
PITCH = 32
FIRST = 8
TILES_STEP = 4
SMALL_ROWS = 8
VMEM_BYTES = 56 * 1024 * 1024


def bits_of(count):
    return [1 << bit for bit in range(count.bit_length() - 1)]


def swap(value, axis, bit):
    count = lax.axis_size(axis)
    return lax.ppermute(value, axis, [(i, i ^ bit) for i in range(count)])


def strip_kernel(tiles, strips, wide):
    count, side = tiles.shape[0], tiles.shape[1]
    for index in range(count):
        strips[index, 0] = tiles[index, 0]
        strips[index, 1] = tiles[index, side - 1]
        base = index * side * side
        for row in range(side):
            wide[base + row * side : base + (row + 1) * side, :] = tiles[index, row].astype(jnp.float32)
        strips[index, 2] = wide[pl.ds(base, side, stride=side), :].astype(jnp.bfloat16)
        strips[index, 3] = wide[pl.ds(base + side - 1, side, stride=side), :].astype(jnp.bfloat16)


def border_strips(tiles):
    slots, side, _, chans = tiles.shape
    step = 16
    return pl.pallas_call(
        strip_kernel,
        grid=(slots // step,),
        in_specs=[pl.BlockSpec((step, side, side, chans), lambda i: (i, 0, 0, 0))],
        out_specs=pl.BlockSpec((step, 4, side, chans), lambda i: (i, 0, 0, 0)),
        out_shape=jax.ShapeDtypeStruct((slots, 4, side, chans), jnp.bfloat16),
        scratch_shapes=[pltpu.VMEM((step * side * side, chans), jnp.float32)],
    )(tiles)


def block_kernel(
    peers,
    work,
    parts,
    meta,
    dealing,
    links,
    feats,
    own,
    before_halo,
    after_halo,
    cot_all,
    kern,
    gain,
    w_in,
    w_in_t,
    w_out,
    w_out_t,
    embed_out,
    grad_out,
    pad,
    unit,
    invs,
    normed,
    gb,
    asum,
    csum,
    ge,
    ga,
    tap_sum,
    gain_sum,
    gi_sum,
    go_sum,
    place,
):
    slots, side = feats.shape[0], feats.shape[1]
    chans, hidden = w_in.shape
    pixels = side * side
    cot_rows = cot_all.shape[0] // peers
    count, begin, me, mine = meta[0], meta[1], meta[2], meta[3]
    tap_sum[...] = jnp.zeros_like(tap_sum)
    gain_sum[...] = jnp.zeros_like(gain_sum)
    gi_sum[...] = jnp.zeros_like(gi_sum)
    asum[...] = jnp.zeros_like(asum)
    csum[...] = jnp.zeros_like(csum)
    ge[...] = jnp.zeros_like(ge)
    embed_out[...] = jnp.zeros_like(embed_out)

    @pl.loop(0, count)
    def _(slot):
        rank = lax.rem(begin + slot, peers * work)
        worker = dealing[lax.rem(rank, peers)]
        row = lax.div(rank, peers)
        block = worker ^ me
        place[slot] = block * work + row
        ge[pl.ds(slot, 1), :] = cot_all[pl.ds(block * cot_rows + row, 1), :] * (1.0 / pixels)

    ga[...] = 0.5 * jnp.dot(
        ge[...], w_out_t[...].astype(jnp.float32), precision=HIGHEST, preferred_element_type=jnp.float32
    )
    gains = gain[...]
    taps = [jnp.broadcast_to(kern[i : i + 1, :], (side, chans)) for i in range(9)]

    def strip(column, which, slot):
        index = links[column, slot] - (me - 1) * slots
        held = links[column, slot] >= 0
        first = before_halo[jnp.clip(index, 0, slots - 1), which]
        middle = own[jnp.clip(index - slots, 0, slots - 1), which]
        last = after_halo[jnp.clip(index - 2 * slots, 0, slots - 1), which]
        chosen = jnp.where(index < slots, first, jnp.where(index < 2 * slots, middle, last)).astype(jnp.float32)
        return jnp.where(held, chosen, 0.0)

    @pl.loop(0, lax.div(count + TILES_STEP - 1, TILES_STEP))
    def _(step):
        for part in range(TILES_STEP):
            slot = step * TILES_STEP + part
            base = part * (side + 2) * PITCH
            total = jnp.zeros((side, chans), jnp.float32)
            for y in range(side):
                row = feats[slot, y].astype(jnp.float32)
                pad[pl.ds(base + (y + 1) * PITCH + FIRST, side), :] = row
                total = total + row
            csum[pl.ds(slot, 1), :] = jnp.sum(total, axis=0, keepdims=True)
            top = base
            low = base + (side + 1) * PITCH
            left, right = FIRST - 1, FIRST + side
            pad[pl.ds(top + FIRST, side), :] = strip(0, 1, slot)
            pad[pl.ds(low + FIRST, side), :] = strip(1, 0, slot)
            pad[pl.ds(top + PITCH + left, side, stride=PITCH), :] = strip(2, 3, slot)
            pad[pl.ds(top + PITCH + right, side, stride=PITCH), :] = strip(3, 2, slot)
            pad[pl.ds(top + left, 1), :] = strip(4, 1, slot)[side - 1 :]
            pad[pl.ds(top + right, 1), :] = strip(5, 1, slot)[:1]
            pad[pl.ds(low + left, 1), :] = strip(6, 0, slot)[side - 1 :]
            pad[pl.ds(low + right, 1), :] = strip(7, 0, slot)[:1]
            for y in range(side):
                depth = None
                for a in range(3):
                    for b in range(3):
                        term = pad[pl.ds(base + (y + a) * PITCH + left + b, side), :] * taps[3 * a + b]
                        depth = term if depth is None else depth + term
                centered = depth - jnp.mean(depth, axis=1, keepdims=True)
                inverse = lax.rsqrt(jnp.mean(centered * centered, axis=1, keepdims=True) + 1e-06)
                units = centered * inverse
                at = part * pixels + y * side
                unit[at : at + side, :] = units
                invs[at : at + side, :] = jnp.broadcast_to(inverse, (side, chans))
                normed[at : at + side, :] = (units * gains).astype(jnp.bfloat16)
        for part in range(TILES_STEP):
            slot = step * TILES_STEP + part
            rows = slice(part * pixels, (part + 1) * pixels)
            before = jnp.dot(normed[rows, :], w_in[...], preferred_element_type=jnp.float32)
            scaled = before * 0.7071067811865476
            twice = 1.0 + lax.erf(scaled)
            bell = jnp.exp(-(scaled * scaled))
            asum[pl.ds(slot, 1), :] = 0.5 * jnp.sum(before * twice, axis=0, keepdims=True)
            slope = twice + (scaled * 1.1283791670955126) * bell
            gb[rows, :] = (slope * ga[pl.ds(slot, 1), :]).astype(jnp.bfloat16)
        gi_sum[...] += lax.dot_general(
            normed[...], gb[...], (((0,), (0,)), ((), ())), preferred_element_type=jnp.float32
        )
        gain_part = jnp.zeros((side, chans), jnp.float32)
        tap_part = [jnp.zeros((side, chans), jnp.float32) for _ in range(9)]
        for part in range(TILES_STEP):
            base = part * (side + 2) * PITCH
            grad_normed = jnp.dot(
                gb[part * pixels : (part + 1) * pixels, :], w_in_t[...], preferred_element_type=jnp.float32
            )
            for y in range(side):
                at = part * pixels + y * side
                rows = grad_normed[y * side : (y + 1) * side]
                units = unit[at : at + side, :]
                product = rows * units
                gain_part = gain_part + product
                grad_unit = rows * gains
                grad_depth = invs[at : at + side, :] * (
                    grad_unit
                    - jnp.mean(grad_unit, axis=1, keepdims=True)
                    - units * jnp.mean(product * gains, axis=1, keepdims=True)
                )
                for a in range(3):
                    for b in range(3):
                        tap_part[3 * a + b] = (
                            tap_part[3 * a + b]
                            + grad_depth * pad[pl.ds(base + (y + a) * PITCH + FIRST - 1 + b, side), :]
                        )
        gain_sum[...] += gain_part
        for i in range(9):
            tap_sum[i * side : (i + 1) * side, :] += tap_part[i]

    go_sum[...] = lax.dot_general(
        asum[...], ge[...], (((0,), (0,)), ((), ())), precision=HIGHEST, preferred_element_type=jnp.float32
    )
    projected = jnp.dot(
        asum[...], w_out[...].astype(jnp.float32), precision=HIGHEST, preferred_element_type=jnp.float32
    )
    csum[...] = (csum[...] + projected) * (1.0 / pixels)

    @pl.loop(0, count)
    def _(slot):
        embed_out[pl.ds(place[slot], 1), :] = csum[pl.ds(slot, 1), :]

    per = hidden // parts
    for block in range(parts):
        to = block ^ mine
        columns, offset = divmod(block * per, chans)
        grad_out[to, :per, :] = gi_sum[offset : offset + per, columns * chans : (columns + 1) * chans]
        grad_out[to, per : 2 * per, :] = go_sum[block * per : (block + 1) * per, :]
        grad_out[to, 2 * per :, :] = jnp.zeros((SMALL_ROWS, chans), jnp.float32)
    for i in range(9):
        grad_out[(i // SMALL_ROWS) ^ mine, pl.ds(2 * per + i % SMALL_ROWS, 1), :] = jnp.sum(
            tap_sum[i * side : (i + 1) * side, :], axis=0, keepdims=True
        )
    grad_out[1 ^ mine, pl.ds(2 * per + 1, 1), :] = jnp.sum(gain_sum[...], axis=0, keepdims=True)


def unpack_kernel(parts, meta, packed, gk, gg, gi, go):
    mine = meta[3]
    hidden, chans = go.shape
    per = hidden // parts
    for block in range(parts):
        at = block ^ mine
        columns, offset = divmod(block * per, chans)
        gi[offset : offset + per, columns * chans : (columns + 1) * chans] = packed[at, :per, :]
        go[block * per : (block + 1) * per, :] = packed[at, per : 2 * per, :]
    gk[:SMALL_ROWS, :] = packed[mine, 2 * per :, :]
    gk[SMALL_ROWS:9, :] = packed[1 ^ mine, 2 * per : 2 * per + 1, :]
    gg[...] = packed[1 ^ mine, 2 * per + 1 : 2 * per + 2, :]


def local(features, tissue_count, neighbors, worker_perm, rotation, kernel, gain, w_in, w_out, cotangent):
    feats = features[0]
    slots, side, _, chans = feats.shape
    hidden = w_in.shape[1]
    cot_rows = cotangent[0]
    work = cot_rows.shape[0]
    peers = lax.axis_size("tile")
    slides = lax.axis_size("slide")
    me = lax.axis_index("tile")
    slide_bits, tile_bits = bits_of(slides), bits_of(peers)
    halving = [("slide", bit) for bit in slide_bits] + [("tile", tile_bits[0])]
    parts = 1 << len(halving)
    mine = jnp.zeros((), jnp.int32)
    for place, (axis, bit) in enumerate(reversed(halving)):
        mine = mine + jnp.where((lax.axis_index(axis) & bit) > 0, 1 << place, 0)

    strips = border_strips(feats)
    before_halo = lax.ppermute(strips, "tile", [(i, i + 1) for i in range(peers - 1)])
    after_halo = lax.ppermute(strips, "tile", [(i + 1, i) for i in range(peers - 1)])

    gathered = jnp.concatenate(
        [cot_rows, jnp.broadcast_to(tissue_count.astype(jnp.float32), (8, chans))], axis=0
    )[None]
    for bit in tile_bits:
        gathered = jnp.concatenate([gathered, swap(gathered, "tile", bit)], axis=0)
    counts = gathered[:, work, 0].astype(jnp.int32)
    whose = jnp.arange(peers, dtype=jnp.int32) ^ me
    begin = jnp.sum(jnp.where(whose < me, counts, 0)) + rotation[0]
    meta = jnp.stack([tissue_count[0, 0], begin, me, mine]).astype(jnp.int32)

    f32 = jnp.float32
    pixels = side * side
    vmem = pl.BlockSpec(memory_space=pltpu.VMEM)
    smem = pl.BlockSpec(memory_space=pltpu.SMEM)
    per = hidden // parts
    block_rows = 2 * per + SMALL_ROWS
    embeds, packed = pl.pallas_call(
        functools.partial(block_kernel, peers, work, parts),
        in_specs=[smem] * 3 + [vmem] * 11,
        out_specs=[vmem] * 2,
        out_shape=[
            jax.ShapeDtypeStruct((peers * work, chans), f32),
            jax.ShapeDtypeStruct((parts, block_rows, chans), f32),
        ],
        scratch_shapes=[
            pltpu.VMEM((TILES_STEP * (side + 2) * PITCH, chans), f32),
            pltpu.VMEM((TILES_STEP * pixels, chans), f32),
            pltpu.VMEM((TILES_STEP * pixels, chans), f32),
            pltpu.VMEM((TILES_STEP * pixels, chans), jnp.bfloat16),
            pltpu.VMEM((TILES_STEP * pixels, hidden), jnp.bfloat16),
            pltpu.VMEM((slots, hidden), f32),
            pltpu.VMEM((slots, chans), f32),
            pltpu.VMEM((slots, chans), f32),
            pltpu.VMEM((slots, hidden), f32),
            pltpu.VMEM((9 * side, chans), f32),
            pltpu.VMEM((side, chans), f32),
            pltpu.VMEM((chans, hidden), f32),
            pltpu.VMEM((hidden, chans), f32),
            pltpu.SMEM((slots,), jnp.int32),
        ],
        compiler_params=pltpu.CompilerParams(vmem_limit_bytes=VMEM_BYTES),
    )(
        meta,
        worker_perm[0],
        neighbors[0].T,
        feats,
        strips,
        before_halo,
        after_halo,
        gathered.reshape(peers * (work + 8), chans),
        kernel.astype(f32),
        gain[None],
        w_in,
        w_in.T,
        w_out,
        w_out.T,
    )

    held = packed
    for axis, bit in halving[:-1]:
        half = held.shape[0] // 2
        held = held[:half] + swap(held[half:], axis, bit)
    embeds = embeds.reshape(peers, work, chans)
    for place, bit in enumerate(tile_bits):
        paired = embeds.reshape(embeds.shape[0] // 2, 2, work, chans)
        keep, send = paired[:, 0], paired[:, 1]
        if place == 0:
            mine_part, other_part = held[0], held[1]
        else:
            mine_part, other_part = held, held
        outgoing = jnp.concatenate([send.reshape(-1, chans), other_part], axis=0)
        incoming = swap(outgoing, "tile", bit)
        rows = send.shape[0] * work
        embeds = keep + incoming[:rows].reshape(keep.shape)
        held = mine_part + incoming[rows:]
    held = held[None]
    for axis, bit in reversed(halving):
        held = jnp.concatenate([held, swap(held, axis, bit)], axis=0)
    gk, gg, gi, go = pl.pallas_call(
        functools.partial(unpack_kernel, parts),
        in_specs=[smem, vmem],
        out_specs=[vmem] * 4,
        out_shape=[
            jax.ShapeDtypeStruct((9, chans), f32),
            jax.ShapeDtypeStruct((1, chans), f32),
            jax.ShapeDtypeStruct((chans, hidden), f32),
            jax.ShapeDtypeStruct((hidden, chans), f32),
        ],
    )(meta, held)
    return embeds, gk, gg[0], gi, go


def solution(mesh):
    placed = (
        P("slide", "tile", None, None, None),
        P("slide", "tile"),
        P("slide", "tile", None),
        P("slide", None),
        P("slide"),
        P(),
        P(),
        P(),
        P(),
        P("slide", "tile", None),
    )
    return jax.shard_map(
        local,
        mesh=mesh,
        in_specs=placed,
        out_specs=(P("slide", "tile", None), P(), P(), P(), P()),
        check_vma=False,
    )
```

time: 465 us -> 159 us (0.34)
  waiting for transfers between devices: 205 us -> 67.3 us
  blocking collectives: 89.1 us -> 0 us
  Pallas kernels: 0 us -> 56.2 us
  other arithmetic: 53 us -> 4.75 us
  local copies, waits for them, and re-layouts: 49.9 us -> 4.79 us
  matrix products: 39.2 us -> 0 us
  between operations: 15.8 us -> 2.87 us
  starting transfers between devices: 11.1 us -> 22.3 us
    all_to_all x1 -> x0, waiting for transfers between devices: 115 us -> none  [local(): lax.all_to_all(outgoing, 'tile', split_axis=0, concat_axis=0, tiled=True)]
    psum x1 -> x0, waiting for transfers between devices: 89.1 us -> none  [local(): lax.psum((grads[0], grads[1], grads[2], grads[3]), ('slide', 'tile'))]
    ppermute x2 -> x13, waiting for transfers between devices: 0.01 us -> 67.3 us  [the longest x11 67.3 us: swap(): return lax.ppermute(value, axis, [(i, i ^ bit) for i in range(count)])]
    pallas_call x0 -> x3, Pallas kernels: none -> 56.2 us  [the longest x1 49.9 us: local(): pl.pallas_call(functools.partial(block_kernel, peers, work, parts), in_sp...]
    all_gather x1 -> x0, blocking collectives: 50.8 us -> none  [local(): counts_all = lax.all_gather(tissue_count[0], 'tile', axis=0, tiled=True)]
    dot_general x48 -> x0, matrix products: 39.2 us -> none  [the longest x8 10.7 us: block_section(): grad_out = jnp.dot(act_sum.T, grad_embed, precision=lax.Precision.HIGHEST)]
    psum x1 -> x0, blocking collectives: 38.3 us -> none  [local(): lax.psum((grads[0], grads[1], grads[2], grads[3]), ('slide', 'tile'))]
    gather x10 -> x0, local copies, waits for them, and re-layouts: 20.6 us -> none  [the longest x1 7.67 us: local(): padded[send_index]]
  transfers between devices with their start and end apart: 4 -> 13, of which waited for: 2 -> 10; matrix products, arithmetic and copies ran while one was open for 1% -> 3% of each run, Pallas kernels for 0% -> 0%
where the time goes in v1:
time: 159 us; the launch traced here: 158 us
  waiting for transfers between devices  67.3 us (42%)
  Pallas kernels  56.2 us (35%)
  starting transfers between devices  22.3 us (14%)
  local copies, waits for them, and re-layouts  4.79 us (3%)
  other arithmetic  4.75 us (3%)
  between operations  2.87 us (2%)
    ppermute x11, waiting for transfers between devices, swap(): return lax.ppermute(value, axis, [(i, i ^ bit) for i in range(count)])  67.3 us
    pallas_call x1, Pallas kernels, local(): pl.pallas_call(functools.partial(block_kernel, peers, work, parts), in_sp...  49.9 us
    ppermute x11, starting transfers between devices, swap(): return lax.ppermute(value, axis, [(i, i ^ bit) for i in range(count)])  15.4 us
    ppermute x1, starting transfers between devices, local(): lax.ppermute(strips, 'tile', [(i, i + 1) for i in range(peers - 1)])  5.56 us
    pallas_call x1, Pallas kernels, border_strips(): pl.pallas_call(strip_kernel, grid=(slots // step,), in_specs=[pl.BlockSpe...  4.48 us
  transfers between devices with their start and end apart: 13, of which 10 were waited for; matrix products, arithmetic and copies ran while one was open for 3% of the time, Pallas kernels for 0%

profile of v1, /device:TPU:0, one launch (start us, length us, event | category | flops | bytes accessed | tf_op | source)
XLA Modules:
  0.0 158.2 jit_solution(4262033009166127687)
XLA Ops:
  0.6 0.0 copy-start.5
  0.6 0.0 copy-start.6
  0.7 0.0 copy-start.3
  0.7 0.0 copy-start.4
  0.7 4.5 %shard_map.137.own = bf16[64,4,16,128]{3,2,1,0:T(8,128)(2,1)} custom-call(bf16[64,16,16,128]{3,2,1,0:T(8,128)(2,1)} %bitcast.55), custom_call_target="tpu_custom_call" | custom-call | tf_op jit(solution)/shard_map/pallas_call | solution.py:42
  5.2 1.3 collective-permute-start.4
  6.4 5.6 %collective-permute-start.3 = (bf16[64,4,16,128]{3,2,1,0:T(8,128)(2,1)}, bf16[64,4,16,128]{3,2,1,0:T(8,128)(2,1)S(1)}, u32[]{:S(2)}, u32[]{:S(2)}) collective-permute-start(bf16[64,4,16,128]{3,2,1,0:T(8,128)(2,1)} %shard_map.137.own), channel_id=1, source_target_pairs={{0,1},{1,2},{2,3},{3,4},{4,5},{5,6},{6,7},{8,9},{9,10},{10,11},{11... | collective-permute-start | bytes 3145736 | tf_op jit(solution)/shard_map/ppermute | solution.py:258
  12.7 0.0 copy-done.5
  12.7 2.9 %collective-permute-start = (f32[1,40,128]{2,1,0:T(8,128)S(1)}, f32[1,40,128]{2,1,0:T(8,128)S(1)}, u32[]{:S(2)}, u32[]{:S(2)}) collective-permute-start(f32[1,40,128]{2,1,0:T(8,128)S(1)} %pad_bitcast_fusion), channel_id=1, source_target_pairs={{0,1},{1,0},{2,3},{3,2},{4,5},{5,4},{6,7},{7,6},{8,9},{9,8},{10,11... | collective-permute-start | bytes 61448 | tf_op jit(solution)/shard_map/ppermute | solution.py:24
  15.6 40.8 %collective-permute-done = f32[1,40,128]{2,1,0:T(8,128)S(1)} collective-permute-done((f32[1,40,128]{2,1,0:T(8,128)S(1)}, f32[1,40,128]{2,1,0:T(8,128)S(1)}, u32[]{:S(2)}, u32[]{:S(2)}) %collective-permute-start) | collective-permute-done | bytes 20512 | tf_op jit(solution)/shard_map/ppermute | solution.py:24
  56.4 1.6 %collective-permute-start.1 = (f32[2,40,128]{2,1,0:T(8,128)S(1)}, f32[2,40,128]{2,1,0:T(8,128)S(1)}, u32[]{:S(2)}, u32[]{:S(2)}) collective-permute-start(f32[2,40,128]{2,1,0:T(8,128)S(1)} %pad_maximum_fusion.8), channel_id=1, source_target_pairs={{0,2},{1,3},{2,0},{3,1},{4,6},{5,7},{6,4},{7,5},{8,10},{9,11},{10,... | collective-permute-start | bytes 122888 | tf_op jit(solution)/shard_map/ppermute | solution.py:24
  58.1 2.4 %collective-permute-done.1 = f32[2,40,128]{2,1,0:T(8,128)S(1)} collective-permute-done((f32[2,40,128]{2,1,0:T(8,128)S(1)}, f32[2,40,128]{2,1,0:T(8,128)S(1)}, u32[]{:S(2)}, u32[]{:S(2)}) %collective-permute-start.1) | collective-permute-done | bytes 40992 | tf_op jit(solution)/shard_map/ppermute | solution.py:24
  60.5 2.7 %collective-permute-start.2 = (f32[4,40,128]{2,1,0:T(8,128)S(1)}, f32[4,40,128]{2,1,0:T(8,128)S(1)}, u32[]{:S(2)}, u32[]{:S(2)}) collective-permute-start(f32[4,40,128]{2,1,0:T(8,128)S(1)} %pad_maximum_fusion.7), channel_id=1, source_target_pairs={{0,4},{1,5},{2,6},{3,7},{4,0},{5,1},{6,2},{7,3},{8,12},{9,13},{10,... | collective-permute-start | bytes 245768 | tf_op jit(solution)/shard_map/ppermute | solution.py:24
  63.8 0.6 convert_element_type.15.kern
  64.4 0.8 copy.18
  65.1 0.8 copy.19
  65.9 0.0 collective-permute-done.2
  65.9 0.0 copy-start.2
  65.9 0.2 fusion.3
  66.2 0.7 fusion.4
  67.6 0.6 pad_add_fusion.meta
  68.2 0.0 collective-permute-done.4.after_halo
  68.2 0.0 collective-permute-done.3.before_halo
  68.2 0.9 copy-done
  69.1 0.4 copy-done.1
  69.5 49.9 %shard_map.138 = (f32[256,128]{1,0:T(8,128)}, f32[8,136,128]{2,1,0:T(8,128)}) custom-call(s32[4]{0:T(128)} %pad_add_fusion.meta, s32[8]{0:T(128)} %bitcast.68, s32[8,64]{1,0:T(8,128)} %bitcast.67, bf16[64,16,16,128]{3,2,1,0:T(8,128)(2,1)} %bitcast.56, bf16[64,4,16,128]{3,2,1,0:T(8,128)(2,1)} %shard_map.137.own, bf16[64,4,16,128]{3,2,1,0:T(8,128)(2,1)} %copy-done.1, ...), custom_call_target="tpu_custom_call" | custom-call | tf_op jit(solution)/shard_map/pallas_call | solution.py:277
  119.4 1.0 slice.61
  120.4 0.1 collective-permute-start.5
  120.5 1.5 collective-permute-done.5
  122.0 1.0 slice_add_fusion
  123.0 0.1 collective-permute-start.6
  123.1 0.9 fusion.5
  124.0 4.8 %collective-permute-done.6 = f32[2,136,128]{2,1,0:T(8,128)S(1)} collective-permute-done((f32[2,136,128]{2,1,0:T(8,128)S(1)}, f32[2,136,128]{2,1,0:T(8,128)S(1)}, u32[]{:S(2)}, u32[]{:S(2)}) %collective-permute-start.6) | collective-permute-done | bytes 139296 | tf_op jit(solution)/shard_map/ppermute | solution.py:24
  128.9 0.1 collective-permute-start.7
  128.9 5.0 %collective-permute-done.7 = f32[264,128]{1,0:T(8,128)S(1)} collective-permute-done((f32[264,128]{1,0:T(8,128)S(1)}, f32[264,128]{1,0:T(8,128)S(1)}, u32[]{:S(2)}, u32[]{:S(2)}) %collective-permute-start.7) | collective-permute-done | bytes 135200 | tf_op jit(solution)/shard_map/ppermute | solution.py:24
  134.0 2.1 %collective-permute-start.8 = (f32[200,128]{1,0:T(8,128)S(1)}, f32[200,128]{1,0:T(8,128)S(1)}, u32[]{:S(2)}, u32[]{:S(2)}) collective-permute-start(f32[200,128]{1,0:T(8,128)S(1)} %pad_maximum_fusion.5), channel_id=1, source_target_pairs={{0,2},{1,3},{2,0},{3,1},{4,6},{5,7},{6,4},{7,5},{8,10},{9,11},{10,... | collective-permute-start | bytes 307208 | tf_op jit(solution)/shard_map/ppermute | solution.py:24
  136.1 2.7 %collective-permute-done.8 = f32[200,128]{1,0:T(8,128)S(1)} collective-permute-done((f32[200,128]{1,0:T(8,128)S(1)}, f32[200,128]{1,0:T(8,128)S(1)}, u32[]{:S(2)}, u32[]{:S(2)}) %collective-permute-start.8) | collective-permute-done | bytes 102432 | tf_op jit(solution)/shard_map/ppermute | solution.py:24
  138.8 2.5 %collective-permute-start.9 = (f32[168,128]{1,0:T(8,128)S(1)}, f32[168,128]{1,0:T(8,128)S(1)}, u32[]{:S(2)}, u32[]{:S(2)}) collective-permute-start(f32[168,128]{1,0:T(8,128)S(1)} %pad_maximum_fusion.6), channel_id=1, source_target_pairs={{0,4},{1,5},{2,6},{3,7},{4,0},{5,1},{6,2},{7,3},{8,12},{9,13},{10,... | collective-permute-start | bytes 258056 | tf_op jit(solution)/shard_map/ppermute | solution.py:24
  141.3 2.9 %collective-permute-done.9 = f32[168,128]{1,0:T(8,128)S(1)} collective-permute-done((f32[168,128]{1,0:T(8,128)S(1)}, f32[168,128]{1,0:T(8,128)S(1)}, u32[]{:S(2)}, u32[]{:S(2)}) %collective-permute-start.9) | collective-permute-done | bytes 86048 | tf_op jit(solution)/shard_map/ppermute | solution.py:24
  144.2 2.2 %collective-permute-start.10 = (f32[1,136,128]{2,1,0:T(8,128)S(1)}, f32[1,136,128]{2,1,0:T(8,128)S(1)}, u32[]{:S(2)}, u32[]{:S(2)}) collective-permute-start(f32[1,136,128]{2,1,0:T(8,128)S(1)} %fusion), channel_id=1, source_target_pairs={{0,1},{1,0},{2,3},{3,2},{4,5},{5,4},{6,7},{7,6},{8,9},{9,8},{10,11... | collective-permute-start | bytes 208904 | tf_op jit(solution)/shard_map/ppermute | solution.py:24
  146.4 2.3 %collective-permute-done.10 = f32[1,136,128]{2,1,0:T(8,128)S(1)} collective-permute-done((f32[1,136,128]{2,1,0:T(8,128)S(1)}, f32[1,136,128]{2,1,0:T(8,128)S(1)}, u32[]{:S(2)}, u32[]{:S(2)}) %collective-permute-start.10) | collective-permute-done | bytes 69664 | tf_op jit(solution)/shard_map/ppermute | solution.py:24
  148.7 1.2 collective-permute-start.11
  149.9 3.9 %collective-permute-done.11 = f32[2,136,128]{2,1,0:T(8,128)S(1)} collective-permute-done((f32[2,136,128]{2,1,0:T(8,128)S(1)}, f32[2,136,128]{2,1,0:T(8,128)S(1)}, u32[]{:S(2)}, u32[]{:S(2)}) %collective-permute-start.11) | collective-permute-done | bytes 139296 | tf_op jit(solution)/shard_map/ppermute | solution.py:24
  153.9 0.1 collective-permute-start.12
  153.9 0.6 fusion.2
  154.5 0.9 collective-permute-done.12
  155.5 0.8 pad_maximum_fusion.packed
  156.3 1.9 %shard_map.139 = (f32[9,128]{1,0:T(8,128)}, f32[1,128]{1,0:T(1,128)}, f32[128,512]{1,0:T(8,128)}, f32[512,128]{1,0:T(8,128)}) custom-call(s32[4]{0:T(128)} %pad_add_fusion.meta, f32[8,136,128]{2,1,0:T(8,128)} %pad_maximum_fusion.packed), custom_call_target="tpu_custom_call" | custom-call | tf_op jit(solution)/shard_map/pallas_call | solution.py:339
  (27 shorter events, 0.2 us)
Async XLA Ops:
  0.6 12.0 %copy-start.5 = (f32[1,32,128]{2,1,0:T(8,128)S(1)}, f32[1,32,128]{2,1,0:T(8,128)}, u32[]{:S(2)}) copy-start(f32[1,32,128]{2,1,0:T(8,128)} %param.19) | copy-start | bytes 49156
  0.6 63.1 %copy-start.6 = (bf16[9,128]{1,0:T(8,128)(2,1)S(1)}, bf16[9,128]{1,0:T(8,128)(2,1)}, u32[]{:S(2)}) copy-start(bf16[9,128]{1,0:T(8,128)(2,1)} %param.15) | copy-start | bytes 6916
  0.7 63.7 %copy-start.3 = (bf16[128,512]{1,0:T(8,128)(2,1)S(1)}, bf16[128,512]{1,0:T(8,128)(2,1)}, u32[]{:S(2)}) copy-start(bf16[128,512]{1,0:T(8,128)(2,1)} %w_in.1) | copy-start | bytes 393220
  0.7 64.5 %copy-start.4 = (bf16[512,128]{1,0:T(8,128)(2,1)S(1)}, bf16[512,128]{1,0:T(8,128)(2,1)}, u32[]{:S(2)}) copy-start(bf16[512,128]{1,0:T(8,128)(2,1)} %w_out.1) | copy-start | bytes 393220
  5.2 63.0 %collective-permute-start.4 = (bf16[64,4,16,128]{3,2,1,0:T(8,128)(2,1)}, bf16[64,4,16,128]{3,2,1,0:T(8,128)(2,1)S(1)}, u32[]{:S(2)}, u32[]{:S(2)}) collective-permute-start(bf16[64,4,16,128]{3,2,1,0:T(8,128)(2,1)} %shard_map.137.own), channel_id=1, source_target_pairs={{1,0},{2,1},{3,2},{4,3},{5,4},{6,5},{7,6},{9,8},{10,9},{11,10},{12... | collective-permute-start | bytes 3145736 | tf_op jit(solution)/shard_map/ppermute | solution.py:259
  6.4 61.7 %collective-permute-start.3 = (bf16[64,4,16,128]{3,2,1,0:T(8,128)(2,1)}, bf16[64,4,16,128]{3,2,1,0:T(8,128)(2,1)S(1)}, u32[]{:S(2)}, u32[]{:S(2)}) collective-permute-start(bf16[64,4,16,128]{3,2,1,0:T(8,128)(2,1)} %shard_map.137.own), channel_id=1, source_target_pairs={{0,1},{1,2},{2,3},{3,4},{4,5},{5,6},{6,7},{8,9},{9,10},{10,11},{11... | collective-permute-start | bytes 3145736 | tf_op jit(solution)/shard_map/ppermute | solution.py:258
  12.7 43.8 %collective-permute-start = (f32[1,40,128]{2,1,0:T(8,128)S(1)}, f32[1,40,128]{2,1,0:T(8,128)S(1)}, u32[]{:S(2)}, u32[]{:S(2)}) collective-permute-start(f32[1,40,128]{2,1,0:T(8,128)S(1)} %pad_bitcast_fusion), channel_id=1, source_target_pairs={{0,1},{1,0},{2,3},{3,2},{4,5},{5,4},{6,7},{7,6},{8,9},{9,8},{10,11... | collective-permute-start | bytes 61448 | tf_op jit(solution)/shard_map/ppermute | solution.py:24
  56.4 4.0 %collective-permute-start.1 = (f32[2,40,128]{2,1,0:T(8,128)S(1)}, f32[2,40,128]{2,1,0:T(8,128)S(1)}, u32[]{:S(2)}, u32[]{:S(2)}) collective-permute-start(f32[2,40,128]{2,1,0:T(8,128)S(1)} %pad_maximum_fusion.8), channel_id=1, source_target_pairs={{0,2},{1,3},{2,0},{3,1},{4,6},{5,7},{6,4},{7,5},{8,10},{9,11},{10,... | collective-permute-start | bytes 122888 | tf_op jit(solution)/shard_map/ppermute | solution.py:24
  60.5 5.5 %collective-permute-start.2 = (f32[4,40,128]{2,1,0:T(8,128)S(1)}, f32[4,40,128]{2,1,0:T(8,128)S(1)}, u32[]{:S(2)}, u32[]{:S(2)}) collective-permute-start(f32[4,40,128]{2,1,0:T(8,128)S(1)} %pad_maximum_fusion.7), channel_id=1, source_target_pairs={{0,4},{1,5},{2,6},{3,7},{4,0},{5,1},{6,2},{7,3},{8,12},{9,13},{10,... | collective-permute-start | bytes 245768 | tf_op jit(solution)/shard_map/ppermute | solution.py:24
  65.9 2.3 %copy-start.2 = (f32[8,40,128]{2,1,0:T(8,128)}, f32[8,40,128]{2,1,0:T(8,128)S(1)}, u32[]{:S(2)}) copy-start(f32[8,40,128]{2,1,0:T(8,128)S(1)} %pad_maximum_fusion.2) | copy-start | bytes 491524
  68.2 1.0 copy-start
  68.2 1.4 copy-start.1
  120.4 1.6 %collective-permute-start.5 = (f32[4,136,128]{2,1,0:T(8,128)S(1)}, f32[4,136,128]{2,1,0:T(8,128)S(1)}, u32[]{:S(2)}, u32[]{:S(2)}) collective-permute-start(f32[4,136,128]{2,1,0:T(8,128)S(1)} %slice.61), channel_id=1, source_target_pairs={{0,8},{8,0},{16,24},{24,16},{1,9},{9,1},{17,25},{25,17},{2,10},{10... | collective-permute-start | bytes 835592 | tf_op jit(solution)/shard_map/ppermute | solution.py:24
  123.0 5.8 %collective-permute-start.6 = (f32[2,136,128]{2,1,0:T(8,128)S(1)}, f32[2,136,128]{2,1,0:T(8,128)S(1)}, u32[]{:S(2)}, u32[]{:S(2)}) collective-permute-start(f32[2,136,128]{2,1,0:T(8,128)S(1)} %slice.80), channel_id=1, source_target_pairs={{0,16},{8,24},{16,0},{24,8},{1,17},{9,25},{17,1},{25,9},{2,18},{10... | collective-permute-start | bytes 417800 | tf_op jit(solution)/shard_map/ppermute | solution.py:24
  128.9 5.1 %collective-permute-start.7 = (f32[264,128]{1,0:T(8,128)S(1)}, f32[264,128]{1,0:T(8,128)S(1)}, u32[]{:S(2)}, u32[]{:S(2)}) collective-permute-start(f32[264,128]{1,0:T(8,128)S(1)} %pad_maximum_fusion.4), channel_id=1, source_target_pairs={{0,1},{1,0},{2,3},{3,2},{4,5},{5,4},{6,7},{7,6},{8,9},{9,8},{10,11... | collective-permute-start | bytes 405512 | tf_op jit(solution)/shard_map/ppermute | solution.py:24
  134.0 4.7 %collective-permute-start.8 = (f32[200,128]{1,0:T(8,128)S(1)}, f32[200,128]{1,0:T(8,128)S(1)}, u32[]{:S(2)}, u32[]{:S(2)}) collective-permute-start(f32[200,128]{1,0:T(8,128)S(1)} %pad_maximum_fusion.5), channel_id=1, source_target_pairs={{0,2},{1,3},{2,0},{3,1},{4,6},{5,7},{6,4},{7,5},{8,10},{9,11},{10,... | collective-permute-start | bytes 307208 | tf_op jit(solution)/shard_map/ppermute | solution.py:24
  138.8 5.4 %collective-permute-start.9 = (f32[168,128]{1,0:T(8,128)S(1)}, f32[168,128]{1,0:T(8,128)S(1)}, u32[]{:S(2)}, u32[]{:S(2)}) collective-permute-start(f32[168,128]{1,0:T(8,128)S(1)} %pad_maximum_fusion.6), channel_id=1, source_target_pairs={{0,4},{1,5},{2,6},{3,7},{4,0},{5,1},{6,2},{7,3},{8,12},{9,13},{10,... | collective-permute-start | bytes 258056 | tf_op jit(solution)/shard_map/ppermute | solution.py:24
  144.2 4.5 %collective-permute-start.10 = (f32[1,136,128]{2,1,0:T(8,128)S(1)}, f32[1,136,128]{2,1,0:T(8,128)S(1)}, u32[]{:S(2)}, u32[]{:S(2)}) collective-permute-start(f32[1,136,128]{2,1,0:T(8,128)S(1)} %fusion), channel_id=1, source_target_pairs={{0,1},{1,0},{2,3},{3,2},{4,5},{5,4},{6,7},{7,6},{8,9},{9,8},{10,11... | collective-permute-start | bytes 208904 | tf_op jit(solution)/shard_map/ppermute | solution.py:24
  148.7 5.1 %collective-permute-start.11 = (f32[2,136,128]{2,1,0:T(8,128)S(1)}, f32[2,136,128]{2,1,0:T(8,128)S(1)}, u32[]{:S(2)}, u32[]{:S(2)}) collective-permute-start(f32[2,136,128]{2,1,0:T(8,128)S(1)} %pad_maximum_fusion.3), channel_id=1, source_target_pairs={{0,16},{8,24},{16,0},{24,8},{1,17},{9,25},{17,1},{25,9},{2,18},{10... | collective-permute-start | bytes 417800 | tf_op jit(solution)/shard_map/ppermute | solution.py:24
  153.9 1.6 %collective-permute-start.12 = (f32[4,136,128]{2,1,0:T(8,128)S(1)}, f32[4,136,128]{2,1,0:T(8,128)S(1)}, u32[]{:S(2)}, u32[]{:S(2)}) collective-permute-start(f32[4,136,128]{2,1,0:T(8,128)S(1)} %pad_maximum_fusion.1), channel_id=1, source_target_pairs={{0,8},{8,0},{16,24},{24,16},{1,9},{9,1},{17,25},{25,17},{2,10},{10... | collective-permute-start | bytes 835592 | tf_op jit(solution)/shard_map/ppermute | solution.py:24

commit v2 on v1

v2 whole, which is shorter than its diff:
```python
import functools

import jax
import jax.numpy as jnp
from jax import lax
from jax.experimental import pallas as pl
from jax.experimental.pallas import tpu as pltpu
from jax.sharding import PartitionSpec as P

HIGHEST = lax.Precision.HIGHEST
FIRST = 8
INNER_PITCH = 24
LINE_PITCH = 32
INNER_TILES = 4
BORDER_TILES = 8
SMALL_ROWS = 8
VMEM_BYTES = 24 * 1024 * 1024


def bits_of(count):
    return [1 << bit for bit in range(count.bit_length() - 1)]


def swap(value, axis, bit):
    count = lax.axis_size(axis)
    return lax.ppermute(value, axis, [(i, i ^ bit) for i in range(count)])


def strip_kernel(tiles, strips, inner, wide):
    count, side = tiles.shape[0], tiles.shape[1]
    for index in range(count):
        base = index * side * side
        for row in range(side):
            wide[base + row * side : base + (row + 1) * side, :] = tiles[index, row].astype(jnp.float32)
        for target, first, last in ((strips, 0, side - 1), (inner, 1, side - 2)):
            target[index, 0] = tiles[index, first]
            target[index, 1] = tiles[index, last]
            target[index, 2] = wide[pl.ds(base + first, side, stride=side), :].astype(jnp.bfloat16)
            target[index, 3] = wide[pl.ds(base + last, side, stride=side), :].astype(jnp.bfloat16)


def border_strips(tiles):
    slots, side, _, chans = tiles.shape
    step = 16
    shape = jax.ShapeDtypeStruct((slots, 4, side, chans), jnp.bfloat16)
    spec = pl.BlockSpec((step, 4, side, chans), lambda i: (i, 0, 0, 0))
    return pl.pallas_call(
        strip_kernel,
        grid=(slots // step,),
        in_specs=[pl.BlockSpec((step, side, side, chans), lambda i: (i, 0, 0, 0))],
        out_specs=[spec, spec],
        out_shape=[shape, shape],
        scratch_shapes=[pltpu.VMEM((step * side * side, chans), jnp.float32)],
    )(tiles)


def spread(rows, lines):
    return rows.reshape(lines, rows.shape[0] // lines, rows.shape[1])


def run_lines(
    step, tiles, starts, masked, weights, state, sums
):
    kern, gains, w_in, w_in_t = weights
    pad, unit, invs, normed, gb = state
    asum, ga, tap_sum, gain_sum, gi_sum = sums
    lines = len(starts)
    pad_rows = pad.shape[0] // tiles
    pixels = normed.shape[0] // tiles
    side = pixels // lines
    chans, hidden = w_in.shape
    taps = [jnp.broadcast_to(kern[i : i + 1, :], (side, chans)) for i in range(9)]
    place = lax.broadcasted_iota(jnp.int32, (side, hidden), 0)
    inside = jnp.where((place > 0) & (place < side - 1), 1.0, 0.0)
    for part in range(tiles):
        base = part * pad_rows
        for line in range(lines):
            depth = None
            for tap in range(9):
                term = pad[pl.ds(base + starts[line][tap], side), :] * taps[tap]
                depth = term if depth is None else depth + term
            centered = depth - jnp.mean(depth, axis=1, keepdims=True)
            inverse = lax.rsqrt(jnp.mean(centered * centered, axis=1, keepdims=True) + 1e-06)
            units = centered * inverse
            at = part * pixels + line * side
            unit[at : at + side, :] = units
            invs[at : at + side, :] = jnp.broadcast_to(inverse, (side, chans))
            normed[at : at + side, :] = (units * gains).astype(jnp.bfloat16)
    for part in range(tiles):
        slot = step * tiles + part
        rows = slice(part * pixels, (part + 1) * pixels)
        before = jnp.dot(normed[rows, :], w_in[...], preferred_element_type=jnp.float32)
        scaled = before * 0.7071067811865476
        twice = 1.0 + lax.erf(scaled)
        bell = jnp.exp(-(scaled * scaled))
        act = spread(before * twice, lines)
        slope = spread(twice + (scaled * 1.1283791670955126) * bell, lines)
        factor = jnp.broadcast_to(ga[pl.ds(slot, 1), :], (side, hidden))
        factor_inside = factor * inside
        whole = [act[line] for line in range(lines) if not masked[line]]
        partial = [act[line] for line in range(lines) if masked[line]]
        total = functools.reduce(jnp.add, partial) * inside
        if whole:
            total = total + functools.reduce(jnp.add, whole)
        asum[pl.ds(slot, 1), :] += jnp.sum(total, axis=0, keepdims=True)
        for line in range(lines):
            at = part * pixels + line * side
            gb[at : at + side, :] = (slope[line] * (factor_inside if masked[line] else factor)).astype(jnp.bfloat16)
    gi_sum[...] += lax.dot_general(normed[...], gb[...], (((0,), (0,)), ((), ())), preferred_element_type=jnp.float32)
    gain_part = jnp.zeros((side, chans), jnp.float32)
    tap_part = [jnp.zeros((side, chans), jnp.float32) for _ in range(9)]
    for part in range(tiles):
        base = part * pad_rows
        grad_normed = jnp.dot(
            gb[part * pixels : (part + 1) * pixels, :], w_in_t[...], preferred_element_type=jnp.float32
        )
        for line in range(lines):
            at = part * pixels + line * side
            rows = grad_normed[line * side : (line + 1) * side]
            units = unit[at : at + side, :]
            product = rows * units
            gain_part = gain_part + product
            grad_unit = rows * gains
            grad_depth = invs[at : at + side, :] * (
                grad_unit
                - jnp.mean(grad_unit, axis=1, keepdims=True)
                - units * jnp.mean(product * gains, axis=1, keepdims=True)
            )
            for tap in range(9):
                tap_part[tap] = tap_part[tap] + grad_depth * pad[pl.ds(base + starts[line][tap], side), :]
    gain_sum[...] += gain_part
    for tap in range(9):
        tap_sum[tap * side : (tap + 1) * side, :] += tap_part[tap]


def inner_kernel(
    peers,
    work,
    meta,
    dealing,
    feats,
    cot_all,
    kern,
    gain,
    w_in,
    w_in_t,
    w_out_t,
    asum,
    csum,
    ge,
    ga,
    tap_sum,
    gain_sum,
    gi_sum,
    pad,
    unit,
    invs,
    normed,
    gb,
):
    side = feats.shape[1]
    chans = feats.shape[3]
    pixels = side * side
    cot_rows = cot_all.shape[0] // peers
    count, begin, me = meta[0], meta[1], meta[2]
    for ref in (asum, csum, ge, tap_sum, gain_sum, gi_sum, pad):
        ref[...] = jnp.zeros_like(ref)

    @pl.loop(0, count)
    def _(slot):
        rank = lax.rem(begin + slot, peers * work)
        block = dealing[lax.rem(rank, peers)] ^ me
        row = block * cot_rows + lax.div(rank, peers)
        ge[pl.ds(slot, 1), :] = cot_all[pl.ds(row, 1), :] * (1.0 / pixels)

    ga[...] = 0.5 * jnp.dot(
        ge[...], w_out_t[...].astype(jnp.float32), precision=HIGHEST, preferred_element_type=jnp.float32
    )
    starts = [
        [(y - 1 + a) * INNER_PITCH + FIRST - 1 + b for a in range(3) for b in range(3)] for y in range(1, side - 1)
    ]

    @pl.loop(0, lax.div(count + INNER_TILES - 1, INNER_TILES))
    def _(step):
        for part in range(INNER_TILES):
            slot = step * INNER_TILES + part
            base = part * (pad.shape[0] // INNER_TILES)
            total = jnp.zeros((side, chans), jnp.float32)
            for y in range(side):
                row = feats[slot, y].astype(jnp.float32)
                pad[pl.ds(base + y * INNER_PITCH + FIRST, side), :] = row
                total = total + row
            csum[pl.ds(slot, 1), :] = jnp.sum(total, axis=0, keepdims=True)
        run_lines(
            step,
            INNER_TILES,
            starts,
            [True] * len(starts),
            (kern, gain[...], w_in, w_in_t),
            (pad, unit, invs, normed, gb),
            (asum, ga, tap_sum, gain_sum, gi_sum),
        )


def border_kernel(
    peers,
    work,
    parts,
    meta,
    dealing,
    links,
    own,
    inner,
    before_halo,
    after_halo,
    kern,
    gain,
    w_in,
    w_in_t,
    w_out,
    asum_in,
    csum,
    ge,
    ga,
    tap_in,
    gain_in,
    gi_in,
    embed_out,
    grad_out,
    pad,
    unit,
    invs,
    normed,
    gb,
    asum,
    tap_sum,
    gain_sum,
    gi_sum,
    go_sum,
    rows_out,
):
    slots, _, side, chans = own.shape
    hidden = w_in.shape[1]
    pixels = side * side
    count, begin, me, mine = meta[0], meta[1], meta[2], meta[3]
    for target, source in ((asum, asum_in), (tap_sum, tap_in), (gain_sum, gain_in), (gi_sum, gi_in)):
        target[...] = source[...]
    embed_out[...] = jnp.zeros_like(embed_out)

    def strip(column, which, slot):
        link = links[column, slot]
        index = link - (me - 1) * slots
        first = before_halo[jnp.clip(index, 0, slots - 1), which]
        middle = own[jnp.clip(index - slots, 0, slots - 1), which]
        last = after_halo[jnp.clip(index - 2 * slots, 0, slots - 1), which]
        chosen = jnp.where(index < slots, first, jnp.where(index < 2 * slots, middle, last)).astype(jnp.float32)
        return jnp.where(link >= 0, chosen, 0.0)

    across = [a * LINE_PITCH + FIRST - 1 + b for a in range(3) for b in range(3)]
    along = [b * LINE_PITCH + FIRST - 1 + a for a in range(3) for b in range(3)]
    starts = [
        [panel * 3 * LINE_PITCH + start for start in (across if panel < 2 else along)] for panel in range(4)
    ]

    @pl.loop(0, lax.div(count + BORDER_TILES - 1, BORDER_TILES))
    def _(step):
        for part in range(BORDER_TILES):
            slot = step * BORDER_TILES + part
            base = part * (pad.shape[0] // BORDER_TILES)
            up, down, left, right = strip(0, 1, slot), strip(1, 0, slot), strip(2, 3, slot), strip(3, 2, slot)
            upper_left, upper_right = strip(4, 1, slot)[side - 1 :], strip(5, 1, slot)[:1]
            lower_left, lower_right = strip(6, 0, slot)[side - 1 :], strip(7, 0, slot)[:1]
            rows = [own[slot, i].astype(jnp.float32) for i in range(4)]
            deep = [inner[slot, i].astype(jnp.float32) for i in range(4)]

            def cut(line, at):
                return line[at : at + 1]

            end = side - 1
            panels = (
                (
                    (upper_left, up, upper_right),
                    (cut(left, 0), rows[0], cut(right, 0)),
                    (cut(left, 1), deep[0], cut(right, 1)),
                ),
                (
                    (cut(left, end - 1), deep[1], cut(right, end - 1)),
                    (cut(left, end), rows[1], cut(right, end)),
                    (lower_left, down, lower_right),
                ),
                (
                    (upper_left, left, lower_left),
                    (cut(up, 0), rows[2], cut(down, 0)),
                    (cut(up, 1), deep[2], cut(down, 1)),
                ),
                (
                    (cut(up, end - 1), deep[3], cut(down, end - 1)),
                    (cut(up, end), rows[3], cut(down, end)),
                    (upper_right, right, lower_right),
                ),
            )
            for panel in range(4):
                for line in range(3):
                    at = base + (panel * 3 + line) * LINE_PITCH + FIRST
                    head, body, tail = panels[panel][line]
                    pad[pl.ds(at - 1, 1), :] = head
                    pad[pl.ds(at, side), :] = body
                    pad[pl.ds(at + side, 1), :] = tail
        run_lines(
            step,
            BORDER_TILES,
            starts,
            [False, False, True, True],
            (kern, gain[...], w_in, w_in_t),
            (pad, unit, invs, normed, gb),
            (asum, ga, tap_sum, gain_sum, gi_sum),
        )

    asum[...] = 0.5 * asum[...]
    go_sum[...] = lax.dot_general(
        asum[...], ge[...], (((0,), (0,)), ((), ())), precision=HIGHEST, preferred_element_type=jnp.float32
    )
    projected = jnp.dot(
        asum[...], w_out[...].astype(jnp.float32), precision=HIGHEST, preferred_element_type=jnp.float32
    )
    rows_out[...] = (csum[...] + projected) * (1.0 / pixels)

    @pl.loop(0, count)
    def _(slot):
        rank = lax.rem(begin + slot, peers * work)
        block = dealing[lax.rem(rank, peers)] ^ me
        embed_out[pl.ds(block * work + lax.div(rank, peers), 1), :] = rows_out[pl.ds(slot, 1), :]

    per = hidden // parts
    for block in range(parts):
        to = block ^ mine
        columns, offset = divmod(block * per, chans)
        grad_out[to, :per, :] = gi_sum[offset : offset + per, columns * chans : (columns + 1) * chans]
        grad_out[to, per : 2 * per, :] = go_sum[block * per : (block + 1) * per, :]
        grad_out[to, 2 * per :, :] = jnp.zeros((SMALL_ROWS, chans), jnp.float32)
    for i in range(9):
        grad_out[(i // SMALL_ROWS) ^ mine, pl.ds(2 * per + i % SMALL_ROWS, 1), :] = jnp.sum(
            tap_sum[i * side : (i + 1) * side, :], axis=0, keepdims=True
        )
    grad_out[1 ^ mine, pl.ds(2 * per + 1, 1), :] = jnp.sum(gain_sum[...], axis=0, keepdims=True)


def unpack_kernel(parts, meta, packed, gk, gg, gi, go):
    mine = meta[3]
    hidden, chans = go.shape
    per = hidden // parts
    for block in range(parts):
        at = block ^ mine
        columns, offset = divmod(block * per, chans)
        gi[offset : offset + per, columns * chans : (columns + 1) * chans] = packed[at, :per, :]
        go[block * per : (block + 1) * per, :] = packed[at, per : 2 * per, :]
    gk[:SMALL_ROWS, :] = packed[mine, 2 * per :, :]
    gk[SMALL_ROWS:9, :] = packed[1 ^ mine, 2 * per : 2 * per + 1, :]
    gg[...] = packed[1 ^ mine, 2 * per + 1 : 2 * per + 2, :]


def local(features, tissue_count, neighbors, worker_perm, rotation, kernel, gain, w_in, w_out, cotangent):
    feats = features[0]
    slots, side, _, chans = feats.shape
    hidden = w_in.shape[1]
    cot_rows = cotangent[0]
    work = cot_rows.shape[0]
    peers = lax.axis_size("tile")
    slides = lax.axis_size("slide")
    me = lax.axis_index("tile")
    slide_bits, tile_bits = bits_of(slides), bits_of(peers)
    halving = [("slide", bit) for bit in slide_bits] + [("tile", tile_bits[0])]
    parts = 1 << len(halving)
    mine = jnp.zeros((), jnp.int32)
    for place, (axis, bit) in enumerate(reversed(halving)):
        mine = mine + jnp.where((lax.axis_index(axis) & bit) > 0, 1 << place, 0)

    strips, inner = border_strips(feats)
    gathered = jnp.concatenate(
        [cot_rows, jnp.broadcast_to(tissue_count.astype(jnp.float32), (8, chans))], axis=0
    )[None]
    for bit in tile_bits:
        gathered = jnp.concatenate([gathered, swap(gathered, "tile", bit)], axis=0)
    gathered, strips = lax.optimization_barrier((gathered, strips))
    before_halo = lax.ppermute(strips, "tile", [(i, i + 1) for i in range(peers - 1)])
    after_halo = lax.ppermute(strips, "tile", [(i + 1, i) for i in range(peers - 1)])

    counts = gathered[:, work, 0].astype(jnp.int32)
    whose = jnp.arange(peers, dtype=jnp.int32) ^ me
    begin = jnp.sum(jnp.where(whose < me, counts, 0)) + rotation[0]
    meta = jnp.stack([tissue_count[0, 0], begin, me, mine]).astype(jnp.int32)

    f32 = jnp.float32
    vmem = pl.BlockSpec(memory_space=pltpu.VMEM)
    smem = pl.BlockSpec(memory_space=pltpu.SMEM)
    shape = jax.ShapeDtypeStruct
    params = pltpu.CompilerParams(vmem_limit_bytes=VMEM_BYTES)
    taps, gains, w_in_t = kernel.astype(f32), gain[None], w_in.T
    per = hidden // parts
    block_rows = 2 * per + SMALL_ROWS

    def line_scratch(pad_rows, pixels):
        return [
            pltpu.VMEM((pad_rows, chans), f32),
            pltpu.VMEM((pixels, chans), f32),
            pltpu.VMEM((pixels, chans), f32),
            pltpu.VMEM((pixels, chans), jnp.bfloat16),
            pltpu.VMEM((pixels, hidden), jnp.bfloat16),
        ]

    asum, csum, ge, ga, tap_sum, gain_sum, gi_sum = pl.pallas_call(
        functools.partial(inner_kernel, peers, work),
        in_specs=[smem] * 2 + [vmem] * 7,
        out_specs=[vmem] * 7,
        out_shape=[
            shape((slots, hidden), f32),
            shape((slots, chans), f32),
            shape((slots, chans), f32),
            shape((slots, hidden), f32),
            shape((9 * side, chans), f32),
            shape((side, chans), f32),
            shape((chans, hidden), f32),
        ],
        scratch_shapes=line_scratch(INNER_TILES * (side + 1) * INNER_PITCH, INNER_TILES * side * (side - 2)),
        compiler_params=params,
        cost_estimate=pl.CostEstimate(flops=30 * 10**9, bytes_accessed=10**7, transcendentals=10**7),
    )(
        meta,
        worker_perm[0],
        feats,
        gathered.reshape(peers * (work + 8), chans),
        taps,
        gains,
        w_in,
        w_in_t,
        w_out.T,
    )
    embeds, packed = pl.pallas_call(
        functools.partial(border_kernel, peers, work, parts),
        in_specs=[smem] * 3 + [vmem] * 16,
        out_specs=[vmem] * 2,
        out_shape=[shape((peers * work, chans), f32), shape((parts, block_rows, chans), f32)],
        scratch_shapes=line_scratch(BORDER_TILES * 12 * LINE_PITCH, BORDER_TILES * 4 * side)
        + [
            pltpu.VMEM((slots, hidden), f32),
            pltpu.VMEM((9 * side, chans), f32),
            pltpu.VMEM((side, chans), f32),
            pltpu.VMEM((chans, hidden), f32),
            pltpu.VMEM((hidden, chans), f32),
            pltpu.VMEM((slots, chans), f32),
        ],
        compiler_params=params,
    )(
        meta,
        worker_perm[0],
        neighbors[0].T,
        strips,
        inner,
        before_halo,
        after_halo,
        taps,
        gains,
        w_in,
        w_in_t,
        w_out,
        asum,
        csum,
        ge,
        ga,
        tap_sum,
        gain_sum,
        gi_sum,
    )

    held = packed
    for axis, bit in halving[:-1]:
        half = held.shape[0] // 2
        held = held[:half] + swap(held[half:], axis, bit)
    embeds = embeds.reshape(peers, work, chans)
    for place, bit in enumerate(tile_bits):
        paired = embeds.reshape(embeds.shape[0] // 2, 2, work, chans)
        keep, send = paired[:, 0], paired[:, 1]
        if place == 0:
            mine_part, other_part = held[0], held[1]
        else:
            mine_part, other_part = held, held
        outgoing = jnp.concatenate([send.reshape(-1, chans), other_part], axis=0)
        incoming = swap(outgoing, "tile", bit)
        rows = send.shape[0] * work
        embeds = keep + incoming[:rows].reshape(keep.shape)
        held = mine_part + incoming[rows:]
    held = held[None]
    for axis, bit in reversed(halving):
        held = jnp.concatenate([held, swap(held, axis, bit)], axis=0)
    gk, gg, gi, go = pl.pallas_call(
        functools.partial(unpack_kernel, parts),
        in_specs=[smem, vmem],
        out_specs=[vmem] * 4,
        out_shape=[
            jax.ShapeDtypeStruct((9, chans), f32),
            jax.ShapeDtypeStruct((1, chans), f32),
            jax.ShapeDtypeStruct((chans, hidden), f32),
            jax.ShapeDtypeStruct((hidden, chans), f32),
        ],
    )(meta, held)
    return embeds, gk, gg[0], gi, go


def solution(mesh):
    placed = (
        P("slide", "tile", None, None, None),
        P("slide", "tile"),
        P("slide", "tile", None),
        P("slide", None),
        P("slide"),
        P(),
        P(),
        P(),
        P(),
        P("slide", "tile", None),
    )
    return jax.shard_map(
        local,
        mesh=mesh,
        in_specs=placed,
        out_specs=(P("slide", "tile", None), P(), P(), P(), P()),
        check_vma=False,
    )
```

time: 159 us -> 125 us (0.79)
  waiting for transfers between devices: 67.3 us -> 45.5 us
  Pallas kernels: 56.2 us -> 39.6 us
  starting transfers between devices: 22.3 us -> 27.5 us
    ppermute x11, waiting for transfers between devices: 67.3 us -> 30.2 us  [swap(): return lax.ppermute(value, axis, [(i, i ^ bit) for i in range(count)])]
    pallas_call x1 -> x2, Pallas kernels: 49.9 us -> 33 us  [the longest x1 21.8 us: local(): pl.pallas_call(functools.partial(inner_kernel, peers, work), in_specs=[sm...]
    ppermute x1, waiting for transfers between devices: 0.01 us -> 15.3 us  [local(): lax.ppermute(strips, 'tile', [(i, i + 1) for i in range(peers - 1)])]
    ppermute x11, starting transfers between devices: 15.4 us -> 21.6 us  [swap(): return lax.ppermute(value, axis, [(i, i ^ bit) for i in range(count)])]
    unnamed x16 -> x20, local copies, waits for them, and re-layouts: 2.89 us -> 4.24 us
  transfers between devices with their start and end apart: 13 -> 13, of which waited for: 10 -> 11; matrix products, arithmetic and copies ran while one was open for 3% -> 3% of each run, Pallas kernels for 0% -> 21%
where the time goes in v2:
time: 125 us; the launch traced here: 124 us
  waiting for transfers between devices  45.5 us (36%)
  Pallas kernels  39.6 us (32%)
  starting transfers between devices  27.5 us (22%)
  local copies, waits for them, and re-layouts  5.03 us (4%)
  other arithmetic  3.31 us (3%)
  between operations  2.86 us (2%)
    ppermute x11, waiting for transfers between devices, swap(): return lax.ppermute(value, axis, [(i, i ^ bit) for i in range(count)])  30.2 us
    pallas_call x1, Pallas kernels, local(): pl.pallas_call(functools.partial(inner_kernel, peers, work), in_specs=[sm...  21.8 us
    ppermute x11, starting transfers between devices, swap(): return lax.ppermute(value, axis, [(i, i ^ bit) for i in range(count)])  21.6 us
    ppermute x1, waiting for transfers between devices, local(): lax.ppermute(strips, 'tile', [(i, i + 1) for i in range(peers - 1)])  15.3 us
    pallas_call x1, Pallas kernels, local(): pl.pallas_call(functools.partial(border_kernel, peers, work, parts), in_s...  11.2 us
    pallas_call x1, Pallas kernels, border_strips(): pl.pallas_call(strip_kernel, grid=(slots // step,), in_specs=[pl.BlockSpe...  4.64 us
    ppermute x1, starting transfers between devices, local(): lax.ppermute(strips, 'tile', [(i, i + 1) for i in range(peers - 1)])  4.61 us
    unnamed x20, local copies, waits for them, and re-layouts  4.24 us
  transfers between devices with their start and end apart: 13, of which 11 were waited for; matrix products, arithmetic and copies ran while one was open for 3% of the time, Pallas kernels for 21%

profile of v2, /device:TPU:0, one launch (start us, length us, event | category | flops | bytes accessed | tf_op | source)
XLA Modules:
  0.0 123.8 jit_solution(13017512803392787596)
XLA Ops:
  0.6 0.0 copy-start.3
  0.6 0.0 copy-start.8
  0.7 0.0 copy-start.7
  1.3 0.7 pad_bitcast_fusion
  2.1 3.0 %collective-permute-start = (f32[1,40,128]{2,1,0:T(8,128)S(1)}, f32[1,40,128]{2,1,0:T(8,128)S(1)}, u32[]{:S(2)}, u32[]{:S(2)}) collective-permute-start(f32[1,40,128]{2,1,0:T(8,128)S(1)} %pad_bitcast_fusion), channel_id=1, source_target_pairs={{0,1},{1,0},{2,3},{3,2},{4,5},{5,4},{6,7},{7,6},{8,9},{9,8},{10,11... | collective-permute-start | bytes 61448 | tf_op jit(solution)/shard_map/ppermute | solution.py:26
  5.0 1.8 %collective-permute-done = f32[1,40,128]{2,1,0:T(8,128)S(1)} collective-permute-done((f32[1,40,128]{2,1,0:T(8,128)S(1)}, f32[1,40,128]{2,1,0:T(8,128)S(1)}, u32[]{:S(2)}, u32[]{:S(2)}) %collective-permute-start) | collective-permute-done | bytes 20512 | tf_op jit(solution)/shard_map/ppermute | solution.py:26
  6.8 2.1 %collective-permute-start.1 = (f32[2,40,128]{2,1,0:T(8,128)S(1)}, f32[2,40,128]{2,1,0:T(8,128)S(1)}, u32[]{:S(2)}, u32[]{:S(2)}) collective-permute-start(f32[2,40,128]{2,1,0:T(8,128)S(1)} %pad_maximum_fusion.8), channel_id=1, source_target_pairs={{0,2},{1,3},{2,0},{3,1},{4,6},{5,7},{6,4},{7,5},{8,10},{9,11},{10,... | collective-permute-start | bytes 122888 | tf_op jit(solution)/shard_map/ppermute | solution.py:26
  8.9 2.0 %collective-permute-done.1 = f32[2,40,128]{2,1,0:T(8,128)S(1)} collective-permute-done((f32[2,40,128]{2,1,0:T(8,128)S(1)}, f32[2,40,128]{2,1,0:T(8,128)S(1)}, u32[]{:S(2)}, u32[]{:S(2)}) %collective-permute-start.1) | collective-permute-done | bytes 40992 | tf_op jit(solution)/shard_map/ppermute | solution.py:26
  10.9 3.0 %collective-permute-start.2 = (f32[4,40,128]{2,1,0:T(8,128)S(1)}, f32[4,40,128]{2,1,0:T(8,128)S(1)}, u32[]{:S(2)}, u32[]{:S(2)}) collective-permute-start(f32[4,40,128]{2,1,0:T(8,128)S(1)} %pad_maximum_fusion.7), channel_id=1, source_target_pairs={{0,4},{1,5},{2,6},{3,7},{4,0},{5,1},{6,2},{7,3},{8,12},{9,13},{10,... | collective-permute-start | bytes 245768 | tf_op jit(solution)/shard_map/ppermute | solution.py:26
  14.6 0.7 convert_element_type.15.kern
  15.2 1.0 copy.19
  16.3 1.0 copy.18
  17.3 4.6 %shard_map.137 = (bf16[64,4,16,128]{3,2,1,0:T(8,128)(2,1)}, bf16[64,4,16,128]{3,2,1,0:T(8,128)(2,1)}) custom-call(bf16[64,16,16,128]{3,2,1,0:T(8,128)(2,1)} %bitcast.55), custom_call_target="tpu_custom_call" | custom-call | tf_op jit(solution)/shard_map/pallas_call | solution.py:47
  21.9 0.0 collective-permute-done.2
  21.9 1.3 %collective-permute-start.4 = (bf16[64,4,16,128]{3,2,1,0:T(8,128)(2,1)}, bf16[64,4,16,128]{3,2,1,0:T(8,128)(2,1)S(1)}, u32[]{:S(2)}, u32[]{:S(2)}) collective-permute-start(bf16[64,4,16,128]{3,2,1,0:T(8,128)(2,1)} %get-tuple-element.24.own), channel_id=1, source_target_pairs={{1,0},{2,1},{3,2},{4,3},{5,4},{6,5},{7,6},{9,8},{10,9},{11,10},{12... | collective-permute-start | bytes 3145736 | tf_op jit(solution)/shard_map/ppermute | solution.py:386
  23.2 4.6 %collective-permute-start.3 = (bf16[64,4,16,128]{3,2,1,0:T(8,128)(2,1)}, bf16[64,4,16,128]{3,2,1,0:T(8,128)(2,1)S(1)}, u32[]{:S(2)}, u32[]{:S(2)}) collective-permute-start(bf16[64,4,16,128]{3,2,1,0:T(8,128)(2,1)} %get-tuple-element.24.own), channel_id=1, source_target_pairs={{0,1},{1,2},{2,3},{3,4},{4,5},{5,6},{6,7},{8,9},{9,10},{10,11},{11... | collective-permute-start | bytes 3145736 | tf_op jit(solution)/shard_map/ppermute | solution.py:385
  27.9 0.2 convert_reduce_fusion
  28.1 0.6 fusion.3
  29.4 0.1 pad_add_fusion.meta
  29.5 0.0 copy-done.3
  29.5 0.0 copy-done.8
  29.5 0.0 copy-done.7
  29.5 0.0 copy-start
  29.5 2.2 %copy-done = bf16[1,64,16,16,128]{4,3,2,1,0:T(8,128)(2,1)S(1)} copy-done((bf16[1,64,16,16,128]{4,3,2,1,0:T(8,128)(2,1)S(1)}, bf16[1,64,16,16,128]{4,3,2,1,0:T(8,128)(2,1)}, u32[]{:S(2)}) %copy-start) | copy-done | bytes 4194328
  31.7 21.8 %shard_map.138 = (f32[64,512]{1,0:T(8,128)S(1)}, f32[64,128]{1,0:T(8,128)S(1)}, f32[64,128]{1,0:T(8,128)S(1)}, f32[64,512]{1,0:T(8,128)S(1)}, f32[144,128]{1,0:T...) custom-call(s32[4]{0:T(128)S(1)} %pad_add_fusion.meta, s32[8]{0:T(128)S(1)} %bitcast.63, ...), custom_call_target="tpu_custom_call" | custom-call | flops 30000001024 | bytes 10000000 | tf_op jit(solution)/shard_map/pallas_call | solution.py:411
  53.5 0.0 collective-permute-done.4.after_halo
  53.6 15.3 %collective-permute-done.3.before_halo = bf16[64,4,16,128]{3,2,1,0:T(8,128)(2,1)S(1)} collective-permute-done((bf16[64,4,16,128]{3,2,1,0:T(8,128)(2,1)}, bf16[64,4,16,128]{3,2,1,0:T(8,128)(2,1)S(1)}, u32[]{:S(2)}, u32[]{:S(2)}) %collective-permute-start.3) | collective-permute-done | bytes 1048608 | tf_op jit(solution)/shard_map/ppermute | solution.py:385
  68.9 0.0 copy-done.5
  68.9 11.2 %shard_map.139 = (f32[256,128]{1,0:T(8,128)S(1)}, f32[8,136,128]{2,1,0:T(8,128)S(1)}) custom-call(s32[4]{0:T(128)S(1)} %pad_add_fusion.meta, s32[8]{0:T(128)S(1)} %bitcast.64, s32[8,64]{1,0:T(8,128)S(1)} %bitcast.62, bf16[64,4,16,128]{3,2,1,0:T(8,128)(2,1)S(1)} %copy-done.1, bf16[64,4,16,128]{3,2,1,0:T(8,128)(2,1)S(1)} %copy-done.2, ...), custom_call_target="tpu_custom_call" | custom-call | tf_op jit(solution)/shard_map/pallas_call | solution.py:438
  80.1 2.2 %collective-permute-start.5 = (f32[4,136,128]{2,1,0:T(8,128)S(1)}, f32[4,136,128]{2,1,0:T(8,128)S(1)}, u32[]{:S(2)}, u32[]{:S(2)}) collective-permute-start(f32[4,136,128]{2,1,0:T(8,128)S(1)} %slice.61), channel_id=1, source_target_pairs={{0,8},{8,0},{16,24},{24,16},{1,9},{9,1},{17,25},{25,17},{2,10},{10... | collective-permute-start | bytes 835592 | tf_op jit(solution)/shard_map/ppermute | solution.py:26
  82.3 1.2 collective-permute-done.5
  83.5 3.5 %collective-permute-start.6 = (f32[2,136,128]{2,1,0:T(8,128)S(1)}, f32[2,136,128]{2,1,0:T(8,128)S(1)}, u32[]{:S(2)}, u32[]{:S(2)}) collective-permute-start(f32[2,136,128]{2,1,0:T(8,128)S(1)} %slice.79), channel_id=1, source_target_pairs={{0,16},{8,24},{16,0},{24,8},{1,17},{9,25},{17,1},{25,9},{2,18},{10... | collective-permute-start | bytes 417800 | tf_op jit(solution)/shard_map/ppermute | solution.py:26
  87.1 4.2 %collective-permute-done.6 = f32[2,136,128]{2,1,0:T(8,128)S(1)} collective-permute-done((f32[2,136,128]{2,1,0:T(8,128)S(1)}, f32[2,136,128]{2,1,0:T(8,128)S(1)}, u32[]{:S(2)}, u32[]{:S(2)}) %collective-permute-start.6) | collective-permute-done | bytes 139296 | tf_op jit(solution)/shard_map/ppermute | solution.py:26
  91.3 0.1 collective-permute-start.7
  91.4 5.3 %collective-permute-done.7 = f32[264,128]{1,0:T(8,128)S(1)} collective-permute-done((f32[264,128]{1,0:T(8,128)S(1)}, f32[264,128]{1,0:T(8,128)S(1)}, u32[]{:S(2)}, u32[]{:S(2)}) %collective-permute-start.7) | collective-permute-done | bytes 135200 | tf_op jit(solution)/shard_map/ppermute | solution.py:26
  96.7 4.6 %collective-permute-start.8 = (f32[200,128]{1,0:T(8,128)S(1)}, f32[200,128]{1,0:T(8,128)S(1)}, u32[]{:S(2)}, u32[]{:S(2)}) collective-permute-start(f32[200,128]{1,0:T(8,128)S(1)} %pad_maximum_fusion.5), channel_id=1, source_target_pairs={{0,2},{1,3},{2,0},{3,1},{4,6},{5,7},{6,4},{7,5},{8,10},{9,11},{10,... | collective-permute-start | bytes 307208 | tf_op jit(solution)/shard_map/ppermute | solution.py:26
  101.3 3.0 %collective-permute-done.8 = f32[200,128]{1,0:T(8,128)S(1)} collective-permute-done((f32[200,128]{1,0:T(8,128)S(1)}, f32[200,128]{1,0:T(8,128)S(1)}, u32[]{:S(2)}, u32[]{:S(2)}) %collective-permute-start.8) | collective-permute-done | bytes 102432 | tf_op jit(solution)/shard_map/ppermute | solution.py:26
  104.4 0.2 collective-permute-start.9
  104.6 5.2 %collective-permute-done.9 = f32[168,128]{1,0:T(8,128)S(1)} collective-permute-done((f32[168,128]{1,0:T(8,128)S(1)}, f32[168,128]{1,0:T(8,128)S(1)}, u32[]{:S(2)}, u32[]{:S(2)}) %collective-permute-start.9) | collective-permute-done | bytes 86048 | tf_op jit(solution)/shard_map/ppermute | solution.py:26
  109.9 1.6 %collective-permute-start.10 = (f32[1,136,128]{2,1,0:T(8,128)S(1)}, f32[1,136,128]{2,1,0:T(8,128)S(1)}, u32[]{:S(2)}, u32[]{:S(2)}) collective-permute-start(f32[1,136,128]{2,1,0:T(8,128)S(1)} %fusion), channel_id=1, source_target_pairs={{0,1},{1,0},{2,3},{3,2},{4,5},{5,4},{6,7},{7,6},{8,9},{9,8},{10,11... | collective-permute-start | bytes 208904 | tf_op jit(solution)/shard_map/ppermute | solution.py:26
  111.5 2.8 %collective-permute-done.10 = f32[1,136,128]{2,1,0:T(8,128)S(1)} collective-permute-done((f32[1,136,128]{2,1,0:T(8,128)S(1)}, f32[1,136,128]{2,1,0:T(8,128)S(1)}, u32[]{:S(2)}, u32[]{:S(2)}) %collective-permute-start.10) | collective-permute-done | bytes 69664 | tf_op jit(solution)/shard_map/ppermute | solution.py:26
  114.3 1.3 %collective-permute-start.11 = (f32[2,136,128]{2,1,0:T(8,128)S(1)}, f32[2,136,128]{2,1,0:T(8,128)S(1)}, u32[]{:S(2)}, u32[]{:S(2)}) collective-permute-start(f32[2,136,128]{2,1,0:T(8,128)S(1)} %pad_maximum_fusion.3), channel_id=1, source_target_pairs={{0,16},{8,24},{16,0},{24,8},{1,17},{9,25},{17,1},{25,9},{2,18},{10... | collective-permute-start | bytes 417800 | tf_op jit(solution)/shard_map/ppermute | solution.py:26
  115.6 3.8 %collective-permute-done.11 = f32[2,136,128]{2,1,0:T(8,128)S(1)} collective-permute-done((f32[2,136,128]{2,1,0:T(8,128)S(1)}, f32[2,136,128]{2,1,0:T(8,128)S(1)}, u32[]{:S(2)}, u32[]{:S(2)}) %collective-permute-start.11) | collective-permute-done | bytes 139296 | tf_op jit(solution)/shard_map/ppermute | solution.py:26
  119.4 0.1 collective-permute-start.12
  119.5 0.6 fusion.2
  120.1 0.9 collective-permute-done.12
  121.1 0.8 pad_maximum_fusion.packed
  121.9 1.9 %shard_map.140 = (f32[9,128]{1,0:T(8,128)}, f32[1,128]{1,0:T(1,128)}, f32[128,512]{1,0:T(8,128)}, f32[512,128]{1,0:T(8,128)}) custom-call(s32[4]{0:T(128)} %copy-done.5, f32[8,136,128]{2,1,0:T(8,128)} %pad_maximum_fusion.packed), custom_call_target="tpu_custom_call" | custom-call | tf_op jit(solution)/shard_map/pallas_call | solution.py:495
  (32 shorter events, 0.3 us)
Async XLA Ops:
  0.6 28.9 %copy-start.3 = (bf16[128,512]{1,0:T(8,128)(2,1)S(1)}, bf16[128,512]{1,0:T(8,128)(2,1)}, u32[]{:S(2)}) copy-start(bf16[128,512]{1,0:T(8,128)(2,1)} %w_in.3) | copy-start | bytes 393220
  0.6 28.8 %copy-start.8 = (f32[128]{0:T(128)S(1)}, f32[128]{0:T(128)}, u32[]{:S(2)}) copy-start(f32[128]{0:T(128)} %param.16) | copy-start | bytes 1540
  0.7 28.8 %copy-start.7 = (s32[1,8]{1,0:T(1,128)S(1)}, s32[1,8]{1,0:T(1,128)}, u32[]{:S(2)}) copy-start(s32[1,8]{1,0:T(1,128)} %param.13) | copy-start | bytes 100
  2.1 4.7 %collective-permute-start = (f32[1,40,128]{2,1,0:T(8,128)S(1)}, f32[1,40,128]{2,1,0:T(8,128)S(1)}, u32[]{:S(2)}, u32[]{:S(2)}) collective-permute-start(f32[1,40,128]{2,1,0:T(8,128)S(1)} %pad_bitcast_fusion), channel_id=1, source_target_pairs={{0,1},{1,0},{2,3},{3,2},{4,5},{5,4},{6,7},{7,6},{8,9},{9,8},{10,11... | collective-permute-start | bytes 61448 | tf_op jit(solution)/shard_map/ppermute | solution.py:26
  6.8 4.1 %collective-permute-start.1 = (f32[2,40,128]{2,1,0:T(8,128)S(1)}, f32[2,40,128]{2,1,0:T(8,128)S(1)}, u32[]{:S(2)}, u32[]{:S(2)}) collective-permute-start(f32[2,40,128]{2,1,0:T(8,128)S(1)} %pad_maximum_fusion.8), channel_id=1, source_target_pairs={{0,2},{1,3},{2,0},{3,1},{4,6},{5,7},{6,4},{7,5},{8,10},{9,11},{10,... | collective-permute-start | bytes 122888 | tf_op jit(solution)/shard_map/ppermute | solution.py:26
  10.9 11.1 %collective-permute-start.2 = (f32[4,40,128]{2,1,0:T(8,128)S(1)}, f32[4,40,128]{2,1,0:T(8,128)S(1)}, u32[]{:S(2)}, u32[]{:S(2)}) collective-permute-start(f32[4,40,128]{2,1,0:T(8,128)S(1)} %pad_maximum_fusion.7), channel_id=1, source_target_pairs={{0,4},{1,5},{2,6},{3,7},{4,0},{5,1},{6,2},{7,3},{8,12},{9,13},{10,... | collective-permute-start | bytes 245768 | tf_op jit(solution)/shard_map/ppermute | solution.py:26
  21.9 31.6 %collective-permute-start.4 = (bf16[64,4,16,128]{3,2,1,0:T(8,128)(2,1)}, bf16[64,4,16,128]{3,2,1,0:T(8,128)(2,1)S(1)}, u32[]{:S(2)}, u32[]{:S(2)}) collective-permute-start(bf16[64,4,16,128]{3,2,1,0:T(8,128)(2,1)} %get-tuple-element.24.own), channel_id=1, source_target_pairs={{1,0},{2,1},{3,2},{4,3},{5,4},{6,5},{7,6},{9,8},{10,9},{11,10},{12... | collective-permute-start | bytes 3145736 | tf_op jit(solution)/shard_map/ppermute | solution.py:386
  23.2 45.6 %collective-permute-start.3 = (bf16[64,4,16,128]{3,2,1,0:T(8,128)(2,1)}, bf16[64,4,16,128]{3,2,1,0:T(8,128)(2,1)S(1)}, u32[]{:S(2)}, u32[]{:S(2)}) collective-permute-start(bf16[64,4,16,128]{3,2,1,0:T(8,128)(2,1)} %get-tuple-element.24.own), channel_id=1, source_target_pairs={{0,1},{1,2},{2,3},{3,4},{4,5},{5,6},{6,7},{8,9},{9,10},{10,11},{11... | collective-permute-start | bytes 3145736 | tf_op jit(solution)/shard_map/ppermute | solution.py:385
  29.5 39.4 %copy-start.5 = (s32[4]{0:T(128)}, s32[4]{0:T(128)S(1)}, u32[]{:S(2)}) copy-start(s32[4]{0:T(128)S(1)} %pad_add_fusion.meta) | copy-start | bytes 52
  29.5 2.2 %copy-start = (bf16[1,64,16,16,128]{4,3,2,1,0:T(8,128)(2,1)S(1)}, bf16[1,64,16,16,128]{4,3,2,1,0:T(8,128)(2,1)}, u32[]{:S(2)}) copy-start(bf16[1,64,16,16,128]{4,3,2,1,0:T(8,128)(2,1)} %param.10) | copy-start | bytes 12582916
  31.7 37.2 %copy-start.1 = (bf16[64,4,16,128]{3,2,1,0:T(8,128)(2,1)S(1)}, bf16[64,4,16,128]{3,2,1,0:T(8,128)(2,1)}, u32[]{:S(2)}) copy-start(bf16[64,4,16,128]{3,2,1,0:T(8,128)(2,1)} %get-tuple-element.24.own) | copy-start | bytes 3145732
  31.7 37.2 %copy-start.2 = (bf16[64,4,16,128]{3,2,1,0:T(8,128)(2,1)S(1)}, bf16[64,4,16,128]{3,2,1,0:T(8,128)(2,1)}, u32[]{:S(2)}) copy-start(bf16[64,4,16,128]{3,2,1,0:T(8,128)(2,1)} %get-tuple-element.25.inner) | copy-start | bytes 3145732
  31.7 37.2 %copy-start.4 = (bf16[512,128]{1,0:T(8,128)(2,1)S(1)}, bf16[512,128]{1,0:T(8,128)(2,1)}, u32[]{:S(2)}) copy-start(bf16[512,128]{1,0:T(8,128)(2,1)} %w_out.1) | copy-start | bytes 393220
  31.7 37.2 %copy-start.6 = (s32[1,64,8]{1,2,0:T(8,128)S(1)}, s32[1,64,8]{1,2,0:T(8,128)}, u32[]{:S(2)}) copy-start(s32[1,64,8]{1,2,0:T(8,128)} %param.12) | copy-start | bytes 6148
  80.1 3.4 %collective-permute-start.5 = (f32[4,136,128]{2,1,0:T(8,128)S(1)}, f32[4,136,128]{2,1,0:T(8,128)S(1)}, u32[]{:S(2)}, u32[]{:S(2)}) collective-permute-start(f32[4,136,128]{2,1,0:T(8,128)S(1)} %slice.61), channel_id=1, source_target_pairs={{0,8},{8,0},{16,24},{24,16},{1,9},{9,1},{17,25},{25,17},{2,10},{10... | collective-permute-start | bytes 835592 | tf_op jit(solution)/shard_map/ppermute | solution.py:26
  83.5 7.7 %collective-permute-start.6 = (f32[2,136,128]{2,1,0:T(8,128)S(1)}, f32[2,136,128]{2,1,0:T(8,128)S(1)}, u32[]{:S(2)}, u32[]{:S(2)}) collective-permute-start(f32[2,136,128]{2,1,0:T(8,128)S(1)} %slice.79), channel_id=1, source_target_pairs={{0,16},{8,24},{16,0},{24,8},{1,17},{9,25},{17,1},{25,9},{2,18},{10... | collective-permute-start | bytes 417800 | tf_op jit(solution)/shard_map/ppermute | solution.py:26
  91.3 5.4 %collective-permute-start.7 = (f32[264,128]{1,0:T(8,128)S(1)}, f32[264,128]{1,0:T(8,128)S(1)}, u32[]{:S(2)}, u32[]{:S(2)}) collective-permute-start(f32[264,128]{1,0:T(8,128)S(1)} %pad_maximum_fusion.4), channel_id=1, source_target_pairs={{0,1},{1,0},{2,3},{3,2},{4,5},{5,4},{6,7},{7,6},{8,9},{9,8},{10,11... | collective-permute-start | bytes 405512 | tf_op jit(solution)/shard_map/ppermute | solution.py:26
  96.7 7.6 %collective-permute-start.8 = (f32[200,128]{1,0:T(8,128)S(1)}, f32[200,128]{1,0:T(8,128)S(1)}, u32[]{:S(2)}, u32[]{:S(2)}) collective-permute-start(f32[200,128]{1,0:T(8,128)S(1)} %pad_maximum_fusion.5), channel_id=1, source_target_pairs={{0,2},{1,3},{2,0},{3,1},{4,6},{5,7},{6,4},{7,5},{8,10},{9,11},{10,... | collective-permute-start | bytes 307208 | tf_op jit(solution)/shard_map/ppermute | solution.py:26
  104.4 5.4 %collective-permute-start.9 = (f32[168,128]{1,0:T(8,128)S(1)}, f32[168,128]{1,0:T(8,128)S(1)}, u32[]{:S(2)}, u32[]{:S(2)}) collective-permute-start(f32[168,128]{1,0:T(8,128)S(1)} %pad_maximum_fusion.6), channel_id=1, source_target_pairs={{0,4},{1,5},{2,6},{3,7},{4,0},{5,1},{6,2},{7,3},{8,12},{9,13},{10,... | collective-permute-start | bytes 258056 | tf_op jit(solution)/shard_map/ppermute | solution.py:26
  109.9 4.4 %collective-permute-start.10 = (f32[1,136,128]{2,1,0:T(8,128)S(1)}, f32[1,136,128]{2,1,0:T(8,128)S(1)}, u32[]{:S(2)}, u32[]{:S(2)}) collective-permute-start(f32[1,136,128]{2,1,0:T(8,128)S(1)} %fusion), channel_id=1, source_target_pairs={{0,1},{1,0},{2,3},{3,2},{4,5},{5,4},{6,7},{7,6},{8,9},{9,8},{10,11... | collective-permute-start | bytes 208904 | tf_op jit(solution)/shard_map/ppermute | solution.py:26
  114.3 5.1 %collective-permute-start.11 = (f32[2,136,128]{2,1,0:T(8,128)S(1)}, f32[2,136,128]{2,1,0:T(8,128)S(1)}, u32[]{:S(2)}, u32[]{:S(2)}) collective-permute-start(f32[2,136,128]{2,1,0:T(8,128)S(1)} %pad_maximum_fusion.3), channel_id=1, source_target_pairs={{0,16},{8,24},{16,0},{24,8},{1,17},{9,25},{17,1},{25,9},{2,18},{10... | collective-permute-start | bytes 417800 | tf_op jit(solution)/shard_map/ppermute | solution.py:26
  119.4 1.6 %collective-permute-start.12 = (f32[4,136,128]{2,1,0:T(8,128)S(1)}, f32[4,136,128]{2,1,0:T(8,128)S(1)}, u32[]{:S(2)}, u32[]{:S(2)}) collective-permute-start(f32[4,136,128]{2,1,0:T(8,128)S(1)} %pad_maximum_fusion.1), channel_id=1, source_target_pairs={{0,8},{8,0},{16,24},{24,16},{1,9},{9,1},{17,25},{25,17},{2,10},{10... | collective-permute-start | bytes 835592 | tf_op jit(solution)/shard_map/ppermute | solution.py:26

commit v3 on v2

--- a/solution.py
+++ b/solution.py
@@ -1,4 +1,5 @@
 import functools
+import math
 
 import jax
 import jax.numpy as jnp
@@ -14,6 +15,7 @@
 INNER_TILES = 4
 BORDER_TILES = 8
 SMALL_ROWS = 8
+STRIP_TILES = 4
 VMEM_BYTES = 24 * 1024 * 1024
 
 
@@ -26,31 +28,46 @@
     return lax.ppermute(value, axis, [(i, i ^ bit) for i in range(count)])
 
 
-def strip_kernel(tiles, strips, inner, wide):
-    count, side = tiles.shape[0], tiles.shape[1]
-    for index in range(count):
-        base = index * side * side
-        for row in range(side):
-            wide[base + row * side : base + (row + 1) * side, :] = tiles[index, row].astype(jnp.float32)
-        for target, first, last in ((strips, 0, side - 1), (inner, 1, side - 2)):
-            target[index, 0] = tiles[index, first]
-            target[index, 1] = tiles[index, last]
-            target[index, 2] = wide[pl.ds(base + first, side, stride=side), :].astype(jnp.bfloat16)
-            target[index, 3] = wide[pl.ds(base + last, side, stride=side), :].astype(jnp.bfloat16)
+def strip_kernel(tiles, strips, inner, csum):
+    slots, side, _, chans = tiles.shape
+    columns = (0, side - 1, 1, side - 2)
+    rows = (len(columns) + 1) * side
+    row = lax.broadcasted_iota(jnp.int32, (rows, side * side), 0)
+    pixel = lax.broadcasted_iota(jnp.int32, (rows, side * side), 1)
+    group = lax.div(row, side)
+    column = jnp.where(group == 0, columns[0], jnp.where(group == 1, columns[1], jnp.where(group == 2, columns[2], columns[3])))
+    picked = (pixel == (row - group * side) * side + column) | (group == len(columns))
+    select = jnp.where(picked, 1.0, 0.0).astype(jnp.bfloat16)
+
+    @pl.loop(0, slots // STRIP_TILES)
+    def _(step):
+        for part in range(STRIP_TILES):
+            slot = step * STRIP_TILES + part
+            tile = tiles[slot].reshape(side * side, chans)
+            found = jnp.dot(select, tile, preferred_element_type=jnp.float32)
+            lines = found[: len(columns) * side].astype(jnp.bfloat16)
+            strips[slot, 0] = tiles[slot, 0]
+            strips[slot, 1] = tiles[slot, side - 1]
+            strips[slot, 2] = lines[:side]
+            strips[slot, 3] = lines[side : 2 * side]
+            inner[slot, 0] = tiles[slot, 1]
+            inner[slot, 1] = tiles[slot, side - 2]
+            inner[slot, 2] = lines[2 * side : 3 * side]
+            inner[slot, 3] = lines[3 * side :]
+            csum[pl.ds(slot, 1), :] = found[len(columns) * side : len(columns) * side + 1]
 
 
 def border_strips(tiles):
     slots, side, _, chans = tiles.shape
-    step = 16
     shape = jax.ShapeDtypeStruct((slots, 4, side, chans), jnp.bfloat16)
-    spec = pl.BlockSpec((step, 4, side, chans), lambda i: (i, 0, 0, 0))
+    spec = pl.BlockSpec(memory_space=pltpu.VMEM)
     return pl.pallas_call(
         strip_kernel,
-        grid=(slots // step,),
-        in_specs=[pl.BlockSpec((step, side, side, chans), lambda i: (i, 0, 0, 0))],
-        out_specs=[spec, spec],
-        out_shape=[shape, shape],
-        scratch_shapes=[pltpu.VMEM((step * side * side, chans), jnp.float32)],
+        in_specs=[spec],
+        out_specs=[spec] * 3,
+        out_shape=[shape, shape, jax.ShapeDtypeStruct((slots, chans), jnp.float32)],
+        compiler_params=pltpu.CompilerParams(vmem_limit_bytes=VMEM_BYTES),
+        cost_estimate=pl.CostEstimate(flops=10**9, bytes_accessed=10**7, transcendentals=0),
     )(tiles)
 
 
@@ -69,7 +86,9 @@
     pixels = normed.shape[0] // tiles
     side = pixels // lines
     chans, hidden = w_in.shape
-    taps = [jnp.broadcast_to(kern[i : i + 1, :], (side, chans)) for i in range(9)]
+    gains_root = gains * math.sqrt(chans)
+    wide_taps = kern[...].astype(jnp.float32)
+    taps = [jnp.broadcast_to(wide_taps[i : i + 1, :], (side, chans)) for i in range(9)]
     place = lax.broadcasted_iota(jnp.int32, (side, hidden), 0)
     inside = jnp.where((place > 0) & (place < side - 1), 1.0, 0.0)
     for part in range(tiles):
@@ -80,19 +99,19 @@
                 term = pad[pl.ds(base + starts[line][tap], side), :] * taps[tap]
                 depth = term if depth is None else depth + term
             centered = depth - jnp.mean(depth, axis=1, keepdims=True)
-            inverse = lax.rsqrt(jnp.mean(centered * centered, axis=1, keepdims=True) + 1e-06)
+            inverse = lax.rsqrt(jnp.sum(centered * centered, axis=1, keepdims=True) + chans * 1e-06)
             units = centered * inverse
             at = part * pixels + line * side
             unit[at : at + side, :] = units
             invs[at : at + side, :] = jnp.broadcast_to(inverse, (side, chans))
-            normed[at : at + side, :] = (units * gains).astype(jnp.bfloat16)
+            normed[at : at + side, :] = (units * gains_root).astype(jnp.bfloat16)
     for part in range(tiles):
         slot = step * tiles + part
         rows = slice(part * pixels, (part + 1) * pixels)
         before = jnp.dot(normed[rows, :], w_in[...], preferred_element_type=jnp.float32)
         scaled = before * 0.7071067811865476
         twice = 1.0 + lax.erf(scaled)
-        bell = jnp.exp(-(scaled * scaled))
+        bell = jnp.exp2(scaled * scaled * -1.4426950408889634)
         act = spread(before * twice, lines)
         slope = spread(twice + (scaled * 1.1283791670955126) * bell, lines)
         factor = jnp.broadcast_to(ga[pl.ds(slot, 1), :], (side, hidden))
@@ -124,7 +143,7 @@
             grad_depth = invs[at : at + side, :] * (
                 grad_unit
                 - jnp.mean(grad_unit, axis=1, keepdims=True)
-                - units * jnp.mean(product * gains, axis=1, keepdims=True)
+                - units * jnp.sum(product * gains, axis=1, keepdims=True)
             )
             for tap in range(9):
                 tap_part[tap] = tap_part[tap] + grad_depth * pad[pl.ds(base + starts[line][tap], side), :]
@@ -143,15 +162,14 @@
     kern,
     gain,
     w_in,
-    w_in_t,
-    w_out_t,
+    w_out,
     asum,
-    csum,
     ge,
     ga,
     tap_sum,
     gain_sum,
     gi_sum,
+    w_in_t,
     pad,
     unit,
     invs,
@@ -163,7 +181,7 @@
     pixels = side * side
     cot_rows = cot_all.shape[0] // peers
     count, begin, me = meta[0], meta[1], meta[2]
-    for ref in (asum, csum, ge, tap_sum, gain_sum, gi_sum, pad):
+    for ref in (asum, ge, tap_sum, gain_sum, gi_sum, pad):
         ref[...] = jnp.zeros_like(ref)
 
     @pl.loop(0, count)
@@ -173,8 +191,13 @@
         row = block * cot_rows + lax.div(rank, peers)
         ge[pl.ds(slot, 1), :] = cot_all[pl.ds(row, 1), :] * (1.0 / pixels)
 
-    ga[...] = 0.5 * jnp.dot(
-        ge[...], w_out_t[...].astype(jnp.float32), precision=HIGHEST, preferred_element_type=jnp.float32
+    w_in_t[...] = w_in[...].astype(jnp.float32).T.astype(jnp.bfloat16)
+    ga[...] = 0.5 * lax.dot_general(
+        ge[...],
+        w_out[...].astype(jnp.float32),
+        (((1,), (1,)), ((), ())),
+        precision=HIGHEST,
+        preferred_element_type=jnp.float32,
     )
     starts = [
         [(y - 1 + a) * INNER_PITCH + FIRST - 1 + b for a in range(3) for b in range(3)] for y in range(1, side - 1)
@@ -185,12 +208,8 @@
         for part in range(INNER_TILES):
             slot = step * INNER_TILES + part
             base = part * (pad.shape[0] // INNER_TILES)
-            total = jnp.zeros((side, chans), jnp.float32)
             for y in range(side):
-                row = feats[slot, y].astype(jnp.float32)
-                pad[pl.ds(base + y * INNER_PITCH + FIRST, side), :] = row
-                total = total + row
-            csum[pl.ds(slot, 1), :] = jnp.sum(total, axis=0, keepdims=True)
+                pad[pl.ds(base + y * INNER_PITCH + FIRST, side), :] = feats[slot, y].astype(jnp.float32)
         run_lines(
             step,
             INNER_TILES,
@@ -211,8 +230,8 @@
     links,
     own,
     inner,
-    before_halo,
-    after_halo,
+    halo_pair,
+    halo_cross,
     kern,
     gain,
     w_in,
@@ -247,65 +266,54 @@
         target[...] = source[...]
     embed_out[...] = jnp.zeros_like(embed_out)
 
+    paired = lax.rem(me, 2) * -2 + 1
+
     def strip(column, which, slot):
         link = links[column, slot]
-        index = link - (me - 1) * slots
-        first = before_halo[jnp.clip(index, 0, slots - 1), which]
-        middle = own[jnp.clip(index - slots, 0, slots - 1), which]
-        last = after_halo[jnp.clip(index - 2 * slots, 0, slots - 1), which]
-        chosen = jnp.where(index < slots, first, jnp.where(index < 2 * slots, middle, last)).astype(jnp.float32)
+        index = lax.rem(jnp.maximum(link, 0), slots)
+        aside = lax.div(link, slots) - me
+        here, pair, cross = own[index, which], halo_pair[index, which], halo_cross[index, which]
+        chosen = jnp.where(aside == 0, here, jnp.where(aside == paired, pair, cross)).astype(jnp.float32)
         return jnp.where(link >= 0, chosen, 0.0)
 
+    lines = side + 2
+    plane = lines * LINE_PITCH
     across = [a * LINE_PITCH + FIRST - 1 + b for a in range(3) for b in range(3)]
-    along = [b * LINE_PITCH + FIRST - 1 + a for a in range(3) for b in range(3)]
+    along = [plane + b * LINE_PITCH + FIRST - 1 + a for a in range(3) for b in range(3)]
+    far = (side - 1) * LINE_PITCH
     starts = [
-        [panel * 3 * LINE_PITCH + start for start in (across if panel < 2 else along)] for panel in range(4)
+        across,
+        [start + far for start in across],
+        along,
+        [start + far for start in along],
     ]
 
     @pl.loop(0, lax.div(count + BORDER_TILES - 1, BORDER_TILES))
     def _(step):
         for part in range(BORDER_TILES):
             slot = step * BORDER_TILES + part
-            base = part * (pad.shape[0] // BORDER_TILES)
+            rows = part * (pad.shape[0] // BORDER_TILES) + FIRST
+            columns = rows + plane
             up, down, left, right = strip(0, 1, slot), strip(1, 0, slot), strip(2, 3, slot), strip(3, 2, slot)
-            upper_left, upper_right = strip(4, 1, slot)[side - 1 :], strip(5, 1, slot)[:1]
-            lower_left, lower_right = strip(6, 0, slot)[side - 1 :], strip(7, 0, slot)[:1]
-            rows = [own[slot, i].astype(jnp.float32) for i in range(4)]
+            edge = [own[slot, i].astype(jnp.float32) for i in range(4)]
             deep = [inner[slot, i].astype(jnp.float32) for i in range(4)]
-
-            def cut(line, at):
-                return line[at : at + 1]
-
-            end = side - 1
-            panels = (
-                (
-                    (upper_left, up, upper_right),
-                    (cut(left, 0), rows[0], cut(right, 0)),
-                    (cut(left, 1), deep[0], cut(right, 1)),
-                ),
-                (
-                    (cut(left, end - 1), deep[1], cut(right, end - 1)),
-                    (cut(left, end), rows[1], cut(right, end)),
-                    (lower_left, down, lower_right),
-                ),
-                (
-                    (upper_left, left, lower_left),
-                    (cut(up, 0), rows[2], cut(down, 0)),
-                    (cut(up, 1), deep[2], cut(down, 1)),
-                ),
-                (
-                    (cut(up, end - 1), deep[3], cut(down, end - 1)),
-                    (cut(up, end), rows[3], cut(down, end)),
-                    (upper_right, right, lower_right),
-                ),
-            )
-            for panel in range(4):
-                for line in range(3):
-                    at = base + (panel * 3 + line) * LINE_PITCH + FIRST
-                    head, body, tail = panels[panel][line]
-                    pad[pl.ds(at - 1, 1), :] = head
-                    pad[pl.ds(at, side), :] = body
-                    pad[pl.ds(at + side, 1), :] = tail
+            for at, bodies, head, tail in (
+                (rows, (up, edge[0], deep[0], deep[1], edge[1], down), left, right),
+                (columns, (left, edge[2], deep[2], deep[3], edge[3], right), up, down),
+            ):
+                for line, body in zip((0, 1, 2, side - 1, side, side + 1), bodies, strict=True):
+                    pad[pl.ds(at + line * LINE_PITCH, side), :] = body
+                pad[pl.ds(at + LINE_PITCH - 1, side, stride=LINE_PITCH), :] = head
+                pad[pl.ds(at + LINE_PITCH + side, side, stride=LINE_PITCH), :] = tail
+            last = (side + 1) * LINE_PITCH
+            for corner, in_rows, in_columns in (
+                (strip(4, 1, slot)[side - 1 :], -1, -1),
+                (strip(5, 1, slot)[:1], side, last - 1),
+                (strip(6, 0, slot)[side - 1 :], last - 1, side),
+                (strip(7, 0, slot)[:1], last + side, last + side),
+            ):
+                pad[pl.ds(rows + in_rows, 1), :] = corner
+                pad[pl.ds(columns + in_columns, 1), :] = corner
         run_lines(
             step,
             BORDER_TILES,
@@ -339,14 +347,18 @@
         grad_out[to, per : 2 * per, :] = go_sum[block * per : (block + 1) * per, :]
         grad_out[to, 2 * per :, :] = jnp.zeros((SMALL_ROWS, chans), jnp.float32)
     for i in range(9):
-        grad_out[(i // SMALL_ROWS) ^ mine, pl.ds(2 * per + i % SMALL_ROWS, 1), :] = jnp.sum(
+        grad_out[(i // SMALL_ROWS) ^ mine, pl.ds(2 * per + i % SMALL_ROWS, 1), :] = math.sqrt(chans) * jnp.sum(
             tap_sum[i * side : (i + 1) * side, :], axis=0, keepdims=True
         )
-    grad_out[1 ^ mine, pl.ds(2 * per + 1, 1), :] = jnp.sum(gain_sum[...], axis=0, keepdims=True)
-
-
-def unpack_kernel(parts, meta, packed, gk, gg, gi, go):
+    grad_out[1 ^ mine, pl.ds(2 * per + 1, 1), :] = math.sqrt(chans) * jnp.sum(
+        gain_sum[...], axis=0, keepdims=True
+    )
+
+
+def unpack_kernel(parts, meta, near, far, gk, gg, gi, go, packed):
     mine = meta[3]
+    packed[: parts // 2] = near[...]
+    packed[parts // 2 :] = far[...]
     hidden, chans = go.shape
     per = hidden // parts
     for block in range(parts):
@@ -375,15 +387,18 @@
     for place, (axis, bit) in enumerate(reversed(halving)):
         mine = mine + jnp.where((lax.axis_index(axis) & bit) > 0, 1 << place, 0)
 
-    strips, inner = border_strips(feats)
+    strips, inner, csum = border_strips(feats)
     gathered = jnp.concatenate(
         [cot_rows, jnp.broadcast_to(tissue_count.astype(jnp.float32), (8, chans))], axis=0
     )[None]
     for bit in tile_bits:
         gathered = jnp.concatenate([gathered, swap(gathered, "tile", bit)], axis=0)
+        if bit == 1:
+            gathered, strips = lax.optimization_barrier((gathered, strips))
+            halo_pair = swap(strips, "tile", 1)
     gathered, strips = lax.optimization_barrier((gathered, strips))
-    before_halo = lax.ppermute(strips, "tile", [(i, i + 1) for i in range(peers - 1)])
-    after_halo = lax.ppermute(strips, "tile", [(i + 1, i) for i in range(peers - 1)])
+    cross = [(i, i + 1) for i in range(1, peers - 1, 2)]
+    halo_cross = lax.ppermute(strips, "tile", cross + [(j, i) for i, j in cross])
 
     counts = gathered[:, work, 0].astype(jnp.int32)
     whose = jnp.arange(peers, dtype=jnp.int32) ^ me
@@ -395,7 +410,7 @@
     smem = pl.BlockSpec(memory_space=pltpu.SMEM)
     shape = jax.ShapeDtypeStruct
     params = pltpu.CompilerParams(vmem_limit_bytes=VMEM_BYTES)
-    taps, gains, w_in_t = kernel.astype(f32), gain[None], w_in.T
+    gains = gain[None]
     per = hidden // parts
     block_rows = 2 * per + SMALL_ROWS
 
@@ -408,39 +423,37 @@
             pltpu.VMEM((pixels, hidden), jnp.bfloat16),
         ]
 
-    asum, csum, ge, ga, tap_sum, gain_sum, gi_sum = pl.pallas_call(
+    asum, ge, ga, tap_sum, gain_sum, gi_sum, w_in_t = pl.pallas_call(
         functools.partial(inner_kernel, peers, work),
-        in_specs=[smem] * 2 + [vmem] * 7,
+        in_specs=[smem] * 2 + [vmem] * 6,
         out_specs=[vmem] * 7,
         out_shape=[
             shape((slots, hidden), f32),
-            shape((slots, chans), f32),
             shape((slots, chans), f32),
             shape((slots, hidden), f32),
             shape((9 * side, chans), f32),
             shape((side, chans), f32),
             shape((chans, hidden), f32),
+            shape((hidden, chans), jnp.bfloat16),
         ],
         scratch_shapes=line_scratch(INNER_TILES * (side + 1) * INNER_PITCH, INNER_TILES * side * (side - 2)),
         compiler_params=params,
-        cost_estimate=pl.CostEstimate(flops=30 * 10**9, bytes_accessed=10**7, transcendentals=10**7),
     )(
         meta,
         worker_perm[0],
         feats,
         gathered.reshape(peers * (work + 8), chans),
-        taps,
+        kernel,
         gains,
         w_in,
-        w_in_t,
-        w_out.T,
+        w_out,
     )
     embeds, packed = pl.pallas_call(
         functools.partial(border_kernel, peers, work, parts),
         in_specs=[smem] * 3 + [vmem] * 16,
         out_specs=[vmem] * 2,
         out_shape=[shape((peers * work, chans), f32), shape((parts, block_rows, chans), f32)],
-        scratch_shapes=line_scratch(BORDER_TILES * 12 * LINE_PITCH, BORDER_TILES * 4 * side)
+        scratch_shapes=line_scratch(BORDER_TILES * 2 * (side + 2) * LINE_PITCH, BORDER_TILES * 4 * side)
         + [
             pltpu.VMEM((slots, hidden), f32),
             pltpu.VMEM((9 * side, chans), f32),
@@ -456,9 +469,9 @@
         neighbors[0].T,
         strips,
         inner,
-        before_halo,
-        after_halo,
-        taps,
+        halo_pair,
+        halo_cross,
+        kernel,
         gains,
         w_in,
         w_in_t,
@@ -490,11 +503,12 @@
         embeds = keep + incoming[:rows].reshape(keep.shape)
         held = mine_part + incoming[rows:]
     held = held[None]
-    for axis, bit in reversed(halving):
+    for axis, bit in reversed(halving[1:]):
         held = jnp.concatenate([held, swap(held, axis, bit)], axis=0)
+    far = swap(held, *halving[0])
     gk, gg, gi, go = pl.pallas_call(
         functools.partial(unpack_kernel, parts),
-        in_specs=[smem, vmem],
+        in_specs=[smem, vmem, vmem],
         out_specs=[vmem] * 4,
         out_shape=[
             jax.ShapeDtypeStruct((9, chans), f32),
@@ -502,7 +516,9 @@
             jax.ShapeDtypeStruct((chans, hidden), f32),
             jax.ShapeDtypeStruct((hidden, chans), f32),
         ],
-    )(meta, held)
+        scratch_shapes=[pltpu.VMEM((parts, block_rows, chans), f32)],
+        compiler_params=params,
+    )(meta, held, far)
     return embeds, gk, gg[0], gi, go
 
 

time: 125 us -> 118 us (0.944)
  waiting for transfers between devices: 45.5 us -> 32.6 us
  Pallas kernels: 39.6 us -> 49.5 us
  starting transfers between devices: 27.5 us -> 24.5 us
  other arithmetic: 3.31 us -> 1.76 us
    ppermute x2 -> x1, waiting for transfers between devices: 15.3 us -> 0.01 us  [local(): lax.ppermute(strips, 'tile', cross + [(j, i) for i, j in cross])]
    pallas_call x1, Pallas kernels: 21.8 us -> 30.3 us  [local(): pl.pallas_call(functools.partial(inner_kernel, peers, work), in_specs=[sm...]
    ppermute x2 -> x1, starting transfers between devices: 5.9 us -> 1.66 us  [local(): lax.ppermute(strips, 'tile', cross + [(j, i) for i, j in cross])]
    pallas_call x1, Pallas kernels: 11.2 us -> 14.6 us  [local(): pl.pallas_call(functools.partial(border_kernel, peers, work, parts), in_s...]
    ppermute x11 -> x12, waiting for transfers between devices: 30.2 us -> 32.6 us  [swap(): return lax.ppermute(value, axis, [(i, i ^ bit) for i in range(count)])]
    pallas_call x1, Pallas kernels: 4.64 us -> 3.08 us  [border_strips(): pl.pallas_call(strip_kernel, in_specs=[spec], out_specs=[spec] * 3, out_s...]
    ppermute x11 -> x12, starting transfers between devices: 21.6 us -> 22.9 us  [swap(): return lax.ppermute(value, axis, [(i, i ^ bit) for i in range(count)])]
    unnamed x20 -> x18, local copies, waits for them, and re-layouts: 4.24 us -> 5.3 us
  transfers between devices with their start and end apart: 13 -> 13, of which waited for: 11 -> 11; matrix products, arithmetic and copies ran while one was open for 3% -> 1% of each run, Pallas kernels for 21% -> 28%
where the time goes in v3:
time: 118 us; the launch traced here: 117 us
  Pallas kernels  49.5 us (42%)
  waiting for transfers between devices  32.6 us (28%)
  starting transfers between devices  24.5 us (21%)
  local copies, waits for them, and re-layouts  6.09 us (5%)
  between operations  2.84 us (2%)
  other arithmetic  1.76 us (1%)
    ppermute x12, waiting for transfers between devices, swap(): return lax.ppermute(value, axis, [(i, i ^ bit) for i in range(count)])  32.6 us
    pallas_call x1, Pallas kernels, local(): pl.pallas_call(functools.partial(inner_kernel, peers, work), in_specs=[sm...  30.3 us
    ppermute x12, starting transfers between devices, swap(): return lax.ppermute(value, axis, [(i, i ^ bit) for i in range(count)])  22.9 us
    pallas_call x1, Pallas kernels, local(): pl.pallas_call(functools.partial(border_kernel, peers, work, parts), in_s...  14.6 us
    unnamed x18, local copies, waits for them, and re-layouts  5.3 us
    pallas_call x1, Pallas kernels, border_strips(): pl.pallas_call(strip_kernel, in_specs=[spec], out_specs=[spec] * 3, out_s...  3.08 us
  transfers between devices with their start and end apart: 13, of which 11 were waited for; matrix products, arithmetic and copies ran while one was open for 1% of the time, Pallas kernels for 28%

profile of v3, /device:TPU:0, one launch (start us, length us, event | category | flops | bytes accessed | tf_op | source)
XLA Modules:
  0.0 117.3 jit_solution(6789544959020381988)
XLA Ops:
  0.6 0.0 copy-start.5
  0.6 0.0 copy-start.8
  0.7 0.0 copy-start.7
  1.3 0.7 pad_bitcast_fusion
  2.1 3.0 %collective-permute-start = (f32[1,40,128]{2,1,0:T(8,128)S(1)}, f32[1,40,128]{2,1,0:T(8,128)S(1)}, u32[]{:S(2)}, u32[]{:S(2)}) collective-permute-start(f32[1,40,128]{2,1,0:T(8,128)S(1)} %pad_bitcast_fusion), channel_id=1, source_target_pairs={{0,1},{1,0},{2,3},{3,2},{4,5},{5,4},{6,7},{7,6},{8,9},{9,8},{10,11... | collective-permute-start | bytes 61448 | tf_op jit(solution)/shard_map/ppermute | solution.py:28
  5.0 2.2 %copy-done = bf16[1,64,16,16,128]{4,3,2,1,0:T(8,128)(2,1)S(1)} copy-done((bf16[1,64,16,16,128]{4,3,2,1,0:T(8,128)(2,1)S(1)}, bf16[1,64,16,16,128]{4,3,2,1,0:T(8,128)(2,1)}, u32[]{:S(2)}) %copy-start) | copy-done | bytes 4194328
  7.2 3.1 %shard_map.137 = (bf16[64,4,16,128]{3,2,1,0:T(8,128)(2,1)S(1)}, bf16[64,4,16,128]{3,2,1,0:T(8,128)(2,1)S(1)}, f32[64,128]{1,0:T(8,128)S(1)}) custom-call(bf16[64,16,16,128]{3,2,1,0:T(8,128)(2,1)S(1)} %bitcast.53), custom_call_target="tpu_custom_call" | custom-call | flops 1000000000 | bytes 10000000 | tf_op jit(solution)/shard_map/pallas_call | solution.py:64
  10.3 0.0 collective-permute-done
  10.3 1.6 %collective-permute-start.1 = (f32[2,40,128]{2,1,0:T(8,128)S(1)}, f32[2,40,128]{2,1,0:T(8,128)S(1)}, u32[]{:S(2)}, u32[]{:S(2)}) collective-permute-start(f32[2,40,128]{2,1,0:T(8,128)S(1)} %pad_maximum_fusion.7), channel_id=1, source_target_pairs={{0,2},{1,3},{2,0},{3,1},{4,6},{5,7},{6,4},{7,5},{8,10},{9,11},{10,... | collective-permute-start | bytes 122888 | tf_op jit(solution)/shard_map/ppermute | solution.py:28
  12.0 2.4 %collective-permute-done.1 = f32[2,40,128]{2,1,0:T(8,128)S(1)} collective-permute-done((f32[2,40,128]{2,1,0:T(8,128)S(1)}, f32[2,40,128]{2,1,0:T(8,128)S(1)}, u32[]{:S(2)}, u32[]{:S(2)}) %collective-permute-start.1) | collective-permute-done | bytes 40992 | tf_op jit(solution)/shard_map/ppermute | solution.py:28
  14.4 2.6 %collective-permute-start.2 = (f32[4,40,128]{2,1,0:T(8,128)S(1)}, f32[4,40,128]{2,1,0:T(8,128)S(1)}, u32[]{:S(2)}, u32[]{:S(2)}) collective-permute-start(f32[4,40,128]{2,1,0:T(8,128)S(1)} %pad_maximum_fusion.6), channel_id=1, source_target_pairs={{0,4},{1,5},{2,6},{3,7},{4,0},{5,1},{6,2},{7,3},{8,12},{9,13},{10,... | collective-permute-start | bytes 245768 | tf_op jit(solution)/shard_map/ppermute | solution.py:28
  17.0 0.5 collective-permute-start.3
  17.5 2.2 %collective-permute-done.2 = f32[4,40,128]{2,1,0:T(8,128)S(1)} collective-permute-done((f32[4,40,128]{2,1,0:T(8,128)S(1)}, f32[4,40,128]{2,1,0:T(8,128)S(1)}, u32[]{:S(2)}, u32[]{:S(2)}) %collective-permute-start.2) | collective-permute-done | bytes 81952 | tf_op jit(solution)/shard_map/ppermute | solution.py:28
  19.8 1.7 %collective-permute-start.4 = (bf16[64,4,16,128]{3,2,1,0:T(8,128)(2,1)S(1)}, bf16[64,4,16,128]{3,2,1,0:T(8,128)(2,1)}, u32[]{:S(2)}, u32[]{:S(2)}) collective-permute-start(bf16[64,4,16,128]{3,2,1,0:T(8,128)(2,1)S(1)} %get-tuple-element.29.own), channel_id=1, source_target_pairs={{1,2},{3,4},{5,6},{2,1},{4,3},{6,5},{9,10},{11,12},{13,14},{10,9},... | collective-permute-start | bytes 3145736 | tf_op jit(solution)/shard_map/ppermute | solution.py:401
  22.1 0.2 convert_reduce_fusion
  22.3 0.6 fusion.3
  23.6 0.1 pad_add_fusion.meta
  23.7 0.0 copy-done.5
  23.7 0.0 copy-done.8
  23.7 0.0 copy-done.7
  23.7 0.0 copy-done.2
  23.7 0.0 copy-start.1
  23.7 2.2 %copy-done.1 = bf16[1,64,16,16,128]{4,3,2,1,0:T(8,128)(2,1)S(1)} copy-done((bf16[1,64,16,16,128]{4,3,2,1,0:T(8,128)(2,1)S(1)}, bf16[1,64,16,16,128]{4,3,2,1,0:T(8,128)(2,1)}, u32[]{:S(2)}) %copy-start.1) | copy-done | bytes 4194328
  25.9 0.9 copy-done.3
  26.8 30.3 %shard_map.138 = (f32[64,512]{1,0:T(8,128)S(1)}, f32[64,128]{1,0:T(8,128)S(1)}, f32[64,512]{1,0:T(8,128)S(1)}, f32[144,128]{1,0:T(8,128)S(1)}, f32[16,128]{1,0:T...) custom-call(s32[4]{0:T(128)S(1)} %pad_add_fusion.meta, s32[8]{0:T(128)S(1)} %bitcast.58, ...), custom_call_target="tpu_custom_call" | custom-call | tf_op jit(solution)/shard_map/pallas_call | solution.py:426
  57.1 3.5 %collective-permute-done.3.halo_pair = bf16[64,4,16,128]{3,2,1,0:T(8,128)(2,1)S(1)} collective-permute-done((bf16[64,4,16,128]{3,2,1,0:T(8,128)(2,1)S(1)}, bf16[64,4,16,128]{3,2,1,0:T(8,128)(2,1)S(1)}, u32[]{:S(2)}, u32[]{:S(2)}) %collective-permute-start.3) | collective-permute-done | bytes 1048608 | tf_op jit(solution)/shard_map/ppermute | solution.py:28
  60.7 0.0 collective-permute-done.4.halo_cross
  60.7 0.0 copy-done.6
  60.7 0.0 copy-done.4
  60.7 14.6 %shard_map.139 = (f32[256,128]{1,0:T(8,128)S(1)}, f32[8,136,128]{2,1,0:T(8,128)S(1)}) custom-call(s32[4]{0:T(128)S(1)} %pad_add_fusion.meta, s32[8]{0:T(128)S(1)} %bitcast.59, s32[8,64]{1,0:T(8,128)S(1)} %bitcast.57, bf16[64,4,16,128]{3,2,1,0:T(8,128)(2,1)S(1)} %get-tuple-element.29.own, bf16[64,4,16,128]{3,2,1,0:T(8,128)(2,1)S(1)} %get-tuple-element.30.inner, ...), custom_call_target="tpu_custom_call" | custom-call | tf_op jit(solution)/shard_map/pallas_call | solution.py:451
  75.4 0.1 collective-permute-start.5
  75.4 1.5 %collective-permute-done.5 = f32[4,136,128]{2,1,0:T(8,128)S(1)} collective-permute-done((f32[4,136,128]{2,1,0:T(8,128)S(1)}, f32[4,136,128]{2,1,0:T(8,128)S(1)}, u32[]{:S(2)}, u32[]{:S(2)}) %collective-permute-start.5) | collective-permute-done | bytes 278560 | tf_op jit(solution)/shard_map/ppermute | solution.py:28
  77.0 0.1 collective-permute-start.6
  77.1 5.7 %collective-permute-done.6 = f32[2,136,128]{2,1,0:T(8,128)S(1)} collective-permute-done((f32[2,136,128]{2,1,0:T(8,128)S(1)}, f32[2,136,128]{2,1,0:T(8,128)S(1)}, u32[]{:S(2)}, u32[]{:S(2)}) %collective-permute-start.6) | collective-permute-done | bytes 139296 | tf_op jit(solution)/shard_map/ppermute | solution.py:28
  82.9 2.3 %collective-permute-start.7 = (f32[264,128]{1,0:T(8,128)S(1)}, f32[264,128]{1,0:T(8,128)S(1)}, u32[]{:S(2)}, u32[]{:S(2)}) collective-permute-start(f32[264,128]{1,0:T(8,128)S(1)} %pad_maximum_fusion.3), channel_id=1, source_target_pairs={{0,1},{1,0},{2,3},{3,2},{4,5},{5,4},{6,7},{7,6},{8,9},{9,8},{10,11... | collective-permute-start | bytes 405512 | tf_op jit(solution)/shard_map/ppermute | solution.py:28
  85.2 3.4 %collective-permute-done.7 = f32[264,128]{1,0:T(8,128)S(1)} collective-permute-done((f32[264,128]{1,0:T(8,128)S(1)}, f32[264,128]{1,0:T(8,128)S(1)}, u32[]{:S(2)}, u32[]{:S(2)}) %collective-permute-start.7) | collective-permute-done | bytes 135200 | tf_op jit(solution)/shard_map/ppermute | solution.py:28
  88.6 7.7 %collective-permute-start.8 = (f32[200,128]{1,0:T(8,128)S(1)}, f32[200,128]{1,0:T(8,128)S(1)}, u32[]{:S(2)}, u32[]{:S(2)}) collective-permute-start(f32[200,128]{1,0:T(8,128)S(1)} %pad_maximum_fusion.4), channel_id=1, source_target_pairs={{0,2},{1,3},{2,0},{3,1},{4,6},{5,7},{6,4},{7,5},{8,10},{9,11},{10,... | collective-permute-start | bytes 307208 | tf_op jit(solution)/shard_map/ppermute | solution.py:28
  96.3 2.6 %collective-permute-done.8 = f32[200,128]{1,0:T(8,128)S(1)} collective-permute-done((f32[200,128]{1,0:T(8,128)S(1)}, f32[200,128]{1,0:T(8,128)S(1)}, u32[]{:S(2)}, u32[]{:S(2)}) %collective-permute-start.8) | collective-permute-done | bytes 102432 | tf_op jit(solution)/shard_map/ppermute | solution.py:28
  99.0 2.1 %collective-permute-start.9 = (f32[168,128]{1,0:T(8,128)S(1)}, f32[168,128]{1,0:T(8,128)S(1)}, u32[]{:S(2)}, u32[]{:S(2)}) collective-permute-start(f32[168,128]{1,0:T(8,128)S(1)} %pad_maximum_fusion.5), channel_id=1, source_target_pairs={{0,4},{1,5},{2,6},{3,7},{4,0},{5,1},{6,2},{7,3},{8,12},{9,13},{10,... | collective-permute-start | bytes 258056 | tf_op jit(solution)/shard_map/ppermute | solution.py:28
  101.1 3.4 %collective-permute-done.9 = f32[168,128]{1,0:T(8,128)S(1)} collective-permute-done((f32[168,128]{1,0:T(8,128)S(1)}, f32[168,128]{1,0:T(8,128)S(1)}, u32[]{:S(2)}, u32[]{:S(2)}) %collective-permute-start.9) | collective-permute-done | bytes 86048 | tf_op jit(solution)/shard_map/ppermute | solution.py:28
  104.5 2.3 %collective-permute-start.10 = (f32[1,136,128]{2,1,0:T(8,128)S(1)}, f32[1,136,128]{2,1,0:T(8,128)S(1)}, u32[]{:S(2)}, u32[]{:S(2)}) collective-permute-start(f32[1,136,128]{2,1,0:T(8,128)S(1)} %fusion), channel_id=1, source_target_pairs={{0,1},{1,0},{2,3},{3,2},{4,5},{5,4},{6,7},{7,6},{8,9},{9,8},{10,11... | collective-permute-start | bytes 208904 | tf_op jit(solution)/shard_map/ppermute | solution.py:28
  106.8 2.3 %collective-permute-done.10 = f32[1,136,128]{2,1,0:T(8,128)S(1)} collective-permute-done((f32[1,136,128]{2,1,0:T(8,128)S(1)}, f32[1,136,128]{2,1,0:T(8,128)S(1)}, u32[]{:S(2)}, u32[]{:S(2)}) %collective-permute-start.10) | collective-permute-done | bytes 69664 | tf_op jit(solution)/shard_map/ppermute | solution.py:28
  109.1 0.6 collective-permute-start.11
  109.7 4.6 %collective-permute-done.11 = f32[2,136,128]{2,1,0:T(8,128)S(1)} collective-permute-done((f32[2,136,128]{2,1,0:T(8,128)S(1)}, f32[2,136,128]{2,1,0:T(8,128)S(1)}, u32[]{:S(2)}, u32[]{:S(2)}) %collective-permute-start.11) | collective-permute-done | bytes 139296 | tf_op jit(solution)/shard_map/ppermute | solution.py:28
  114.2 0.1 collective-permute-start.12
  114.3 0.6 fusion.2
  114.9 0.9 collective-permute-done.12.far
  115.9 1.4 %shard_map.140 = (f32[9,128]{1,0:T(8,128)}, f32[1,128]{1,0:T(1,128)}, f32[128,512]{1,0:T(8,128)}, f32[512,128]{1,0:T(8,128)}) custom-call(s32[4]{0:T(128)S(1)} %pad_add_fusion.meta, f32[4,136,128]{2,1,0:T(8,128)S(1)} %pad_maximum_fusion.near, f32[4,136,128]{2,1,0:T(8,128)S(1)} %collective-permute-done.12.far), custom_call_target="tpu_custom_call" | custom-call | tf_op jit(solution)/shard_map/pallas_call | solution.py:509
  (28 shorter events, 0.3 us)
Async XLA Ops:
  0.6 23.1 %copy-start.5 = (bf16[9,128]{1,0:T(8,128)(2,1)S(1)}, bf16[9,128]{1,0:T(8,128)(2,1)}, u32[]{:S(2)}) copy-start(bf16[9,128]{1,0:T(8,128)(2,1)} %kern.3) | copy-start | bytes 6916
  0.6 23.0 %copy-start.8 = (f32[128]{0:T(128)S(1)}, f32[128]{0:T(128)}, u32[]{:S(2)}) copy-start(f32[128]{0:T(128)} %param.16) | copy-start | bytes 1540
  0.7 23.0 %copy-start.7 = (s32[1,8]{1,0:T(1,128)S(1)}, s32[1,8]{1,0:T(1,128)}, u32[]{:S(2)}) copy-start(s32[1,8]{1,0:T(1,128)} %param.13) | copy-start | bytes 100
  2.1 8.3 %collective-permute-start = (f32[1,40,128]{2,1,0:T(8,128)S(1)}, f32[1,40,128]{2,1,0:T(8,128)S(1)}, u32[]{:S(2)}, u32[]{:S(2)}) collective-permute-start(f32[1,40,128]{2,1,0:T(8,128)S(1)} %pad_bitcast_fusion), channel_id=1, source_target_pairs={{0,1},{1,0},{2,3},{3,2},{4,5},{5,4},{6,7},{7,6},{8,9},{9,8},{10,11... | collective-permute-start | bytes 61448 | tf_op jit(solution)/shard_map/ppermute | solution.py:28
  5.0 2.2 %copy-start = (bf16[1,64,16,16,128]{4,3,2,1,0:T(8,128)(2,1)S(1)}, bf16[1,64,16,16,128]{4,3,2,1,0:T(8,128)(2,1)}, u32[]{:S(2)}) copy-start(bf16[1,64,16,16,128]{4,3,2,1,0:T(8,128)(2,1)} %param.10) | copy-start | bytes 12582916
  7.2 16.5 %copy-start.2 = (bf16[128,512]{1,0:T(8,128)(2,1)S(1)}, bf16[128,512]{1,0:T(8,128)(2,1)}, u32[]{:S(2)}) copy-start(bf16[128,512]{1,0:T(8,128)(2,1)} %w_in.3) | copy-start | bytes 393220
  7.2 53.5 %copy-start.6 = (s32[1,64,8]{1,2,0:T(8,128)S(1)}, s32[1,64,8]{1,2,0:T(8,128)}, u32[]{:S(2)}) copy-start(s32[1,64,8]{1,2,0:T(8,128)} %param.12) | copy-start | bytes 6148
  10.3 4.1 %collective-permute-start.1 = (f32[2,40,128]{2,1,0:T(8,128)S(1)}, f32[2,40,128]{2,1,0:T(8,128)S(1)}, u32[]{:S(2)}, u32[]{:S(2)}) collective-permute-start(f32[2,40,128]{2,1,0:T(8,128)S(1)} %pad_maximum_fusion.7), channel_id=1, source_target_pairs={{0,2},{1,3},{2,0},{3,1},{4,6},{5,7},{6,4},{7,5},{8,10},{9,11},{10,... | collective-permute-start | bytes 122888 | tf_op jit(solution)/shard_map/ppermute | solution.py:28
  14.4 5.3 %collective-permute-start.2 = (f32[4,40,128]{2,1,0:T(8,128)S(1)}, f32[4,40,128]{2,1,0:T(8,128)S(1)}, u32[]{:S(2)}, u32[]{:S(2)}) collective-permute-start(f32[4,40,128]{2,1,0:T(8,128)S(1)} %pad_maximum_fusion.6), channel_id=1, source_target_pairs={{0,4},{1,5},{2,6},{3,7},{4,0},{5,1},{6,2},{7,3},{8,12},{9,13},{10,... | collective-permute-start | bytes 245768 | tf_op jit(solution)/shard_map/ppermute | solution.py:28
  17.0 43.7 %collective-permute-start.3 = (bf16[64,4,16,128]{3,2,1,0:T(8,128)(2,1)S(1)}, bf16[64,4,16,128]{3,2,1,0:T(8,128)(2,1)S(1)}, u32[]{:S(2)}, u32[]{:S(2)}) collective-permute-start(bf16[64,4,16,128]{3,2,1,0:T(8,128)(2,1)S(1)} %get-tuple-element.29.own), channel_id=1, source_target_pairs={{0,1},{1,0},{2,3},{3,2},{4,5},{5,4},{6,7},{7,6},{8,9},{9,8},{10,11... | collective-permute-start | bytes 3145736 | tf_op jit(solution)/shard_map/ppermute | solution.py:28
  19.8 40.9 %collective-permute-start.4 = (bf16[64,4,16,128]{3,2,1,0:T(8,128)(2,1)S(1)}, bf16[64,4,16,128]{3,2,1,0:T(8,128)(2,1)}, u32[]{:S(2)}, u32[]{:S(2)}) collective-permute-start(bf16[64,4,16,128]{3,2,1,0:T(8,128)(2,1)S(1)} %get-tuple-element.29.own), channel_id=1, source_target_pairs={{1,2},{3,4},{5,6},{2,1},{4,3},{6,5},{9,10},{11,12},{13,14},{10,9},... | collective-permute-start | bytes 3145736 | tf_op jit(solution)/shard_map/ppermute | solution.py:401
  23.7 2.2 %copy-start.1 = (bf16[1,64,16,16,128]{4,3,2,1,0:T(8,128)(2,1)S(1)}, bf16[1,64,16,16,128]{4,3,2,1,0:T(8,128)(2,1)}, u32[]{:S(2)}) copy-start(bf16[1,64,16,16,128]{4,3,2,1,0:T(8,128)(2,1)} %param.10) | copy-start | bytes 12582916
  25.9 0.9 copy-start.3
  26.8 33.9 %copy-start.4 = (bf16[512,128]{1,0:T(8,128)(2,1)S(1)}, bf16[512,128]{1,0:T(8,128)(2,1)}, u32[]{:S(2)}) copy-start(bf16[512,128]{1,0:T(8,128)(2,1)} %w_out.3) | copy-start | bytes 393220
  75.4 1.6 %collective-permute-start.5 = (f32[4,136,128]{2,1,0:T(8,128)S(1)}, f32[4,136,128]{2,1,0:T(8,128)S(1)}, u32[]{:S(2)}, u32[]{:S(2)}) collective-permute-start(f32[4,136,128]{2,1,0:T(8,128)S(1)} %slice.61), channel_id=1, source_target_pairs={{0,8},{8,0},{16,24},{24,16},{1,9},{9,1},{17,25},{25,17},{2,10},{10... | collective-permute-start | bytes 835592 | tf_op jit(solution)/shard_map/ppermute | solution.py:28
  77.0 5.8 %collective-permute-start.6 = (f32[2,136,128]{2,1,0:T(8,128)S(1)}, f32[2,136,128]{2,1,0:T(8,128)S(1)}, u32[]{:S(2)}, u32[]{:S(2)}) collective-permute-start(f32[2,136,128]{2,1,0:T(8,128)S(1)} %slice.79), channel_id=1, source_target_pairs={{0,16},{8,24},{16,0},{24,8},{1,17},{9,25},{17,1},{25,9},{2,18},{10... | collective-permute-start | bytes 417800 | tf_op jit(solution)/shard_map/ppermute | solution.py:28
  82.9 5.7 %collective-permute-start.7 = (f32[264,128]{1,0:T(8,128)S(1)}, f32[264,128]{1,0:T(8,128)S(1)}, u32[]{:S(2)}, u32[]{:S(2)}) collective-permute-start(f32[264,128]{1,0:T(8,128)S(1)} %pad_maximum_fusion.3), channel_id=1, source_target_pairs={{0,1},{1,0},{2,3},{3,2},{4,5},{5,4},{6,7},{7,6},{8,9},{9,8},{10,11... | collective-permute-start | bytes 405512 | tf_op jit(solution)/shard_map/ppermute | solution.py:28
  88.6 10.3 %collective-permute-start.8 = (f32[200,128]{1,0:T(8,128)S(1)}, f32[200,128]{1,0:T(8,128)S(1)}, u32[]{:S(2)}, u32[]{:S(2)}) collective-permute-start(f32[200,128]{1,0:T(8,128)S(1)} %pad_maximum_fusion.4), channel_id=1, source_target_pairs={{0,2},{1,3},{2,0},{3,1},{4,6},{5,7},{6,4},{7,5},{8,10},{9,11},{10,... | collective-permute-start | bytes 307208 | tf_op jit(solution)/shard_map/ppermute | solution.py:28
  99.0 5.4 %collective-permute-start.9 = (f32[168,128]{1,0:T(8,128)S(1)}, f32[168,128]{1,0:T(8,128)S(1)}, u32[]{:S(2)}, u32[]{:S(2)}) collective-permute-start(f32[168,128]{1,0:T(8,128)S(1)} %pad_maximum_fusion.5), channel_id=1, source_target_pairs={{0,4},{1,5},{2,6},{3,7},{4,0},{5,1},{6,2},{7,3},{8,12},{9,13},{10,... | collective-permute-start | bytes 258056 | tf_op jit(solution)/shard_map/ppermute | solution.py:28
  104.5 4.6 %collective-permute-start.10 = (f32[1,136,128]{2,1,0:T(8,128)S(1)}, f32[1,136,128]{2,1,0:T(8,128)S(1)}, u32[]{:S(2)}, u32[]{:S(2)}) collective-permute-start(f32[1,136,128]{2,1,0:T(8,128)S(1)} %fusion), channel_id=1, source_target_pairs={{0,1},{1,0},{2,3},{3,2},{4,5},{5,4},{6,7},{7,6},{8,9},{9,8},{10,11... | collective-permute-start | bytes 208904 | tf_op jit(solution)/shard_map/ppermute | solution.py:28
  109.1 5.1 %collective-permute-start.11 = (f32[2,136,128]{2,1,0:T(8,128)S(1)}, f32[2,136,128]{2,1,0:T(8,128)S(1)}, u32[]{:S(2)}, u32[]{:S(2)}) collective-permute-start(f32[2,136,128]{2,1,0:T(8,128)S(1)} %pad_maximum_fusion.2), channel_id=1, source_target_pairs={{0,16},{8,24},{16,0},{24,8},{1,17},{9,25},{17,1},{25,9},{2,18},{10... | collective-permute-start | bytes 417800 | tf_op jit(solution)/shard_map/ppermute | solution.py:28
  114.2 1.6 %collective-permute-start.12 = (f32[4,136,128]{2,1,0:T(8,128)S(1)}, f32[4,136,128]{2,1,0:T(8,128)S(1)}, u32[]{:S(2)}, u32[]{:S(2)}) collective-permute-start(f32[4,136,128]{2,1,0:T(8,128)S(1)} %pad_maximum_fusion.near), channel_id=1, source_target_pairs={{0,8},{8,0},{16,24},{24,16},{1,9},{9,1},{17,25},{25,17},{2,10},{10... | collective-permute-start | bytes 835592 | tf_op jit(solution)/shard_map/ppermute | solution.py:28

commit v4 on v3

--- a/solution.py
+++ b/solution.py
@@ -13,10 +13,10 @@
 INNER_PITCH = 24
 LINE_PITCH = 32
 INNER_TILES = 4
-BORDER_TILES = 8
+BORDER_TILES = 16
 SMALL_ROWS = 8
 STRIP_TILES = 4
-VMEM_BYTES = 24 * 1024 * 1024
+VMEM_BYTES = 32 * 1024 * 1024
 
 
 def bits_of(count):
@@ -28,7 +28,7 @@
     return lax.ppermute(value, axis, [(i, i ^ bit) for i in range(count)])
 
 
-def strip_kernel(tiles, strips, inner, csum):
+def strip_kernel(tiles, held, strips, inner, csum):
     slots, side, _, chans = tiles.shape
     columns = (0, side - 1, 1, side - 2)
     rows = (len(columns) + 1) * side
@@ -64,8 +64,14 @@
     return pl.pallas_call(
         strip_kernel,
         in_specs=[spec],
-        out_specs=[spec] * 3,
-        out_shape=[shape, shape, jax.ShapeDtypeStruct((slots, chans), jnp.float32)],
+        out_specs=[spec] * 4,
+        out_shape=[
+            jax.ShapeDtypeStruct(tiles.shape, tiles.dtype),
+            shape,
+            shape,
+            jax.ShapeDtypeStruct((slots, chans), jnp.float32),
+        ],
+        input_output_aliases={0: 0},
         compiler_params=pltpu.CompilerParams(vmem_limit_bytes=VMEM_BYTES),
         cost_estimate=pl.CostEstimate(flops=10**9, bytes_accessed=10**7, transcendentals=0),
     )(tiles)
@@ -78,14 +84,15 @@
 def run_lines(
     step, tiles, starts, masked, weights, state, sums
 ):
-    kern, gains, w_in, w_in_t = weights
-    pad, unit, invs, normed, gb = state
+    kern, gains, w_gelu, w_in_t = weights
+    pad, unit, invs, normed, gb, back = state
     asum, ga, tap_sum, gain_sum, gi_sum = sums
     lines = len(starts)
     pad_rows = pad.shape[0] // tiles
     pixels = normed.shape[0] // tiles
     side = pixels // lines
-    chans, hidden = w_in.shape
+    hidden, chans = w_in_t.shape
+    half = side // 2
     gains_root = gains * math.sqrt(chans)
     wide_taps = kern[...].astype(jnp.float32)
     taps = [jnp.broadcast_to(wide_taps[i : i + 1, :], (side, chans)) for i in range(9)]
@@ -108,11 +115,11 @@
     for part in range(tiles):
         slot = step * tiles + part
         rows = slice(part * pixels, (part + 1) * pixels)
-        before = jnp.dot(normed[rows, :], w_in[...], preferred_element_type=jnp.float32)
-        scaled = before * 0.7071067811865476
+        doubled = jnp.concatenate([normed[rows, :]] * 2, axis=1)
+        scaled = jnp.dot(doubled, w_gelu[...], preferred_element_type=jnp.float32)
         twice = 1.0 + lax.erf(scaled)
         bell = jnp.exp2(scaled * scaled * -1.4426950408889634)
-        act = spread(before * twice, lines)
+        act = spread(scaled * twice, lines)
         slope = spread(twice + (scaled * 1.1283791670955126) * bell, lines)
         factor = jnp.broadcast_to(ga[pl.ds(slot, 1), :], (side, hidden))
         factor_inside = factor * inside
@@ -125,31 +132,51 @@
         for line in range(lines):
             at = part * pixels + line * side
             gb[at : at + side, :] = (slope[line] * (factor_inside if masked[line] else factor)).astype(jnp.bfloat16)
+    back[...] = jnp.dot(gb[...], w_in_t[...], preferred_element_type=jnp.float32)
     gi_sum[...] += lax.dot_general(normed[...], gb[...], (((0,), (0,)), ((), ())), preferred_element_type=jnp.float32)
-    gain_part = jnp.zeros((side, chans), jnp.float32)
-    tap_part = [jnp.zeros((side, chans), jnp.float32) for _ in range(9)]
+    gain_part = jnp.zeros((half, chans), jnp.float32)
+    tap_part = [jnp.zeros((half, chans), jnp.float32) for _ in range(9)]
     for part in range(tiles):
         base = part * pad_rows
-        grad_normed = jnp.dot(
-            gb[part * pixels : (part + 1) * pixels, :], w_in_t[...], preferred_element_type=jnp.float32
-        )
         for line in range(lines):
             at = part * pixels + line * side
-            rows = grad_normed[line * side : (line + 1) * side]
             units = unit[at : at + side, :]
-            product = rows * units
-            gain_part = gain_part + product
-            grad_unit = rows * gains
+            grad_unit = back[at : at + side, :] * gains
+            product = grad_unit * units
+            gain_part = gain_part + (product[:half] + product[half:])
             grad_depth = invs[at : at + side, :] * (
                 grad_unit
                 - jnp.mean(grad_unit, axis=1, keepdims=True)
-                - units * jnp.sum(product * gains, axis=1, keepdims=True)
+                - units * jnp.sum(product, axis=1, keepdims=True)
             )
             for tap in range(9):
-                tap_part[tap] = tap_part[tap] + grad_depth * pad[pl.ds(base + starts[line][tap], side), :]
+                term = grad_depth * pad[pl.ds(base + starts[line][tap], side), :]
+                tap_part[tap] = tap_part[tap] + (term[:half] + term[half:])
     gain_sum[...] += gain_part
     for tap in range(9):
-        tap_sum[tap * side : (tap + 1) * side, :] += tap_part[tap]
+        tap_sum[tap * half : (tap + 1) * half, :] += tap_part[tap]
+
+
+def line_scratch(tiles, pad_rows, lines, side, chans, hidden):
+    f32, bf16 = jnp.float32, jnp.bfloat16
+    pixels = tiles * lines * side
+    return [
+        pltpu.VMEM((tiles * pad_rows, chans), f32),
+        pltpu.VMEM((pixels, chans), f32),
+        pltpu.VMEM((pixels, chans), f32),
+        pltpu.VMEM((pixels, chans), bf16),
+        pltpu.VMEM((pixels, hidden), bf16),
+        pltpu.VMEM((pixels, chans), f32),
+        pltpu.VMEM((2 * chans, hidden), bf16),
+    ]
+
+
+def split_weights(w_in, w_gelu):
+    chans = w_in.shape[0]
+    scaled = w_in[...].astype(jnp.float32) * 0.7071067811865476
+    high = scaled.astype(jnp.bfloat16)
+    w_gelu[:chans, :] = high
+    w_gelu[chans:, :] = (scaled - high.astype(jnp.float32)).astype(jnp.bfloat16)
 
 
 def inner_kernel(
@@ -175,12 +202,15 @@
     invs,
     normed,
     gb,
+    back,
+    w_gelu,
 ):
     side = feats.shape[1]
     chans = feats.shape[3]
     pixels = side * side
     cot_rows = cot_all.shape[0] // peers
     count, begin, me = meta[0], meta[1], meta[2]
+    split_weights(w_in, w_gelu)
     for ref in (asum, ge, tap_sum, gain_sum, gi_sum, pad):
         ref[...] = jnp.zeros_like(ref)
 
@@ -215,8 +245,8 @@
             INNER_TILES,
             starts,
             [True] * len(starts),
-            (kern, gain[...], w_in, w_in_t),
-            (pad, unit, invs, normed, gb),
+            (kern, gain[...], w_gelu, w_in_t),
+            (pad, unit, invs, normed, gb, back),
             (asum, ga, tap_sum, gain_sum, gi_sum),
         )
 
@@ -251,6 +281,8 @@
     invs,
     normed,
     gb,
+    back,
+    w_gelu,
     asum,
     tap_sum,
     gain_sum,
@@ -266,6 +298,7 @@
         target[...] = source[...]
     embed_out[...] = jnp.zeros_like(embed_out)
 
+    split_weights(w_in, w_gelu)
     paired = lax.rem(me, 2) * -2 + 1
 
     def strip(column, which, slot):
@@ -319,12 +352,12 @@
             BORDER_TILES,
             starts,
             [False, False, True, True],
-            (kern, gain[...], w_in, w_in_t),
-            (pad, unit, invs, normed, gb),
+            (kern, gain[...], w_gelu, w_in_t),
+            (pad, unit, invs, normed, gb, back),
             (asum, ga, tap_sum, gain_sum, gi_sum),
         )
 
-    asum[...] = 0.5 * asum[...]
+    asum[...] = 0.7071067811865476 * asum[...]
     go_sum[...] = lax.dot_general(
         asum[...], ge[...], (((0,), (0,)), ((), ())), precision=HIGHEST, preferred_element_type=jnp.float32
     )
@@ -346,12 +379,13 @@
         grad_out[to, :per, :] = gi_sum[offset : offset + per, columns * chans : (columns + 1) * chans]
         grad_out[to, per : 2 * per, :] = go_sum[block * per : (block + 1) * per, :]
         grad_out[to, 2 * per :, :] = jnp.zeros((SMALL_ROWS, chans), jnp.float32)
+    half = side // 2
     for i in range(9):
         grad_out[(i // SMALL_ROWS) ^ mine, pl.ds(2 * per + i % SMALL_ROWS, 1), :] = math.sqrt(chans) * jnp.sum(
-            tap_sum[i * side : (i + 1) * side, :], axis=0, keepdims=True
+            tap_sum[i * half : (i + 1) * half, :], axis=0, keepdims=True
         )
-    grad_out[1 ^ mine, pl.ds(2 * per + 1, 1), :] = math.sqrt(chans) * jnp.sum(
-        gain_sum[...], axis=0, keepdims=True
+    grad_out[1 ^ mine, pl.ds(2 * per + 1, 1), :] = math.sqrt(chans) * (
+        jnp.sum(gain_sum[...], axis=0, keepdims=True) / gain[...]
     )
 
 
@@ -387,7 +421,7 @@
     for place, (axis, bit) in enumerate(reversed(halving)):
         mine = mine + jnp.where((lax.axis_index(axis) & bit) > 0, 1 << place, 0)
 
-    strips, inner, csum = border_strips(feats)
+    feats, strips, inner, csum = border_strips(feats)
     gathered = jnp.concatenate(
         [cot_rows, jnp.broadcast_to(tissue_count.astype(jnp.float32), (8, chans))], axis=0
     )[None]
@@ -414,15 +448,6 @@
     per = hidden // parts
     block_rows = 2 * per + SMALL_ROWS
 
-    def line_scratch(pad_rows, pixels):
-        return [
-            pltpu.VMEM((pad_rows, chans), f32),
-            pltpu.VMEM((pixels, chans), f32),
-            pltpu.VMEM((pixels, chans), f32),
-            pltpu.VMEM((pixels, chans), jnp.bfloat16),
-            pltpu.VMEM((pixels, hidden), jnp.bfloat16),
-        ]
-
     asum, ge, ga, tap_sum, gain_sum, gi_sum, w_in_t = pl.pallas_call(
         functools.partial(inner_kernel, peers, work),
         in_specs=[smem] * 2 + [vmem] * 6,
@@ -431,12 +456,12 @@
             shape((slots, hidden), f32),
             shape((slots, chans), f32),
             shape((slots, hidden), f32),
-            shape((9 * side, chans), f32),
-            shape((side, chans), f32),
+            shape((9 * (side // 2), chans), f32),
+            shape((side // 2, chans), f32),
             shape((chans, hidden), f32),
             shape((hidden, chans), jnp.bfloat16),
         ],
-        scratch_shapes=line_scratch(INNER_TILES * (side + 1) * INNER_PITCH, INNER_TILES * side * (side - 2)),
+        scratch_shapes=line_scratch(INNER_TILES, (side + 1) * INNER_PITCH, side - 2, side, chans, hidden),
         compiler_params=params,
     )(
         meta,
@@ -453,11 +478,11 @@
         in_specs=[smem] * 3 + [vmem] * 16,
         out_specs=[vmem] * 2,
         out_shape=[shape((peers * work, chans), f32), shape((parts, block_rows, chans), f32)],
-        scratch_shapes=line_scratch(BORDER_TILES * 2 * (side + 2) * LINE_PITCH, BORDER_TILES * 4 * side)
+        scratch_shapes=line_scratch(BORDER_TILES, 2 * (side + 2) * LINE_PITCH, 4, side, chans, hidden)
         + [
             pltpu.VMEM((slots, hidden), f32),
-            pltpu.VMEM((9 * side, chans), f32),
-            pltpu.VMEM((side, chans), f32),
+            pltpu.VMEM((9 * (side // 2), chans), f32),
+            pltpu.VMEM((side // 2, chans), f32),
             pltpu.VMEM((chans, hidden), f32),
             pltpu.VMEM((hidden, chans), f32),
             pltpu.VMEM((slots, chans), f32),

time: 118 us -> 113 us (0.958)
  Pallas kernels: 49.5 us -> 7.46 us
  waiting for transfers between devices: 32.6 us -> 59.4 us
  starting transfers between devices: 24.5 us -> 34.4 us
  local copies, waits for them, and re-layouts: 6.09 us -> 7.31 us
    pallas_call x1, Pallas kernels: 30.3 us -> 1.06 us  [local(): pl.pallas_call(functools.partial(inner_kernel, peers, work), in_specs=[sm...]
    ppermute x12, waiting for transfers between devices: 32.6 us -> 59.4 us  [swap(): return lax.ppermute(value, axis, [(i, i ^ bit) for i in range(count)])]
    pallas_call x1, Pallas kernels: 14.6 us -> 1.9 us  [local(): pl.pallas_call(functools.partial(border_kernel, peers, work, parts), in_s...]
    ppermute x12, starting transfers between devices: 22.9 us -> 32.7 us  [swap(): return lax.ppermute(value, axis, [(i, i ^ bit) for i in range(count)])]
    unnamed x18 -> x21, local copies, waits for them, and re-layouts: 5.3 us -> 7.24 us
  transfers between devices with their start and end apart: 13 -> 13, of which waited for: 11 -> 11; matrix products, arithmetic and copies ran while one was open for 1% -> 1% of each run, Pallas kernels for 28% -> 4%
where the time goes in v4:
time: 113 us
  waiting for transfers between devices  59.4 us (53%)
  starting transfers between devices  34.4 us (30%)
  Pallas kernels  7.46 us (7%)
  local copies, waits for them, and re-layouts  7.31 us (6%)
  between operations  2.83 us (3%)
  other arithmetic  1.76 us (2%)
    ppermute x12, waiting for transfers between devices, swap(): return lax.ppermute(value, axis, [(i, i ^ bit) for i in range(count)])  59.4 us
    ppermute x12, starting transfers between devices, swap(): return lax.ppermute(value, axis, [(i, i ^ bit) for i in range(count)])  32.7 us
    unnamed x21, local copies, waits for them, and re-layouts  7.24 us
    pallas_call x1, Pallas kernels, border_strips(): pl.pallas_call(strip_kernel, in_specs=[spec], out_specs=[spec] * 4, out_s...  3.09 us
  transfers between devices with their start and end apart: 13, of which 11 were waited for; matrix products, arithmetic and copies ran while one was open for 1% of the time, Pallas kernels for 4%

profile of v4, /device:TPU:0, one launch (start us, length us, event | category | flops | bytes accessed | tf_op | source)
XLA Modules:
  0.0 113.1 jit_solution(3356878427724432220)
XLA Ops:
  0.6 0.0 copy-start.9
  0.6 2.2 %copy.29 = bf16[1,64,16,16,128]{4,3,2,1,0:T(8,128)(2,1)S(1)} copy(bf16[1,64,16,16,128]{4,3,2,1,0:T(8,128)(2,1)} %param.10) | data formatting | bytes 8388608
  3.5 0.0 copy-done.9
  3.6 3.0 %collective-permute-start = (f32[1,40,128]{2,1,0:T(8,128)S(1)}, f32[1,40,128]{2,1,0:T(8,128)S(1)}, u32[]{:S(2)}, u32[]{:S(2)}) collective-permute-start(f32[1,40,128]{2,1,0:T(8,128)S(1)} %pad_bitcast_fusion), channel_id=1, source_target_pairs={{0,1},{1,0},{2,3},{3,2},{4,5},{5,4},{6,7},{7,6},{8,9},{9,8},{10,11... | collective-permute-start | bytes 61448 | tf_op jit(solution)/shard_map/ppermute | solution.py:28
  6.6 3.1 %shard_map.137 = (bf16[64,16,16,128]{3,2,1,0:T(8,128)(2,1)S(1)}, bf16[64,4,16,128]{3,2,1,0:T(8,128)(2,1)S(1)}, bf16[64,4,16,128]{3,2,1,0:T(8,128)(2,1)S(1)}, f32[64,128]{1,0:T(8,128)S(1)}) custom-call(bf16[64,16,16,128]{3,2,1,0:T(8,128)(2,1)S(1)} %bitcast.53), custom_call_target="tpu_custom_call", output_to_operand_aliasing={{0}: (0, {})} | custom-call | flops 1000000000 | bytes 10000000 | tf_op jit(solution)/shard_map/pallas_call | solution.py:64
  9.7 0.0 copy-start
  9.7 1.9 %copy-done = bf16[64,16,16,128]{3,2,1,0:T(8,128)(2,1)} copy-done((bf16[64,16,16,128]{3,2,1,0:T(8,128)(2,1)}, bf16[64,16,16,128]{3,2,1,0:T(8,128)(2,1)S(1)}, u32[]{:S(2)}) %copy-start) | copy-done | bytes 4194328
  11.6 0.0 collective-permute-done
  11.6 1.6 %collective-permute-start.1 = (f32[2,40,128]{2,1,0:T(8,128)S(1)}, f32[2,40,128]{2,1,0:T(8,128)S(1)}, u32[]{:S(2)}, u32[]{:S(2)}) collective-permute-start(f32[2,40,128]{2,1,0:T(8,128)S(1)} %pad_maximum_fusion.7), channel_id=1, source_target_pairs={{0,2},{1,3},{2,0},{3,1},{4,6},{5,7},{6,4},{7,5},{8,10},{9,11},{10,... | collective-permute-start | bytes 122888 | tf_op jit(solution)/shard_map/ppermute | solution.py:28
  13.2 2.4 %collective-permute-done.1 = f32[2,40,128]{2,1,0:T(8,128)S(1)} collective-permute-done((f32[2,40,128]{2,1,0:T(8,128)S(1)}, f32[2,40,128]{2,1,0:T(8,128)S(1)}, u32[]{:S(2)}, u32[]{:S(2)}) %collective-permute-start.1) | collective-permute-done | bytes 40992 | tf_op jit(solution)/shard_map/ppermute | solution.py:28
  15.6 2.6 %collective-permute-start.2 = (f32[4,40,128]{2,1,0:T(8,128)S(1)}, f32[4,40,128]{2,1,0:T(8,128)S(1)}, u32[]{:S(2)}, u32[]{:S(2)}) collective-permute-start(f32[4,40,128]{2,1,0:T(8,128)S(1)} %pad_maximum_fusion.6), channel_id=1, source_target_pairs={{0,4},{1,5},{2,6},{3,7},{4,0},{5,1},{6,2},{7,3},{8,12},{9,13},{10,... | collective-permute-start | bytes 245768 | tf_op jit(solution)/shard_map/ppermute | solution.py:28
  18.2 0.5 collective-permute-start.3
  18.7 2.2 %collective-permute-done.2 = f32[4,40,128]{2,1,0:T(8,128)S(1)} collective-permute-done((f32[4,40,128]{2,1,0:T(8,128)S(1)}, f32[4,40,128]{2,1,0:T(8,128)S(1)}, u32[]{:S(2)}, u32[]{:S(2)}) %collective-permute-start.2) | collective-permute-done | bytes 81952 | tf_op jit(solution)/shard_map/ppermute | solution.py:28
  21.0 1.7 %collective-permute-start.4 = (bf16[64,4,16,128]{3,2,1,0:T(8,128)(2,1)S(1)}, bf16[64,4,16,128]{3,2,1,0:T(8,128)(2,1)}, u32[]{:S(2)}, u32[]{:S(2)}) collective-permute-start(bf16[64,4,16,128]{3,2,1,0:T(8,128)(2,1)S(1)} %get-tuple-element.30.own), channel_id=1, source_target_pairs={{1,2},{3,4},{5,6},{2,1},{4,3},{6,5},{9,10},{11,12},{13,14},{10,9},... | collective-permute-start | bytes 3145736 | tf_op jit(solution)/shard_map/ppermute | solution.py:435
  23.3 0.2 convert_reduce_fusion
  23.6 0.6 fusion.3
  24.9 0.1 pad_add_fusion.meta
  24.9 0.0 copy-done.2
  24.9 0.0 copy-done.5
  24.9 0.0 copy-done.7
  24.9 0.0 copy-done.8
  25.0 0.0 copy-start.1
  25.0 2.2 %copy-done.1 = bf16[64,16,16,128]{3,2,1,0:T(8,128)(2,1)S(1)} copy-done((bf16[64,16,16,128]{3,2,1,0:T(8,128)(2,1)S(1)}, bf16[64,16,16,128]{3,2,1,0:T(8,128)(2,1)}, u32[]{:S(2)}) %copy-start.1) | copy-done | bytes 4194328
  27.1 0.9 copy-done.3
  28.1 1.1 shard_map.138
  29.1 32.8 %collective-permute-done.3.halo_pair = bf16[64,4,16,128]{3,2,1,0:T(8,128)(2,1)S(1)} collective-permute-done((bf16[64,4,16,128]{3,2,1,0:T(8,128)(2,1)S(1)}, bf16[64,4,16,128]{3,2,1,0:T(8,128)(2,1)S(1)}, u32[]{:S(2)}, u32[]{:S(2)}) %collective-permute-start.3) | collective-permute-done | bytes 1048608 | tf_op jit(solution)/shard_map/ppermute | solution.py:28
  61.9 0.0 collective-permute-done.4.halo_cross
  61.9 0.0 copy-done.6
  61.9 0.0 copy-done.4
  61.9 1.9 %shard_map.139 = (f32[256,128]{1,0:T(8,128)S(1)}, f32[8,136,128]{2,1,0:T(8,128)S(1)}) custom-call(s32[4]{0:T(128)S(1)} %pad_add_fusion.meta, s32[8]{0:T(128)S(1)} %bitcast.58, s32[8,64]{1,0:T(8,128)S(1)} %bitcast.56, bf16[64,4,16,128]{3,2,1,0:T(8,128)(2,1)S(1)} %get-tuple-element.30.own, bf16[64,4,16,128]{3,2,1,0:T(8,128)(2,1)S(1)} %get-tuple-element.31.inner, ...), custom_call_target="tpu_custom_call" | custom-call | tf_op jit(solution)/shard_map/pallas_call | solution.py:476
  63.9 8.8 %collective-permute-start.5 = (f32[4,136,128]{2,1,0:T(8,128)S(1)}, f32[4,136,128]{2,1,0:T(8,128)S(1)}, u32[]{:S(2)}, u32[]{:S(2)}) collective-permute-start(f32[4,136,128]{2,1,0:T(8,128)S(1)} %slice.61), channel_id=1, source_target_pairs={{0,8},{8,0},{16,24},{24,16},{1,9},{9,1},{17,25},{25,17},{2,10},{10... | collective-permute-start | bytes 835592 | tf_op jit(solution)/shard_map/ppermute | solution.py:28
  72.7 1.2 %collective-permute-done.5 = f32[4,136,128]{2,1,0:T(8,128)S(1)} collective-permute-done((f32[4,136,128]{2,1,0:T(8,128)S(1)}, f32[4,136,128]{2,1,0:T(8,128)S(1)}, u32[]{:S(2)}, u32[]{:S(2)}) %collective-permute-start.5) | collective-permute-done | bytes 278560 | tf_op jit(solution)/shard_map/ppermute | solution.py:28
  73.9 1.7 %collective-permute-start.6 = (f32[2,136,128]{2,1,0:T(8,128)S(1)}, f32[2,136,128]{2,1,0:T(8,128)S(1)}, u32[]{:S(2)}, u32[]{:S(2)}) collective-permute-start(f32[2,136,128]{2,1,0:T(8,128)S(1)} %slice.79), channel_id=1, source_target_pairs={{0,16},{8,24},{16,0},{24,8},{1,17},{9,25},{17,1},{25,9},{2,18},{10... | collective-permute-start | bytes 417800 | tf_op jit(solution)/shard_map/ppermute | solution.py:28
  75.6 4.3 %collective-permute-done.6 = f32[2,136,128]{2,1,0:T(8,128)S(1)} collective-permute-done((f32[2,136,128]{2,1,0:T(8,128)S(1)}, f32[2,136,128]{2,1,0:T(8,128)S(1)}, u32[]{:S(2)}, u32[]{:S(2)}) %collective-permute-start.6) | collective-permute-done | bytes 139296 | tf_op jit(solution)/shard_map/ppermute | solution.py:28
  80.0 2.5 %collective-permute-start.7 = (f32[264,128]{1,0:T(8,128)S(1)}, f32[264,128]{1,0:T(8,128)S(1)}, u32[]{:S(2)}, u32[]{:S(2)}) collective-permute-start(f32[264,128]{1,0:T(8,128)S(1)} %pad_maximum_fusion.3), channel_id=1, source_target_pairs={{0,1},{1,0},{2,3},{3,2},{4,5},{5,4},{6,7},{7,6},{8,9},{9,8},{10,11... | collective-permute-start | bytes 405512 | tf_op jit(solution)/shard_map/ppermute | solution.py:28
  82.4 3.1 %collective-permute-done.7 = f32[264,128]{1,0:T(8,128)S(1)} collective-permute-done((f32[264,128]{1,0:T(8,128)S(1)}, f32[264,128]{1,0:T(8,128)S(1)}, u32[]{:S(2)}, u32[]{:S(2)}) %collective-permute-start.7) | collective-permute-done | bytes 135200 | tf_op jit(solution)/shard_map/ppermute | solution.py:28
  85.5 4.8 %collective-permute-start.8 = (f32[200,128]{1,0:T(8,128)S(1)}, f32[200,128]{1,0:T(8,128)S(1)}, u32[]{:S(2)}, u32[]{:S(2)}) collective-permute-start(f32[200,128]{1,0:T(8,128)S(1)} %pad_maximum_fusion.4), channel_id=1, source_target_pairs={{0,2},{1,3},{2,0},{3,1},{4,6},{5,7},{6,4},{7,5},{8,10},{9,11},{10,... | collective-permute-start | bytes 307208 | tf_op jit(solution)/shard_map/ppermute | solution.py:28
  90.3 2.6 %collective-permute-done.8 = f32[200,128]{1,0:T(8,128)S(1)} collective-permute-done((f32[200,128]{1,0:T(8,128)S(1)}, f32[200,128]{1,0:T(8,128)S(1)}, u32[]{:S(2)}, u32[]{:S(2)}) %collective-permute-start.8) | collective-permute-done | bytes 102432 | tf_op jit(solution)/shard_map/ppermute | solution.py:28
  93.0 3.6 %collective-permute-start.9 = (f32[168,128]{1,0:T(8,128)S(1)}, f32[168,128]{1,0:T(8,128)S(1)}, u32[]{:S(2)}, u32[]{:S(2)}) collective-permute-start(f32[168,128]{1,0:T(8,128)S(1)} %pad_maximum_fusion.5), channel_id=1, source_target_pairs={{0,4},{1,5},{2,6},{3,7},{4,0},{5,1},{6,2},{7,3},{8,12},{9,13},{10,... | collective-permute-start | bytes 258056 | tf_op jit(solution)/shard_map/ppermute | solution.py:28
  96.6 2.5 %collective-permute-done.9 = f32[168,128]{1,0:T(8,128)S(1)} collective-permute-done((f32[168,128]{1,0:T(8,128)S(1)}, f32[168,128]{1,0:T(8,128)S(1)}, u32[]{:S(2)}, u32[]{:S(2)}) %collective-permute-start.9) | collective-permute-done | bytes 86048 | tf_op jit(solution)/shard_map/ppermute | solution.py:28
  99.1 3.5 %collective-permute-start.10 = (f32[1,136,128]{2,1,0:T(8,128)S(1)}, f32[1,136,128]{2,1,0:T(8,128)S(1)}, u32[]{:S(2)}, u32[]{:S(2)}) collective-permute-start(f32[1,136,128]{2,1,0:T(8,128)S(1)} %fusion), channel_id=1, source_target_pairs={{0,1},{1,0},{2,3},{3,2},{4,5},{5,4},{6,7},{7,6},{8,9},{9,8},{10,11... | collective-permute-start | bytes 208904 | tf_op jit(solution)/shard_map/ppermute | solution.py:28
  102.6 2.3 %collective-permute-done.10 = f32[1,136,128]{2,1,0:T(8,128)S(1)} collective-permute-done((f32[1,136,128]{2,1,0:T(8,128)S(1)}, f32[1,136,128]{2,1,0:T(8,128)S(1)}, u32[]{:S(2)}, u32[]{:S(2)}) %collective-permute-start.10) | collective-permute-done | bytes 69664 | tf_op jit(solution)/shard_map/ppermute | solution.py:28
  104.9 0.1 collective-permute-start.11
  105.0 5.0 %collective-permute-done.11 = f32[2,136,128]{2,1,0:T(8,128)S(1)} collective-permute-done((f32[2,136,128]{2,1,0:T(8,128)S(1)}, f32[2,136,128]{2,1,0:T(8,128)S(1)}, u32[]{:S(2)}, u32[]{:S(2)}) %collective-permute-start.11) | collective-permute-done | bytes 139296 | tf_op jit(solution)/shard_map/ppermute | solution.py:28
  110.1 0.1 collective-permute-start.12
  110.2 0.6 fusion.2
  110.8 0.9 collective-permute-done.12.far
  111.7 1.4 %shard_map.140 = (f32[9,128]{1,0:T(8,128)}, f32[1,128]{1,0:T(1,128)}, f32[128,512]{1,0:T(8,128)}, f32[512,128]{1,0:T(8,128)}) custom-call(s32[4]{0:T(128)S(1)} %pad_add_fusion.meta, f32[4,136,128]{2,1,0:T(8,128)S(1)} %pad_maximum_fusion.near, f32[4,136,128]{2,1,0:T(8,128)S(1)} %collective-permute-done.12.far), custom_call_target="tpu_custom_call" | custom-call | tf_op jit(solution)/shard_map/pallas_call | solution.py:534
  (31 shorter events, 0.3 us)
Async XLA Ops:
  0.6 2.9 %copy-start.9 = (f32[1,32,128]{2,1,0:T(8,128)S(1)}, f32[1,32,128]{2,1,0:T(8,128)}, u32[]{:S(2)}) copy-start(f32[1,32,128]{2,1,0:T(8,128)} %param.19) | copy-start | bytes 49156
  2.8 22.1 %copy-start.2 = (bf16[128,512]{1,0:T(8,128)(2,1)S(1)}, bf16[128,512]{1,0:T(8,128)(2,1)}, u32[]{:S(2)}) copy-start(bf16[128,512]{1,0:T(8,128)(2,1)} %w_in.3) | copy-start | bytes 393220
  2.8 22.1 %copy-start.5 = (bf16[9,128]{1,0:T(8,128)(2,1)S(1)}, bf16[9,128]{1,0:T(8,128)(2,1)}, u32[]{:S(2)}) copy-start(bf16[9,128]{1,0:T(8,128)(2,1)} %kern.3) | copy-start | bytes 6916
  2.8 22.1 %copy-start.7 = (s32[1,8]{1,0:T(1,128)S(1)}, s32[1,8]{1,0:T(1,128)}, u32[]{:S(2)}) copy-start(s32[1,8]{1,0:T(1,128)} %param.13) | copy-start | bytes 100
  2.8 22.1 %copy-start.8 = (f32[128]{0:T(128)S(1)}, f32[128]{0:T(128)}, u32[]{:S(2)}) copy-start(f32[128]{0:T(128)} %param.16) | copy-start | bytes 1540
  3.6 8.1 %collective-permute-start = (f32[1,40,128]{2,1,0:T(8,128)S(1)}, f32[1,40,128]{2,1,0:T(8,128)S(1)}, u32[]{:S(2)}, u32[]{:S(2)}) collective-permute-start(f32[1,40,128]{2,1,0:T(8,128)S(1)} %pad_bitcast_fusion), channel_id=1, source_target_pairs={{0,1},{1,0},{2,3},{3,2},{4,5},{5,4},{6,7},{7,6},{8,9},{9,8},{10,11... | collective-permute-start | bytes 61448 | tf_op jit(solution)/shard_map/ppermute | solution.py:28
  6.6 55.3 %copy-start.6 = (s32[1,64,8]{1,2,0:T(8,128)S(1)}, s32[1,64,8]{1,2,0:T(8,128)}, u32[]{:S(2)}) copy-start(s32[1,64,8]{1,2,0:T(8,128)} %param.12) | copy-start | bytes 6148
  9.7 1.9 %copy-start = (bf16[64,16,16,128]{3,2,1,0:T(8,128)(2,1)}, bf16[64,16,16,128]{3,2,1,0:T(8,128)(2,1)S(1)}, u32[]{:S(2)}) copy-start(bf16[64,16,16,128]{3,2,1,0:T(8,128)(2,1)S(1)} %get-tuple-element.32.feats) | copy-start | bytes 12582916
  11.6 4.0 %collective-permute-start.1 = (f32[2,40,128]{2,1,0:T(8,128)S(1)}, f32[2,40,128]{2,1,0:T(8,128)S(1)}, u32[]{:S(2)}, u32[]{:S(2)}) collective-permute-start(f32[2,40,128]{2,1,0:T(8,128)S(1)} %pad_maximum_fusion.7), channel_id=1, source_target_pairs={{0,2},{1,3},{2,0},{3,1},{4,6},{5,7},{6,4},{7,5},{8,10},{9,11},{10,... | collective-permute-start | bytes 122888 | tf_op jit(solution)/shard_map/ppermute | solution.py:28
  15.6 5.3 %collective-permute-start.2 = (f32[4,40,128]{2,1,0:T(8,128)S(1)}, f32[4,40,128]{2,1,0:T(8,128)S(1)}, u32[]{:S(2)}, u32[]{:S(2)}) collective-permute-start(f32[4,40,128]{2,1,0:T(8,128)S(1)} %pad_maximum_fusion.6), channel_id=1, source_target_pairs={{0,4},{1,5},{2,6},{3,7},{4,0},{5,1},{6,2},{7,3},{8,12},{9,13},{10,... | collective-permute-start | bytes 245768 | tf_op jit(solution)/shard_map/ppermute | solution.py:28
  18.2 43.7 %collective-permute-start.3 = (bf16[64,4,16,128]{3,2,1,0:T(8,128)(2,1)S(1)}, bf16[64,4,16,128]{3,2,1,0:T(8,128)(2,1)S(1)}, u32[]{:S(2)}, u32[]{:S(2)}) collective-permute-start(bf16[64,4,16,128]{3,2,1,0:T(8,128)(2,1)S(1)} %get-tuple-element.30.own), channel_id=1, source_target_pairs={{0,1},{1,0},{2,3},{3,2},{4,5},{5,4},{6,7},{7,6},{8,9},{9,8},{10,11... | collective-permute-start | bytes 3145736 | tf_op jit(solution)/shard_map/ppermute | solution.py:28
  21.0 40.9 %collective-permute-start.4 = (bf16[64,4,16,128]{3,2,1,0:T(8,128)(2,1)S(1)}, bf16[64,4,16,128]{3,2,1,0:T(8,128)(2,1)}, u32[]{:S(2)}, u32[]{:S(2)}) collective-permute-start(bf16[64,4,16,128]{3,2,1,0:T(8,128)(2,1)S(1)} %get-tuple-element.30.own), channel_id=1, source_target_pairs={{1,2},{3,4},{5,6},{2,1},{4,3},{6,5},{9,10},{11,12},{13,14},{10,9},... | collective-permute-start | bytes 3145736 | tf_op jit(solution)/shard_map/ppermute | solution.py:435
  25.0 2.2 %copy-start.1 = (bf16[64,16,16,128]{3,2,1,0:T(8,128)(2,1)S(1)}, bf16[64,16,16,128]{3,2,1,0:T(8,128)(2,1)}, u32[]{:S(2)}) copy-start(bf16[64,16,16,128]{3,2,1,0:T(8,128)(2,1)} %copy-done) | copy-start | bytes 12582916
  27.1 0.9 copy-start.3
  28.0 33.9 %copy-start.4 = (bf16[512,128]{1,0:T(8,128)(2,1)S(1)}, bf16[512,128]{1,0:T(8,128)(2,1)}, u32[]{:S(2)}) copy-start(bf16[512,128]{1,0:T(8,128)(2,1)} %w_out.3) | copy-start | bytes 393220
  63.9 10.0 %collective-permute-start.5 = (f32[4,136,128]{2,1,0:T(8,128)S(1)}, f32[4,136,128]{2,1,0:T(8,128)S(1)}, u32[]{:S(2)}, u32[]{:S(2)}) collective-permute-start(f32[4,136,128]{2,1,0:T(8,128)S(1)} %slice.61), channel_id=1, source_target_pairs={{0,8},{8,0},{16,24},{24,16},{1,9},{9,1},{17,25},{25,17},{2,10},{10... | collective-permute-start | bytes 835592 | tf_op jit(solution)/shard_map/ppermute | solution.py:28
  73.9 6.0 %collective-permute-start.6 = (f32[2,136,128]{2,1,0:T(8,128)S(1)}, f32[2,136,128]{2,1,0:T(8,128)S(1)}, u32[]{:S(2)}, u32[]{:S(2)}) collective-permute-start(f32[2,136,128]{2,1,0:T(8,128)S(1)} %slice.79), channel_id=1, source_target_pairs={{0,16},{8,24},{16,0},{24,8},{1,17},{9,25},{17,1},{25,9},{2,18},{10... | collective-permute-start | bytes 417800 | tf_op jit(solution)/shard_map/ppermute | solution.py:28
  80.0 5.5 %collective-permute-start.7 = (f32[264,128]{1,0:T(8,128)S(1)}, f32[264,128]{1,0:T(8,128)S(1)}, u32[]{:S(2)}, u32[]{:S(2)}) collective-permute-start(f32[264,128]{1,0:T(8,128)S(1)} %pad_maximum_fusion.3), channel_id=1, source_target_pairs={{0,1},{1,0},{2,3},{3,2},{4,5},{5,4},{6,7},{7,6},{8,9},{9,8},{10,11... | collective-permute-start | bytes 405512 | tf_op jit(solution)/shard_map/ppermute | solution.py:28
  85.5 7.4 %collective-permute-start.8 = (f32[200,128]{1,0:T(8,128)S(1)}, f32[200,128]{1,0:T(8,128)S(1)}, u32[]{:S(2)}, u32[]{:S(2)}) collective-permute-start(f32[200,128]{1,0:T(8,128)S(1)} %pad_maximum_fusion.4), channel_id=1, source_target_pairs={{0,2},{1,3},{2,0},{3,1},{4,6},{5,7},{6,4},{7,5},{8,10},{9,11},{10,... | collective-permute-start | bytes 307208 | tf_op jit(solution)/shard_map/ppermute | solution.py:28
  93.0 6.1 %collective-permute-start.9 = (f32[168,128]{1,0:T(8,128)S(1)}, f32[168,128]{1,0:T(8,128)S(1)}, u32[]{:S(2)}, u32[]{:S(2)}) collective-permute-start(f32[168,128]{1,0:T(8,128)S(1)} %pad_maximum_fusion.5), channel_id=1, source_target_pairs={{0,4},{1,5},{2,6},{3,7},{4,0},{5,1},{6,2},{7,3},{8,12},{9,13},{10,... | collective-permute-start | bytes 258056 | tf_op jit(solution)/shard_map/ppermute | solution.py:28
  99.1 5.8 %collective-permute-start.10 = (f32[1,136,128]{2,1,0:T(8,128)S(1)}, f32[1,136,128]{2,1,0:T(8,128)S(1)}, u32[]{:S(2)}, u32[]{:S(2)}) collective-permute-start(f32[1,136,128]{2,1,0:T(8,128)S(1)} %fusion), channel_id=1, source_target_pairs={{0,1},{1,0},{2,3},{3,2},{4,5},{5,4},{6,7},{7,6},{8,9},{9,8},{10,11... | collective-permute-start | bytes 208904 | tf_op jit(solution)/shard_map/ppermute | solution.py:28
  104.9 5.1 %collective-permute-start.11 = (f32[2,136,128]{2,1,0:T(8,128)S(1)}, f32[2,136,128]{2,1,0:T(8,128)S(1)}, u32[]{:S(2)}, u32[]{:S(2)}) collective-permute-start(f32[2,136,128]{2,1,0:T(8,128)S(1)} %pad_maximum_fusion.2), channel_id=1, source_target_pairs={{0,16},{8,24},{16,0},{24,8},{1,17},{9,25},{17,1},{25,9},{2,18},{10... | collective-permute-start | bytes 417800 | tf_op jit(solution)/shard_map/ppermute | solution.py:28
  110.1 1.6 %collective-permute-start.12 = (f32[4,136,128]{2,1,0:T(8,128)S(1)}, f32[4,136,128]{2,1,0:T(8,128)S(1)}, u32[]{:S(2)}, u32[]{:S(2)}) collective-permute-start(f32[4,136,128]{2,1,0:T(8,128)S(1)} %pad_maximum_fusion.near), channel_id=1, source_target_pairs={{0,8},{8,0},{16,24},{24,16},{1,9},{9,1},{17,25},{25,17},{2,10},{10... | collective-permute-start | bytes 835592 | tf_op jit(solution)/shard_map/ppermute | solution.py:28

commit v5 on v4

--- a/solution.py
+++ b/solution.py
@@ -17,6 +17,7 @@
 SMALL_ROWS = 8
 STRIP_TILES = 4
 VMEM_BYTES = 32 * 1024 * 1024
+INNER_BYTES = 53 * 1024 * 1024
 
 
 def bits_of(count):
@@ -28,7 +29,7 @@
     return lax.ppermute(value, axis, [(i, i ^ bit) for i in range(count)])
 
 
-def strip_kernel(tiles, held, strips, inner, csum):
+def strip_kernel(tiles, strips, inner, csum):
     slots, side, _, chans = tiles.shape
     columns = (0, side - 1, 1, side - 2)
     rows = (len(columns) + 1) * side
@@ -64,14 +65,8 @@
     return pl.pallas_call(
         strip_kernel,
         in_specs=[spec],
-        out_specs=[spec] * 4,
-        out_shape=[
-            jax.ShapeDtypeStruct(tiles.shape, tiles.dtype),
-            shape,
-            shape,
-            jax.ShapeDtypeStruct((slots, chans), jnp.float32),
-        ],
-        input_output_aliases={0: 0},
+        out_specs=[spec] * 3,
+        out_shape=[shape, shape, jax.ShapeDtypeStruct((slots, chans), jnp.float32)],
         compiler_params=pltpu.CompilerParams(vmem_limit_bytes=VMEM_BYTES),
         cost_estimate=pl.CostEstimate(flops=10**9, bytes_accessed=10**7, transcendentals=0),
     )(tiles)
@@ -184,12 +179,13 @@
     work,
     meta,
     dealing,
-    feats,
-    cot_all,
+    feats_hbm,
+    cot_near,
+    cot_far,
     kern,
     gain,
     w_in,
-    w_out,
+    w_out_hbm,
     asum,
     ge,
     ga,
@@ -197,6 +193,7 @@
     gain_sum,
     gi_sum,
     w_in_t,
+    begin_out,
     pad,
     unit,
     invs,
@@ -204,12 +201,38 @@
     gb,
     back,
     w_gelu,
+    feats,
+    w_out,
+    cot_all,
+    tile_sems,
+    weight_sem,
 ):
     side = feats.shape[1]
     chans = feats.shape[3]
     pixels = side * side
     cot_rows = cot_all.shape[0] // peers
-    count, begin, me = meta[0], meta[1], meta[2]
+    count, turned, me = meta[0], meta[1], meta[2]
+    steps = lax.div(count + INNER_TILES - 1, INNER_TILES)
+
+    def tiles_copy(step):
+        taken = pl.ds(step * INNER_TILES, INNER_TILES)
+        return pltpu.make_async_copy(feats_hbm.at[taken], feats.at[taken], tile_sems.at[step])
+
+    weight_copy = pltpu.make_async_copy(w_out_hbm, w_out, weight_sem)
+    weight_copy.start()
+
+    @pl.loop(0, steps)
+    def _(step):
+        tiles_copy(step).start()
+
+    half_rows = cot_near.shape[0]
+    cot_all[:half_rows, :] = cot_near[...]
+    cot_all[half_rows:, :] = cot_far[...]
+    counts = cot_all[pl.ds(work, peers, stride=cot_rows), :]
+    whose = lax.broadcasted_iota(jnp.int32, counts.shape, 0) ^ me
+    lane = lax.broadcasted_iota(jnp.int32, counts.shape, 1)
+    begin = turned + jnp.sum(jnp.where((whose < me) & (lane == 0), counts, 0.0)).astype(jnp.int32)
+    begin_out[0] = begin
     split_weights(w_in, w_gelu)
     for ref in (asum, ge, tap_sum, gain_sum, gi_sum, pad):
         ref[...] = jnp.zeros_like(ref)
@@ -222,6 +245,7 @@
         ge[pl.ds(slot, 1), :] = cot_all[pl.ds(row, 1), :] * (1.0 / pixels)
 
     w_in_t[...] = w_in[...].astype(jnp.float32).T.astype(jnp.bfloat16)
+    weight_copy.wait()
     ga[...] = 0.5 * lax.dot_general(
         ge[...],
         w_out[...].astype(jnp.float32),
@@ -233,8 +257,9 @@
         [(y - 1 + a) * INNER_PITCH + FIRST - 1 + b for a in range(3) for b in range(3)] for y in range(1, side - 1)
     ]
 
-    @pl.loop(0, lax.div(count + INNER_TILES - 1, INNER_TILES))
+    @pl.loop(0, steps)
     def _(step):
+        tiles_copy(step).wait()
         for part in range(INNER_TILES):
             slot = step * INNER_TILES + part
             base = part * (pad.shape[0] // INNER_TILES)
@@ -256,6 +281,7 @@
     work,
     parts,
     meta,
+    begin_in,
     dealing,
     links,
     own,
@@ -293,7 +319,7 @@
     slots, _, side, chans = own.shape
     hidden = w_in.shape[1]
     pixels = side * side
-    count, begin, me, mine = meta[0], meta[1], meta[2], meta[3]
+    count, begin, me, mine = meta[0], begin_in[0], meta[2], meta[3]
     for target, source in ((asum, asum_in), (tap_sum, tap_in), (gain_sum, gain_in), (gi_sum, gi_in)):
         target[...] = source[...]
     embed_out[...] = jnp.zeros_like(embed_out)
@@ -421,37 +447,38 @@
     for place, (axis, bit) in enumerate(reversed(halving)):
         mine = mine + jnp.where((lax.axis_index(axis) & bit) > 0, 1 << place, 0)
 
-    feats, strips, inner, csum = border_strips(feats)
+    strips, inner, csum = border_strips(feats)
     gathered = jnp.concatenate(
         [cot_rows, jnp.broadcast_to(tissue_count.astype(jnp.float32), (8, chans))], axis=0
     )[None]
     for bit in tile_bits:
-        gathered = jnp.concatenate([gathered, swap(gathered, "tile", bit)], axis=0)
-        if bit == 1:
-            gathered, strips = lax.optimization_barrier((gathered, strips))
+        arrived = swap(gathered, "tile", bit)
+        if bit == tile_bits[0]:
+            arrived, strips = lax.optimization_barrier((arrived, strips))
             halo_pair = swap(strips, "tile", 1)
-    gathered, strips = lax.optimization_barrier((gathered, strips))
+        if bit < tile_bits[-1]:
+            gathered = jnp.concatenate([gathered, arrived], axis=0)
+    arrived, strips = lax.optimization_barrier((arrived, strips))
     cross = [(i, i + 1) for i in range(1, peers - 1, 2)]
     halo_cross = lax.ppermute(strips, "tile", cross + [(j, i) for i, j in cross])
-
-    counts = gathered[:, work, 0].astype(jnp.int32)
-    whose = jnp.arange(peers, dtype=jnp.int32) ^ me
-    begin = jnp.sum(jnp.where(whose < me, counts, 0)) + rotation[0]
-    meta = jnp.stack([tissue_count[0, 0], begin, me, mine]).astype(jnp.int32)
+    meta = jnp.stack([tissue_count[0, 0], rotation[0], me, mine]).astype(jnp.int32)
 
     f32 = jnp.float32
     vmem = pl.BlockSpec(memory_space=pltpu.VMEM)
     smem = pl.BlockSpec(memory_space=pltpu.SMEM)
     shape = jax.ShapeDtypeStruct
     params = pltpu.CompilerParams(vmem_limit_bytes=VMEM_BYTES)
+    inner_params = pltpu.CompilerParams(vmem_limit_bytes=INNER_BYTES)
     gains = gain[None]
     per = hidden // parts
     block_rows = 2 * per + SMALL_ROWS
 
-    asum, ge, ga, tap_sum, gain_sum, gi_sum, w_in_t = pl.pallas_call(
+    far_space = pl.BlockSpec(memory_space=pltpu.HBM)
+    near_rows = peers // 2 * (work + 8)
+    asum, ge, ga, tap_sum, gain_sum, gi_sum, w_in_t, begin = pl.pallas_call(
         functools.partial(inner_kernel, peers, work),
-        in_specs=[smem] * 2 + [vmem] * 6,
-        out_specs=[vmem] * 7,
+        in_specs=[smem] * 2 + [far_space] + [vmem] * 5 + [far_space],
+        out_specs=[vmem] * 7 + [smem],
         out_shape=[
             shape((slots, hidden), f32),
             shape((slots, chans), f32),
@@ -460,14 +487,23 @@
             shape((side // 2, chans), f32),
             shape((chans, hidden), f32),
             shape((hidden, chans), jnp.bfloat16),
+            shape((1,), jnp.int32),
         ],
-        scratch_shapes=line_scratch(INNER_TILES, (side + 1) * INNER_PITCH, side - 2, side, chans, hidden),
-        compiler_params=params,
+        scratch_shapes=line_scratch(INNER_TILES, (side + 1) * INNER_PITCH, side - 2, side, chans, hidden)
+        + [
+            pltpu.VMEM(feats.shape, jnp.bfloat16),
+            pltpu.VMEM((hidden, chans), jnp.bfloat16),
+            pltpu.VMEM((2 * near_rows, chans), f32),
+            pltpu.SemaphoreType.DMA((slots // INNER_TILES,)),
+            pltpu.SemaphoreType.DMA,
+        ],
+        compiler_params=inner_params,
     )(
         meta,
         worker_perm[0],
         feats,
-        gathered.reshape(peers * (work + 8), chans),
+        gathered.reshape(near_rows, chans),
+        arrived.reshape(near_rows, chans),
         kernel,
         gains,
         w_in,
@@ -475,7 +511,7 @@
     )
     embeds, packed = pl.pallas_call(
         functools.partial(border_kernel, peers, work, parts),
-        in_specs=[smem] * 3 + [vmem] * 16,
+        in_specs=[smem] * 4 + [vmem] * 16,
         out_specs=[vmem] * 2,
         out_shape=[shape((peers * work, chans), f32), shape((parts, block_rows, chans), f32)],
         scratch_shapes=line_scratch(BORDER_TILES, 2 * (side + 2) * LINE_PITCH, 4, side, chans, hidden)
@@ -490,6 +526,7 @@
         compiler_params=params,
     )(
         meta,
+        begin,
         worker_perm[0],
         neighbors[0].T,
         strips,

time: 113 us -> 114 us (level)
  Pallas kernels: 7.46 us -> 28.9 us
  starting transfers between devices: 34.4 us -> 24.3 us
  waiting for transfers between devices: 59.4 us -> 51.5 us
  local copies, waits for them, and re-layouts: 7.31 us -> 5.47 us
    pallas_call x1, Pallas kernels: 1.06 us -> 16.1 us  [local(): pl.pallas_call(functools.partial(inner_kernel, peers, work), in_specs=[sm...]
    ppermute x12, starting transfers between devices: 32.7 us -> 22.6 us  [swap(): return lax.ppermute(value, axis, [(i, i ^ bit) for i in range(count)])]
    ppermute x12, waiting for transfers between devices: 59.4 us -> 51.4 us  [swap(): return lax.ppermute(value, axis, [(i, i ^ bit) for i in range(count)])]
    pallas_call x1, Pallas kernels: 1.9 us -> 8.29 us  [local(): pl.pallas_call(functools.partial(border_kernel, peers, work, parts), in_s...]
    unnamed x21 -> x20, local copies, waits for them, and re-layouts: 7.24 us -> 4.68 us
  transfers between devices with their start and end apart: 13 -> 13, of which waited for: 11 -> 11; matrix products, arithmetic and copies ran while one was open for 1% -> 1% of each run, Pallas kernels for 4% -> 17%
where the time goes in v5:
time: 114 us; the launch traced here: 113 us
  waiting for transfers between devices  51.5 us (45%)
  Pallas kernels  28.9 us (25%)
  starting transfers between devices  24.3 us (21%)
  local copies, waits for them, and re-layouts  5.47 us (5%)
  between operations  2.17 us (2%)
    ppermute x12, waiting for transfers between devices, swap(): return lax.ppermute(value, axis, [(i, i ^ bit) for i in range(count)])  51.4 us
    ppermute x12, starting transfers between devices, swap(): return lax.ppermute(value, axis, [(i, i ^ bit) for i in range(count)])  22.6 us
    pallas_call x1, Pallas kernels, local(): pl.pallas_call(functools.partial(inner_kernel, peers, work), in_specs=[sm...  16.1 us
    pallas_call x1, Pallas kernels, local(): pl.pallas_call(functools.partial(border_kernel, peers, work, parts), in_s...  8.29 us
    unnamed x20, local copies, waits for them, and re-layouts  4.68 us
    pallas_call x1, Pallas kernels, border_strips(): pl.pallas_call(strip_kernel, in_specs=[spec], out_specs=[spec] * 3, out_s...  3.09 us
  transfers between devices with their start and end apart: 13, of which 11 were waited for; matrix products, arithmetic and copies ran while one was open for 1% of the time, Pallas kernels for 17%

profile of v5, /device:TPU:0, one launch (start us, length us, event | category | flops | bytes accessed | tf_op | source)
XLA Modules:
  0.0 113.1 jit_solution(7193761214810456821)
XLA Ops:
  0.6 0.0 copy-start.6
  0.6 0.0 copy-start.9
  0.7 0.0 copy-start.8
  1.3 0.7 pad_bitcast_fusion
  2.1 3.0 %collective-permute-start = (f32[1,40,128]{2,1,0:T(8,128)S(1)}, f32[1,40,128]{2,1,0:T(8,128)S(1)}, u32[]{:S(2)}, u32[]{:S(2)}) collective-permute-start(f32[1,40,128]{2,1,0:T(8,128)S(1)} %pad_bitcast_fusion), channel_id=1, source_target_pairs={{0,1},{1,0},{2,3},{3,2},{4,5},{5,4},{6,7},{7,6},{8,9},{9,8},{10,11... | collective-permute-start | bytes 61448 | tf_op jit(solution)/shard_map/ppermute | solution.py:29
  5.0 0.0 copy-start
  5.0 2.2 %copy-done = bf16[1,64,16,16,128]{4,3,2,1,0:T(8,128)(2,1)S(1)} copy-done((bf16[1,64,16,16,128]{4,3,2,1,0:T(8,128)(2,1)S(1)}, bf16[1,64,16,16,128]{4,3,2,1,0:T(8,128)(2,1)}, u32[]{:S(2)}) %copy-start) | copy-done | bytes 4194328
  7.2 3.1 %shard_map.137 = (bf16[64,4,16,128]{3,2,1,0:T(8,128)(2,1)S(1)}, bf16[64,4,16,128]{3,2,1,0:T(8,128)(2,1)S(1)}, f32[64,128]{1,0:T(8,128)S(1)}) custom-call(bf16[64,16,16,128]{3,2,1,0:T(8,128)(2,1)S(1)} %bitcast.52), custom_call_target="tpu_custom_call" | custom-call | flops 1000000000 | bytes 10000000 | tf_op jit(solution)/shard_map/pallas_call | solution.py:65
  10.3 0.0 collective-permute-done
  10.3 1.6 %collective-permute-start.1 = (f32[2,40,128]{2,1,0:T(8,128)S(1)}, f32[2,40,128]{2,1,0:T(8,128)S(1)}, u32[]{:S(2)}, u32[]{:S(2)}) collective-permute-start(f32[2,40,128]{2,1,0:T(8,128)S(1)} %pad_maximum_fusion.6), channel_id=1, source_target_pairs={{0,2},{1,3},{2,0},{3,1},{4,6},{5,7},{6,4},{7,5},{8,10},{9,11},{10,... | collective-permute-start | bytes 122888 | tf_op jit(solution)/shard_map/ppermute | solution.py:29
  12.0 2.4 %collective-permute-done.1 = f32[2,40,128]{2,1,0:T(8,128)S(1)} collective-permute-done((f32[2,40,128]{2,1,0:T(8,128)S(1)}, f32[2,40,128]{2,1,0:T(8,128)S(1)}, u32[]{:S(2)}, u32[]{:S(2)}) %collective-permute-start.1) | collective-permute-done | bytes 40992 | tf_op jit(solution)/shard_map/ppermute | solution.py:29
  14.4 2.6 %collective-permute-start.2 = (f32[4,40,128]{2,1,0:T(8,128)S(1)}, f32[4,40,128]{2,1,0:T(8,128)S(1)}, u32[]{:S(2)}, u32[]{:S(2)}) collective-permute-start(f32[4,40,128]{2,1,0:T(8,128)S(1)} %pad_maximum_fusion.5), channel_id=1, source_target_pairs={{0,4},{1,5},{2,6},{3,7},{4,0},{5,1},{6,2},{7,3},{8,12},{9,13},{10,... | collective-permute-start | bytes 245768 | tf_op jit(solution)/shard_map/ppermute | solution.py:29
  17.0 0.5 collective-permute-start.3
  17.5 2.2 %collective-permute-done.2 = f32[4,40,128]{2,1,0:T(8,128)S(1)} collective-permute-done((f32[4,40,128]{2,1,0:T(8,128)S(1)}, f32[4,40,128]{2,1,0:T(8,128)S(1)}, u32[]{:S(2)}, u32[]{:S(2)}) %collective-permute-start.2) | collective-permute-done | bytes 81952 | tf_op jit(solution)/shard_map/ppermute | solution.py:29
  19.7 0.6 copy-done.4
  20.4 1.7 %collective-permute-start.4 = (bf16[64,4,16,128]{3,2,1,0:T(8,128)(2,1)S(1)}, bf16[64,4,16,128]{3,2,1,0:T(8,128)(2,1)}, u32[]{:S(2)}, u32[]{:S(2)}) collective-permute-start(bf16[64,4,16,128]{3,2,1,0:T(8,128)(2,1)S(1)} %get-tuple-element.31.own), channel_id=1, source_target_pairs={{1,2},{3,4},{5,6},{2,1},{4,3},{6,5},{9,10},{11,12},{13,14},{10,9},... | collective-permute-start | bytes 3145736 | tf_op jit(solution)/shard_map/ppermute | solution.py:463
  22.7 0.1 pad_add_fusion.meta
  22.8 0.0 copy-done.6
  22.8 0.0 copy-done.9
  22.8 0.0 copy-done.8
  22.8 0.0 copy-done.1
  22.8 0.0 copy-done.2
  22.8 0.0 copy-start.5
  22.8 0.9 copy-done.5
  23.7 16.1 %shard_map.138 = (f32[64,512]{1,0:T(8,128)S(1)}, f32[64,128]{1,0:T(8,128)S(1)}, f32[64,512]{1,0:T(8,128)S(1)}, f32[72,128]{1,0:T(8,128)S(1)}, f32[8,128]{1,0:T(8...) custom-call(s32[4]{0:T(128)S(1)} %pad_add_fusion.meta, s32[8]{0:T(128)S(1)} %bitcast.57, ...), custom_call_target="tpu_custom_call" | custom-call | tf_op jit(solution)/shard_map/pallas_call | solution.py:478
  39.8 20.9 %collective-permute-done.3.halo_pair = bf16[64,4,16,128]{3,2,1,0:T(8,128)(2,1)S(1)} collective-permute-done((bf16[64,4,16,128]{3,2,1,0:T(8,128)(2,1)S(1)}, bf16[64,4,16,128]{3,2,1,0:T(8,128)(2,1)S(1)}, u32[]{:S(2)}, u32[]{:S(2)}) %collective-permute-start.3) | collective-permute-done | bytes 1048608 | tf_op jit(solution)/shard_map/ppermute | solution.py:29
  60.7 0.0 collective-permute-done.4.halo_cross
  60.7 0.0 copy-done.7
  60.7 0.9 copy-done.3
  61.6 8.3 %shard_map.139 = (f32[256,128]{1,0:T(8,128)S(1)}, f32[8,136,128]{2,1,0:T(8,128)S(1)}) custom-call(s32[4]{0:T(128)S(1)} %pad_add_fusion.meta, s32[1]{0:T(128)} %get-tuple-element.30.begin_in, s32[8]{0:T(128)S(1)} %bitcast.58, s32[8,64]{1,0:T(8,128)S(1)} %bitcast.56, bf16[64,4,16,128]{3,2,1,0:T(8,128)(2,1)S(1)} %get-tuple-element.31.own, ...), custom_call_target="tpu_custom_call" | custom-call | tf_op jit(solution)/shard_map/pallas_call | solution.py:512
  70.0 3.1 %collective-permute-start.5 = (f32[4,136,128]{2,1,0:T(8,128)S(1)}, f32[4,136,128]{2,1,0:T(8,128)S(1)}, u32[]{:S(2)}, u32[]{:S(2)}) collective-permute-start(f32[4,136,128]{2,1,0:T(8,128)S(1)} %slice.57), channel_id=1, source_target_pairs={{0,8},{8,0},{16,24},{24,16},{1,9},{9,1},{17,25},{25,17},{2,10},{10... | collective-permute-start | bytes 835592 | tf_op jit(solution)/shard_map/ppermute | solution.py:29
  73.1 1.2 %collective-permute-done.5 = f32[4,136,128]{2,1,0:T(8,128)S(1)} collective-permute-done((f32[4,136,128]{2,1,0:T(8,128)S(1)}, f32[4,136,128]{2,1,0:T(8,128)S(1)}, u32[]{:S(2)}, u32[]{:S(2)}) %collective-permute-start.5) | collective-permute-done | bytes 278560 | tf_op jit(solution)/shard_map/ppermute | solution.py:29
  74.3 1.7 %collective-permute-start.6 = (f32[2,136,128]{2,1,0:T(8,128)S(1)}, f32[2,136,128]{2,1,0:T(8,128)S(1)}, u32[]{:S(2)}, u32[]{:S(2)}) collective-permute-start(f32[2,136,128]{2,1,0:T(8,128)S(1)} %slice.75), channel_id=1, source_target_pairs={{0,16},{8,24},{16,0},{24,8},{1,17},{9,25},{17,1},{25,9},{2,18},{10... | collective-permute-start | bytes 417800 | tf_op jit(solution)/shard_map/ppermute | solution.py:29
  76.1 4.3 %collective-permute-done.6 = f32[2,136,128]{2,1,0:T(8,128)S(1)} collective-permute-done((f32[2,136,128]{2,1,0:T(8,128)S(1)}, f32[2,136,128]{2,1,0:T(8,128)S(1)}, u32[]{:S(2)}, u32[]{:S(2)}) %collective-permute-start.6) | collective-permute-done | bytes 139296 | tf_op jit(solution)/shard_map/ppermute | solution.py:29
  80.4 2.5 %collective-permute-start.7 = (f32[264,128]{1,0:T(8,128)S(1)}, f32[264,128]{1,0:T(8,128)S(1)}, u32[]{:S(2)}, u32[]{:S(2)}) collective-permute-start(f32[264,128]{1,0:T(8,128)S(1)} %pad_maximum_fusion.2), channel_id=1, source_target_pairs={{0,1},{1,0},{2,3},{3,2},{4,5},{5,4},{6,7},{7,6},{8,9},{9,8},{10,11... | collective-permute-start | bytes 405512 | tf_op jit(solution)/shard_map/ppermute | solution.py:29
  82.9 3.2 %collective-permute-done.7 = f32[264,128]{1,0:T(8,128)S(1)} collective-permute-done((f32[264,128]{1,0:T(8,128)S(1)}, f32[264,128]{1,0:T(8,128)S(1)}, u32[]{:S(2)}, u32[]{:S(2)}) %collective-permute-start.7) | collective-permute-done | bytes 135200 | tf_op jit(solution)/shard_map/ppermute | solution.py:29
  86.2 5.7 %collective-permute-start.8 = (f32[200,128]{1,0:T(8,128)S(1)}, f32[200,128]{1,0:T(8,128)S(1)}, u32[]{:S(2)}, u32[]{:S(2)}) collective-permute-start(f32[200,128]{1,0:T(8,128)S(1)} %pad_maximum_fusion.3), channel_id=1, source_target_pairs={{0,2},{1,3},{2,0},{3,1},{4,6},{5,7},{6,4},{7,5},{8,10},{9,11},{10,... | collective-permute-start | bytes 307208 | tf_op jit(solution)/shard_map/ppermute | solution.py:29
  92.0 3.0 %collective-permute-done.8 = f32[200,128]{1,0:T(8,128)S(1)} collective-permute-done((f32[200,128]{1,0:T(8,128)S(1)}, f32[200,128]{1,0:T(8,128)S(1)}, u32[]{:S(2)}, u32[]{:S(2)}) %collective-permute-start.8) | collective-permute-done | bytes 102432 | tf_op jit(solution)/shard_map/ppermute | solution.py:29
  95.1 0.1 collective-permute-start.9
  95.1 5.4 %collective-permute-done.9 = f32[168,128]{1,0:T(8,128)S(1)} collective-permute-done((f32[168,128]{1,0:T(8,128)S(1)}, f32[168,128]{1,0:T(8,128)S(1)}, u32[]{:S(2)}, u32[]{:S(2)}) %collective-permute-start.9) | collective-permute-done | bytes 86048 | tf_op jit(solution)/shard_map/ppermute | solution.py:29
  100.5 0.3 collective-permute-start.10
  100.8 4.0 %collective-permute-done.10 = f32[1,136,128]{2,1,0:T(8,128)S(1)} collective-permute-done((f32[1,136,128]{2,1,0:T(8,128)S(1)}, f32[1,136,128]{2,1,0:T(8,128)S(1)}, u32[]{:S(2)}, u32[]{:S(2)}) %collective-permute-start.10) | collective-permute-done | bytes 69664 | tf_op jit(solution)/shard_map/ppermute | solution.py:29
  104.9 1.3 %collective-permute-start.11 = (f32[2,136,128]{2,1,0:T(8,128)S(1)}, f32[2,136,128]{2,1,0:T(8,128)S(1)}, u32[]{:S(2)}, u32[]{:S(2)}) collective-permute-start(f32[2,136,128]{2,1,0:T(8,128)S(1)} %pad_maximum_fusion.1), channel_id=1, source_target_pairs={{0,16},{8,24},{16,0},{24,8},{1,17},{9,25},{17,1},{25,9},{2,18},{10... | collective-permute-start | bytes 417800 | tf_op jit(solution)/shard_map/ppermute | solution.py:29
  106.2 3.8 %collective-permute-done.11 = f32[2,136,128]{2,1,0:T(8,128)S(1)} collective-permute-done((f32[2,136,128]{2,1,0:T(8,128)S(1)}, f32[2,136,128]{2,1,0:T(8,128)S(1)}, u32[]{:S(2)}, u32[]{:S(2)}) %collective-permute-start.11) | collective-permute-done | bytes 139296 | tf_op jit(solution)/shard_map/ppermute | solution.py:29
  110.1 0.1 collective-permute-start.12
  110.1 0.6 fusion.2
  110.7 0.9 collective-permute-done.12.far
  111.7 1.4 %shard_map.140 = (f32[9,128]{1,0:T(8,128)}, f32[1,128]{1,0:T(1,128)}, f32[128,512]{1,0:T(8,128)}, f32[512,128]{1,0:T(8,128)}) custom-call(s32[4]{0:T(128)S(1)} %pad_add_fusion.meta, f32[4,136,128]{2,1,0:T(8,128)S(1)} %pad_maximum_fusion.near, f32[4,136,128]{2,1,0:T(8,128)S(1)} %collective-permute-done.12.far), custom_call_target="tpu_custom_call" | custom-call | tf_op jit(solution)/shard_map/pallas_call | solution.py:571
  (27 shorter events, 0.3 us)
Async XLA Ops:
  0.6 22.2 %copy-start.6 = (bf16[9,128]{1,0:T(8,128)(2,1)S(1)}, bf16[9,128]{1,0:T(8,128)(2,1)}, u32[]{:S(2)}) copy-start(bf16[9,128]{1,0:T(8,128)(2,1)} %kern.3) | copy-start | bytes 6916
  0.6 22.1 %copy-start.9 = (f32[128]{0:T(128)S(1)}, f32[128]{0:T(128)}, u32[]{:S(2)}) copy-start(f32[128]{0:T(128)} %param.16) | copy-start | bytes 1540
  0.7 22.1 %copy-start.8 = (s32[1,8]{1,0:T(1,128)S(1)}, s32[1,8]{1,0:T(1,128)}, u32[]{:S(2)}) copy-start(s32[1,8]{1,0:T(1,128)} %param.13) | copy-start | bytes 100
  2.1 8.3 %collective-permute-start = (f32[1,40,128]{2,1,0:T(8,128)S(1)}, f32[1,40,128]{2,1,0:T(8,128)S(1)}, u32[]{:S(2)}, u32[]{:S(2)}) collective-permute-start(f32[1,40,128]{2,1,0:T(8,128)S(1)} %pad_bitcast_fusion), channel_id=1, source_target_pairs={{0,1},{1,0},{2,3},{3,2},{4,5},{5,4},{6,7},{7,6},{8,9},{9,8},{10,11... | collective-permute-start | bytes 61448 | tf_op jit(solution)/shard_map/ppermute | solution.py:29
  5.0 2.2 %copy-start = (bf16[1,64,16,16,128]{4,3,2,1,0:T(8,128)(2,1)S(1)}, bf16[1,64,16,16,128]{4,3,2,1,0:T(8,128)(2,1)}, u32[]{:S(2)}) copy-start(bf16[1,64,16,16,128]{4,3,2,1,0:T(8,128)(2,1)} %param.10) | copy-start | bytes 12582916
  7.2 15.6 %copy-start.1 = (bf16[128,512]{1,0:T(8,128)(2,1)S(1)}, bf16[128,512]{1,0:T(8,128)(2,1)}, u32[]{:S(2)}) copy-start(bf16[128,512]{1,0:T(8,128)(2,1)} %w_in.3) | copy-start | bytes 393220
  7.2 15.6 %copy-start.2 = (bf16[512,128]{1,0:T(8,128)(2,1)S(1)}, bf16[512,128]{1,0:T(8,128)(2,1)}, u32[]{:S(2)}) copy-start(bf16[512,128]{1,0:T(8,128)(2,1)} %w_out.1) | copy-start | bytes 393220
  7.2 53.5 %copy-start.7 = (s32[1,64,8]{1,2,0:T(8,128)S(1)}, s32[1,64,8]{1,2,0:T(8,128)}, u32[]{:S(2)}) copy-start(s32[1,64,8]{1,2,0:T(8,128)} %param.12) | copy-start | bytes 6148
  10.3 4.1 %collective-permute-start.1 = (f32[2,40,128]{2,1,0:T(8,128)S(1)}, f32[2,40,128]{2,1,0:T(8,128)S(1)}, u32[]{:S(2)}, u32[]{:S(2)}) collective-permute-start(f32[2,40,128]{2,1,0:T(8,128)S(1)} %pad_maximum_fusion.6), channel_id=1, source_target_pairs={{0,2},{1,3},{2,0},{3,1},{4,6},{5,7},{6,4},{7,5},{8,10},{9,11},{10,... | collective-permute-start | bytes 122888 | tf_op jit(solution)/shard_map/ppermute | solution.py:29
  14.4 5.3 %collective-permute-start.2 = (f32[4,40,128]{2,1,0:T(8,128)S(1)}, f32[4,40,128]{2,1,0:T(8,128)S(1)}, u32[]{:S(2)}, u32[]{:S(2)}) collective-permute-start(f32[4,40,128]{2,1,0:T(8,128)S(1)} %pad_maximum_fusion.5), channel_id=1, source_target_pairs={{0,4},{1,5},{2,6},{3,7},{4,0},{5,1},{6,2},{7,3},{8,12},{9,13},{10,... | collective-permute-start | bytes 245768 | tf_op jit(solution)/shard_map/ppermute | solution.py:29
  17.0 43.7 %collective-permute-start.3 = (bf16[64,4,16,128]{3,2,1,0:T(8,128)(2,1)S(1)}, bf16[64,4,16,128]{3,2,1,0:T(8,128)(2,1)S(1)}, u32[]{:S(2)}, u32[]{:S(2)}) collective-permute-start(bf16[64,4,16,128]{3,2,1,0:T(8,128)(2,1)S(1)} %get-tuple-element.31.own), channel_id=1, source_target_pairs={{0,1},{1,0},{2,3},{3,2},{4,5},{5,4},{6,7},{7,6},{8,9},{9,8},{10,11... | collective-permute-start | bytes 3145736 | tf_op jit(solution)/shard_map/ppermute | solution.py:29
  19.7 0.6 copy-start.4
  20.4 40.3 %collective-permute-start.4 = (bf16[64,4,16,128]{3,2,1,0:T(8,128)(2,1)S(1)}, bf16[64,4,16,128]{3,2,1,0:T(8,128)(2,1)}, u32[]{:S(2)}, u32[]{:S(2)}) collective-permute-start(bf16[64,4,16,128]{3,2,1,0:T(8,128)(2,1)S(1)} %get-tuple-element.31.own), channel_id=1, source_target_pairs={{1,2},{3,4},{5,6},{2,1},{4,3},{6,5},{9,10},{11,12},{13,14},{10,9},... | collective-permute-start | bytes 3145736 | tf_op jit(solution)/shard_map/ppermute | solution.py:463
  22.8 0.9 copy-start.5
  60.7 1.0 copy-start.3
  70.0 4.3 %collective-permute-start.5 = (f32[4,136,128]{2,1,0:T(8,128)S(1)}, f32[4,136,128]{2,1,0:T(8,128)S(1)}, u32[]{:S(2)}, u32[]{:S(2)}) collective-permute-start(f32[4,136,128]{2,1,0:T(8,128)S(1)} %slice.57), channel_id=1, source_target_pairs={{0,8},{8,0},{16,24},{24,16},{1,9},{9,1},{17,25},{25,17},{2,10},{10... | collective-permute-start | bytes 835592 | tf_op jit(solution)/shard_map/ppermute | solution.py:29
  74.3 6.0 %collective-permute-start.6 = (f32[2,136,128]{2,1,0:T(8,128)S(1)}, f32[2,136,128]{2,1,0:T(8,128)S(1)}, u32[]{:S(2)}, u32[]{:S(2)}) collective-permute-start(f32[2,136,128]{2,1,0:T(8,128)S(1)} %slice.75), channel_id=1, source_target_pairs={{0,16},{8,24},{16,0},{24,8},{1,17},{9,25},{17,1},{25,9},{2,18},{10... | collective-permute-start | bytes 417800 | tf_op jit(solution)/shard_map/ppermute | solution.py:29
  80.4 5.7 %collective-permute-start.7 = (f32[264,128]{1,0:T(8,128)S(1)}, f32[264,128]{1,0:T(8,128)S(1)}, u32[]{:S(2)}, u32[]{:S(2)}) collective-permute-start(f32[264,128]{1,0:T(8,128)S(1)} %pad_maximum_fusion.2), channel_id=1, source_target_pairs={{0,1},{1,0},{2,3},{3,2},{4,5},{5,4},{6,7},{7,6},{8,9},{9,8},{10,11... | collective-permute-start | bytes 405512 | tf_op jit(solution)/shard_map/ppermute | solution.py:29
  86.2 8.8 %collective-permute-start.8 = (f32[200,128]{1,0:T(8,128)S(1)}, f32[200,128]{1,0:T(8,128)S(1)}, u32[]{:S(2)}, u32[]{:S(2)}) collective-permute-start(f32[200,128]{1,0:T(8,128)S(1)} %pad_maximum_fusion.3), channel_id=1, source_target_pairs={{0,2},{1,3},{2,0},{3,1},{4,6},{5,7},{6,4},{7,5},{8,10},{9,11},{10,... | collective-permute-start | bytes 307208 | tf_op jit(solution)/shard_map/ppermute | solution.py:29
  95.1 5.4 %collective-permute-start.9 = (f32[168,128]{1,0:T(8,128)S(1)}, f32[168,128]{1,0:T(8,128)S(1)}, u32[]{:S(2)}, u32[]{:S(2)}) collective-permute-start(f32[168,128]{1,0:T(8,128)S(1)} %pad_maximum_fusion.4), channel_id=1, source_target_pairs={{0,4},{1,5},{2,6},{3,7},{4,0},{5,1},{6,2},{7,3},{8,12},{9,13},{10,... | collective-permute-start | bytes 258056 | tf_op jit(solution)/shard_map/ppermute | solution.py:29
  100.5 4.4 %collective-permute-start.10 = (f32[1,136,128]{2,1,0:T(8,128)S(1)}, f32[1,136,128]{2,1,0:T(8,128)S(1)}, u32[]{:S(2)}, u32[]{:S(2)}) collective-permute-start(f32[1,136,128]{2,1,0:T(8,128)S(1)} %fusion), channel_id=1, source_target_pairs={{0,1},{1,0},{2,3},{3,2},{4,5},{5,4},{6,7},{7,6},{8,9},{9,8},{10,11... | collective-permute-start | bytes 208904 | tf_op jit(solution)/shard_map/ppermute | solution.py:29
  104.9 5.1 %collective-permute-start.11 = (f32[2,136,128]{2,1,0:T(8,128)S(1)}, f32[2,136,128]{2,1,0:T(8,128)S(1)}, u32[]{:S(2)}, u32[]{:S(2)}) collective-permute-start(f32[2,136,128]{2,1,0:T(8,128)S(1)} %pad_maximum_fusion.1), channel_id=1, source_target_pairs={{0,16},{8,24},{16,0},{24,8},{1,17},{9,25},{17,1},{25,9},{2,18},{10... | collective-permute-start | bytes 417800 | tf_op jit(solution)/shard_map/ppermute | solution.py:29
  110.1 1.6 %collective-permute-start.12 = (f32[4,136,128]{2,1,0:T(8,128)S(1)}, f32[4,136,128]{2,1,0:T(8,128)S(1)}, u32[]{:S(2)}, u32[]{:S(2)}) collective-permute-start(f32[4,136,128]{2,1,0:T(8,128)S(1)} %pad_maximum_fusion.near), channel_id=1, source_target_pairs={{0,8},{8,0},{16,24},{24,16},{1,9},{9,1},{17,25},{25,17},{2,10},{10... | collective-permute-start | bytes 835592 | tf_op jit(solution)/shard_map/ppermute | solution.py:29

commit v6 on v5

--- a/solution.py
+++ b/solution.py
@@ -15,9 +15,10 @@
 INNER_TILES = 4
 BORDER_TILES = 16
 SMALL_ROWS = 8
-STRIP_TILES = 4
+STRIP_TILES = 8
 VMEM_BYTES = 32 * 1024 * 1024
-INNER_BYTES = 53 * 1024 * 1024
+STRIP_BYTES = 54 * 1024 * 1024
+INNER_BYTES = 48 * 1024 * 1024
 
 
 def bits_of(count):
@@ -29,8 +30,8 @@
     return lax.ppermute(value, axis, [(i, i ^ bit) for i in range(count)])
 
 
-def strip_kernel(tiles, strips, inner, csum):
-    slots, side, _, chans = tiles.shape
+def strip_kernel(tiles_hbm, strips, inner, csum, tiles, sems):
+    slots, side, _, chans = tiles_hbm.shape
     columns = (0, side - 1, 1, side - 2)
     rows = (len(columns) + 1) * side
     row = lax.broadcasted_iota(jnp.int32, (rows, side * side), 0)
@@ -40,8 +41,17 @@
     picked = (pixel == (row - group * side) * side + column) | (group == len(columns))
     select = jnp.where(picked, 1.0, 0.0).astype(jnp.bfloat16)
 
+    def tiles_copy(step):
+        taken = pl.ds(step * STRIP_TILES, STRIP_TILES)
+        return pltpu.make_async_copy(tiles_hbm.at[taken], tiles.at[taken], sems.at[step])
+
     @pl.loop(0, slots // STRIP_TILES)
     def _(step):
+        tiles_copy(step).start()
+
+    @pl.loop(0, slots // STRIP_TILES)
+    def _(step):
+        tiles_copy(step).wait()
         for part in range(STRIP_TILES):
             slot = step * STRIP_TILES + part
             tile = tiles[slot].reshape(side * side, chans)
@@ -64,11 +74,14 @@
     spec = pl.BlockSpec(memory_space=pltpu.VMEM)
     return pl.pallas_call(
         strip_kernel,
-        in_specs=[spec],
+        in_specs=[pl.BlockSpec(memory_space=pltpu.HBM)],
         out_specs=[spec] * 3,
         out_shape=[shape, shape, jax.ShapeDtypeStruct((slots, chans), jnp.float32)],
-        compiler_params=pltpu.CompilerParams(vmem_limit_bytes=VMEM_BYTES),
-        cost_estimate=pl.CostEstimate(flops=10**9, bytes_accessed=10**7, transcendentals=0),
+        scratch_shapes=[
+            pltpu.VMEM(tiles.shape, jnp.bfloat16),
+            pltpu.SemaphoreType.DMA((slots // STRIP_TILES,)),
+        ],
+        compiler_params=pltpu.CompilerParams(vmem_limit_bytes=STRIP_BYTES),
     )(tiles)
 
 
@@ -454,8 +467,8 @@
     for bit in tile_bits:
         arrived = swap(gathered, "tile", bit)
         if bit == tile_bits[0]:
+            halo_pair = swap(strips, "tile", 1)
             arrived, strips = lax.optimization_barrier((arrived, strips))
-            halo_pair = swap(strips, "tile", 1)
         if bit < tile_bits[-1]:
             gathered = jnp.concatenate([gathered, arrived], axis=0)
     arrived, strips = lax.optimization_barrier((arrived, strips))

time: 114 us -> 111 us (0.974)
  Pallas kernels: 28.9 us -> 9.8 us
  waiting for transfers between devices: 51.5 us -> 61.6 us
  starting transfers between devices: 24.3 us -> 31.8 us
  local copies, waits for them, and re-layouts: 5.47 us -> 3.01 us
    pallas_call x1, Pallas kernels: 16.1 us -> 2.08 us  [local(): pl.pallas_call(functools.partial(inner_kernel, peers, work), in_specs=[sm...]
    ppermute x12, waiting for transfers between devices: 51.4 us -> 61.6 us  [swap(): return lax.ppermute(value, axis, [(i, i ^ bit) for i in range(count)])]
    ppermute x12, starting transfers between devices: 22.6 us -> 31.1 us  [swap(): return lax.ppermute(value, axis, [(i, i ^ bit) for i in range(count)])]
    pallas_call x1, Pallas kernels: 8.29 us -> 1.91 us  [local(): pl.pallas_call(functools.partial(border_kernel, peers, work, parts), in_s...]
    unnamed x20, local copies, waits for them, and re-layouts: 4.68 us -> 2.22 us
    pallas_call x1, Pallas kernels: 3.09 us -> 4.39 us  [border_strips(): pl.pallas_call(strip_kernel, in_specs=[pl.BlockSpec(memory_space=pltpu.HB...]
  transfers between devices with their start and end apart: 13 -> 13, of which waited for: 11 -> 11; matrix products, arithmetic and copies ran while one was open for 1% -> 1% of each run, Pallas kernels for 17% -> 6%
where the time goes in v6:
time: 111 us; the launch traced here: 109 us
  waiting for transfers between devices  61.6 us (55%)
  starting transfers between devices  31.8 us (29%)
  Pallas kernels  9.8 us (9%)
  local copies, waits for them, and re-layouts  3.01 us (3%)
  between operations  2.25 us (2%)
    ppermute x12, waiting for transfers between devices, swap(): return lax.ppermute(value, axis, [(i, i ^ bit) for i in range(count)])  61.6 us
    ppermute x12, starting transfers between devices, swap(): return lax.ppermute(value, axis, [(i, i ^ bit) for i in range(count)])  31.1 us
    pallas_call x1, Pallas kernels, border_strips(): pl.pallas_call(strip_kernel, in_specs=[pl.BlockSpec(memory_space=pltpu.HB...  4.39 us
    unnamed x20, local copies, waits for them, and re-layouts  2.22 us
  transfers between devices with their start and end apart: 13, of which 11 were waited for; matrix products, arithmetic and copies ran while one was open for 1% of the time, Pallas kernels for 6%

profile of v6, /device:TPU:0, one launch (start us, length us, event | category | flops | bytes accessed | tf_op | source)
XLA Modules:
  0.0 109.4 jit_solution(8228633790102170819)
XLA Ops:
  0.6 0.0 copy-start.4
  0.6 0.0 copy-start.3
  0.7 0.0 copy-start.6
  0.7 0.0 copy-start.9
  0.7 0.0 copy-start.8
  1.4 0.7 pad_bitcast_fusion
  2.1 3.0 %collective-permute-start = (f32[1,40,128]{2,1,0:T(8,128)S(1)}, f32[1,40,128]{2,1,0:T(8,128)S(1)}, u32[]{:S(2)}, u32[]{:S(2)}) collective-permute-start(f32[1,40,128]{2,1,0:T(8,128)S(1)} %pad_bitcast_fusion), channel_id=1, source_target_pairs={{0,1},{1,0},{2,3},{3,2},{4,5},{5,4},{6,7},{7,6},{8,9},{9,8},{10,11... | collective-permute-start | bytes 61448 | tf_op jit(solution)/shard_map/ppermute | solution.py:30
  5.1 4.4 %shard_map.137 = (bf16[64,4,16,128]{3,2,1,0:T(8,128)(2,1)}, bf16[64,4,16,128]{3,2,1,0:T(8,128)(2,1)}, f32[64,128]{1,0:T(8,128)}) custom-call(bf16[64,16,16,128]{3,2,1,0:T(8,128)(2,1)} %bitcast.51), custom_call_target="tpu_custom_call" | custom-call | tf_op jit(solution)/shard_map/pallas_call | solution.py:75
  9.5 0.0 copy-start.5
  9.5 0.0 collective-permute-done
  9.5 1.6 %collective-permute-start.1 = (f32[2,40,128]{2,1,0:T(8,128)S(1)}, f32[2,40,128]{2,1,0:T(8,128)S(1)}, u32[]{:S(2)}, u32[]{:S(2)}) collective-permute-start(f32[2,40,128]{2,1,0:T(8,128)S(1)} %pad_maximum_fusion.6), channel_id=1, source_target_pairs={{0,2},{1,3},{2,0},{3,1},{4,6},{5,7},{6,4},{7,5},{8,10},{9,11},{10,... | collective-permute-start | bytes 122888 | tf_op jit(solution)/shard_map/ppermute | solution.py:30
  11.2 2.4 %collective-permute-done.1 = f32[2,40,128]{2,1,0:T(8,128)S(1)} collective-permute-done((f32[2,40,128]{2,1,0:T(8,128)S(1)}, f32[2,40,128]{2,1,0:T(8,128)S(1)}, u32[]{:S(2)}, u32[]{:S(2)}) %collective-permute-start.1) | collective-permute-done | bytes 40992 | tf_op jit(solution)/shard_map/ppermute | solution.py:30
  13.6 2.6 %collective-permute-start.2 = (f32[4,40,128]{2,1,0:T(8,128)S(1)}, f32[4,40,128]{2,1,0:T(8,128)S(1)}, u32[]{:S(2)}, u32[]{:S(2)}) collective-permute-start(f32[4,40,128]{2,1,0:T(8,128)S(1)} %pad_maximum_fusion.5), channel_id=1, source_target_pairs={{0,4},{1,5},{2,6},{3,7},{4,0},{5,1},{6,2},{7,3},{8,12},{9,13},{10,... | collective-permute-start | bytes 245768 | tf_op jit(solution)/shard_map/ppermute | solution.py:30
  16.2 0.5 collective-permute-start.3
  16.7 2.2 %collective-permute-done.2 = f32[4,40,128]{2,1,0:T(8,128)S(1)} collective-permute-done((f32[4,40,128]{2,1,0:T(8,128)S(1)}, f32[4,40,128]{2,1,0:T(8,128)S(1)}, u32[]{:S(2)}, u32[]{:S(2)}) %collective-permute-start.2) | collective-permute-done | bytes 81952 | tf_op jit(solution)/shard_map/ppermute | solution.py:30
  18.9 0.7 collective-permute-start.4
  20.3 0.1 pad_add_fusion.meta
  20.4 0.0 copy-done.4
  20.4 0.0 copy-done.3
  20.4 0.0 copy-done.6
  20.4 0.0 copy-done.9
  20.4 0.0 copy-done.8
  20.4 0.0 copy-start
  20.4 2.2 %copy-done = bf16[1,64,16,16,128]{4,3,2,1,0:T(8,128)(2,1)S(1)} copy-done((bf16[1,64,16,16,128]{4,3,2,1,0:T(8,128)(2,1)S(1)}, bf16[1,64,16,16,128]{4,3,2,1,0:T(8,128)(2,1)}, u32[]{:S(2)}) %copy-start) | copy-done | bytes 4194328
  22.6 2.1 %shard_map.138 = (f32[64,512]{1,0:T(8,128)S(1)}, f32[64,128]{1,0:T(8,128)S(1)}, f32[64,512]{1,0:T(8,128)S(1)}, f32[72,128]{1,0:T(8,128)S(1)}, f32[8,128]{1,0:T(8...) custom-call(s32[4]{0:T(128)S(1)} %pad_add_fusion.meta, s32[8]{0:T(128)S(1)} %bitcast.57, ...), custom_call_target="tpu_custom_call" | custom-call | tf_op jit(solution)/shard_map/pallas_call | solution.py:491
  24.7 35.5 %collective-permute-done.3.halo_pair = bf16[64,4,16,128]{3,2,1,0:T(8,128)(2,1)S(1)} collective-permute-done((bf16[64,4,16,128]{3,2,1,0:T(8,128)(2,1)}, bf16[64,4,16,128]{3,2,1,0:T(8,128)(2,1)S(1)}, u32[]{:S(2)}, u32[]{:S(2)}) %collective-permute-start.3) | collective-permute-done | bytes 1048608 | tf_op jit(solution)/shard_map/ppermute | solution.py:30
  60.2 0.0 collective-permute-done.4.halo_cross
  60.2 0.0 copy-done.7
  60.2 0.0 copy-done.5
  60.2 1.9 %shard_map.139 = (f32[256,128]{1,0:T(8,128)S(1)}, f32[8,136,128]{2,1,0:T(8,128)S(1)}) custom-call(s32[4]{0:T(128)S(1)} %pad_add_fusion.meta, s32[1]{0:T(128)} %get-tuple-element.30.begin_in, s32[8]{0:T(128)S(1)} %bitcast.58, s32[8,64]{1,0:T(8,128)S(1)} %bitcast.56, bf16[64,4,16,128]{3,2,1,0:T(8,128)(2,1)S(1)} %copy-done.1, ...), custom_call_target="tpu_custom_call" | custom-call | tf_op jit(solution)/shard_map/pallas_call | solution.py:525
  62.2 6.0 %collective-permute-start.5 = (f32[4,136,128]{2,1,0:T(8,128)S(1)}, f32[4,136,128]{2,1,0:T(8,128)S(1)}, u32[]{:S(2)}, u32[]{:S(2)}) collective-permute-start(f32[4,136,128]{2,1,0:T(8,128)S(1)} %slice.57), channel_id=1, source_target_pairs={{0,8},{8,0},{16,24},{24,16},{1,9},{9,1},{17,25},{25,17},{2,10},{10... | collective-permute-start | bytes 835592 | tf_op jit(solution)/shard_map/ppermute | solution.py:30
  68.2 1.2 %collective-permute-done.5 = f32[4,136,128]{2,1,0:T(8,128)S(1)} collective-permute-done((f32[4,136,128]{2,1,0:T(8,128)S(1)}, f32[4,136,128]{2,1,0:T(8,128)S(1)}, u32[]{:S(2)}, u32[]{:S(2)}) %collective-permute-start.5) | collective-permute-done | bytes 278560 | tf_op jit(solution)/shard_map/ppermute | solution.py:30
  69.4 4.6 %collective-permute-start.6 = (f32[2,136,128]{2,1,0:T(8,128)S(1)}, f32[2,136,128]{2,1,0:T(8,128)S(1)}, u32[]{:S(2)}, u32[]{:S(2)}) collective-permute-start(f32[2,136,128]{2,1,0:T(8,128)S(1)} %slice.75), channel_id=1, source_target_pairs={{0,16},{8,24},{16,0},{24,8},{1,17},{9,25},{17,1},{25,9},{2,18},{10... | collective-permute-start | bytes 417800 | tf_op jit(solution)/shard_map/ppermute | solution.py:30
  74.0 4.0 %collective-permute-done.6 = f32[2,136,128]{2,1,0:T(8,128)S(1)} collective-permute-done((f32[2,136,128]{2,1,0:T(8,128)S(1)}, f32[2,136,128]{2,1,0:T(8,128)S(1)}, u32[]{:S(2)}, u32[]{:S(2)}) %collective-permute-start.6) | collective-permute-done | bytes 139296 | tf_op jit(solution)/shard_map/ppermute | solution.py:30
  78.0 2.4 %collective-permute-start.7 = (f32[264,128]{1,0:T(8,128)S(1)}, f32[264,128]{1,0:T(8,128)S(1)}, u32[]{:S(2)}, u32[]{:S(2)}) collective-permute-start(f32[264,128]{1,0:T(8,128)S(1)} %pad_maximum_fusion.2), channel_id=1, source_target_pairs={{0,1},{1,0},{2,3},{3,2},{4,5},{5,4},{6,7},{7,6},{8,9},{9,8},{10,11... | collective-permute-start | bytes 405512 | tf_op jit(solution)/shard_map/ppermute | solution.py:30
  80.4 3.5 %collective-permute-done.7 = f32[264,128]{1,0:T(8,128)S(1)} collective-permute-done((f32[264,128]{1,0:T(8,128)S(1)}, f32[264,128]{1,0:T(8,128)S(1)}, u32[]{:S(2)}, u32[]{:S(2)}) %collective-permute-start.7) | collective-permute-done | bytes 135200 | tf_op jit(solution)/shard_map/ppermute | solution.py:30
  84.0 4.6 %collective-permute-start.8 = (f32[200,128]{1,0:T(8,128)S(1)}, f32[200,128]{1,0:T(8,128)S(1)}, u32[]{:S(2)}, u32[]{:S(2)}) collective-permute-start(f32[200,128]{1,0:T(8,128)S(1)} %pad_maximum_fusion.3), channel_id=1, source_target_pairs={{0,2},{1,3},{2,0},{3,1},{4,6},{5,7},{6,4},{7,5},{8,10},{9,11},{10,... | collective-permute-start | bytes 307208 | tf_op jit(solution)/shard_map/ppermute | solution.py:30
  88.6 2.6 %collective-permute-done.8 = f32[200,128]{1,0:T(8,128)S(1)} collective-permute-done((f32[200,128]{1,0:T(8,128)S(1)}, f32[200,128]{1,0:T(8,128)S(1)}, u32[]{:S(2)}, u32[]{:S(2)}) %collective-permute-start.8) | collective-permute-done | bytes 102432 | tf_op jit(solution)/shard_map/ppermute | solution.py:30
  91.3 2.2 %collective-permute-start.9 = (f32[168,128]{1,0:T(8,128)S(1)}, f32[168,128]{1,0:T(8,128)S(1)}, u32[]{:S(2)}, u32[]{:S(2)}) collective-permute-start(f32[168,128]{1,0:T(8,128)S(1)} %pad_maximum_fusion.4), channel_id=1, source_target_pairs={{0,4},{1,5},{2,6},{3,7},{4,0},{5,1},{6,2},{7,3},{8,12},{9,13},{10,... | collective-permute-start | bytes 258056 | tf_op jit(solution)/shard_map/ppermute | solution.py:30
  93.5 3.3 %collective-permute-done.9 = f32[168,128]{1,0:T(8,128)S(1)} collective-permute-done((f32[168,128]{1,0:T(8,128)S(1)}, f32[168,128]{1,0:T(8,128)S(1)}, u32[]{:S(2)}, u32[]{:S(2)}) %collective-permute-start.9) | collective-permute-done | bytes 86048 | tf_op jit(solution)/shard_map/ppermute | solution.py:30
  96.8 1.8 %collective-permute-start.10 = (f32[1,136,128]{2,1,0:T(8,128)S(1)}, f32[1,136,128]{2,1,0:T(8,128)S(1)}, u32[]{:S(2)}, u32[]{:S(2)}) collective-permute-start(f32[1,136,128]{2,1,0:T(8,128)S(1)} %fusion), channel_id=1, source_target_pairs={{0,1},{1,0},{2,3},{3,2},{4,5},{5,4},{6,7},{7,6},{8,9},{9,8},{10,11... | collective-permute-start | bytes 208904 | tf_op jit(solution)/shard_map/ppermute | solution.py:30
  98.6 2.6 %collective-permute-done.10 = f32[1,136,128]{2,1,0:T(8,128)S(1)} collective-permute-done((f32[1,136,128]{2,1,0:T(8,128)S(1)}, f32[1,136,128]{2,1,0:T(8,128)S(1)}, u32[]{:S(2)}, u32[]{:S(2)}) %collective-permute-start.10) | collective-permute-done | bytes 69664 | tf_op jit(solution)/shard_map/ppermute | solution.py:30
  101.2 1.8 %collective-permute-start.11 = (f32[2,136,128]{2,1,0:T(8,128)S(1)}, f32[2,136,128]{2,1,0:T(8,128)S(1)}, u32[]{:S(2)}, u32[]{:S(2)}) collective-permute-start(f32[2,136,128]{2,1,0:T(8,128)S(1)} %pad_maximum_fusion.1), channel_id=1, source_target_pairs={{0,16},{8,24},{16,0},{24,8},{1,17},{9,25},{17,1},{25,9},{2,18},{10... | collective-permute-start | bytes 417800 | tf_op jit(solution)/shard_map/ppermute | solution.py:30
  103.0 3.3 %collective-permute-done.11 = f32[2,136,128]{2,1,0:T(8,128)S(1)} collective-permute-done((f32[2,136,128]{2,1,0:T(8,128)S(1)}, f32[2,136,128]{2,1,0:T(8,128)S(1)}, u32[]{:S(2)}, u32[]{:S(2)}) %collective-permute-start.11) | collective-permute-done | bytes 139296 | tf_op jit(solution)/shard_map/ppermute | solution.py:30
  106.3 0.1 collective-permute-start.12
  106.4 0.6 fusion.2
  107.0 0.9 collective-permute-done.12.far
  107.9 1.4 %shard_map.140 = (f32[9,128]{1,0:T(8,128)}, f32[1,128]{1,0:T(1,128)}, f32[128,512]{1,0:T(8,128)}, f32[512,128]{1,0:T(8,128)}) custom-call(s32[4]{0:T(128)S(1)} %pad_add_fusion.meta, f32[4,136,128]{2,1,0:T(8,128)S(1)} %pad_maximum_fusion.near, f32[4,136,128]{2,1,0:T(8,128)S(1)} %collective-permute-done.12.far), custom_call_target="tpu_custom_call" | custom-call | tf_op jit(solution)/shard_map/pallas_call | solution.py:584
  (27 shorter events, 0.3 us)
Async XLA Ops:
  0.6 19.8 %copy-start.4 = (bf16[512,128]{1,0:T(8,128)(2,1)S(1)}, bf16[512,128]{1,0:T(8,128)(2,1)}, u32[]{:S(2)}) copy-start(bf16[512,128]{1,0:T(8,128)(2,1)} %w_out.1) | copy-start | bytes 393220
  0.6 19.8 %copy-start.3 = (bf16[128,512]{1,0:T(8,128)(2,1)S(1)}, bf16[128,512]{1,0:T(8,128)(2,1)}, u32[]{:S(2)}) copy-start(bf16[128,512]{1,0:T(8,128)(2,1)} %w_in.3) | copy-start | bytes 393220
  0.7 19.8 %copy-start.6 = (bf16[9,128]{1,0:T(8,128)(2,1)S(1)}, bf16[9,128]{1,0:T(8,128)(2,1)}, u32[]{:S(2)}) copy-start(bf16[9,128]{1,0:T(8,128)(2,1)} %kern.3) | copy-start | bytes 6916
  0.7 19.8 %copy-start.9 = (f32[128]{0:T(128)S(1)}, f32[128]{0:T(128)}, u32[]{:S(2)}) copy-start(f32[128]{0:T(128)} %param.16) | copy-start | bytes 1540
  0.7 19.8 %copy-start.8 = (s32[1,8]{1,0:T(1,128)S(1)}, s32[1,8]{1,0:T(1,128)}, u32[]{:S(2)}) copy-start(s32[1,8]{1,0:T(1,128)} %param.13) | copy-start | bytes 100
  2.1 7.4 %collective-permute-start = (f32[1,40,128]{2,1,0:T(8,128)S(1)}, f32[1,40,128]{2,1,0:T(8,128)S(1)}, u32[]{:S(2)}, u32[]{:S(2)}) collective-permute-start(f32[1,40,128]{2,1,0:T(8,128)S(1)} %pad_bitcast_fusion), channel_id=1, source_target_pairs={{0,1},{1,0},{2,3},{3,2},{4,5},{5,4},{6,7},{7,6},{8,9},{9,8},{10,11... | collective-permute-start | bytes 61448 | tf_op jit(solution)/shard_map/ppermute | solution.py:30
  5.1 55.1 %copy-start.7 = (s32[1,64,8]{1,2,0:T(8,128)S(1)}, s32[1,64,8]{1,2,0:T(8,128)}, u32[]{:S(2)}) copy-start(s32[1,64,8]{1,2,0:T(8,128)} %param.12) | copy-start | bytes 6148
  9.5 50.7 %copy-start.5 = (f32[64,128]{1,0:T(8,128)S(1)}, f32[64,128]{1,0:T(8,128)}, u32[]{:S(2)}) copy-start(f32[64,128]{1,0:T(8,128)} %get-tuple-element.35.csum) | copy-start | bytes 98308
  9.5 4.1 %collective-permute-start.1 = (f32[2,40,128]{2,1,0:T(8,128)S(1)}, f32[2,40,128]{2,1,0:T(8,128)S(1)}, u32[]{:S(2)}, u32[]{:S(2)}) collective-permute-start(f32[2,40,128]{2,1,0:T(8,128)S(1)} %pad_maximum_fusion.6), channel_id=1, source_target_pairs={{0,2},{1,3},{2,0},{3,1},{4,6},{5,7},{6,4},{7,5},{8,10},{9,11},{10,... | collective-permute-start | bytes 122888 | tf_op jit(solution)/shard_map/ppermute | solution.py:30
  13.6 5.3 %collective-permute-start.2 = (f32[4,40,128]{2,1,0:T(8,128)S(1)}, f32[4,40,128]{2,1,0:T(8,128)S(1)}, u32[]{:S(2)}, u32[]{:S(2)}) collective-permute-start(f32[4,40,128]{2,1,0:T(8,128)S(1)} %pad_maximum_fusion.5), channel_id=1, source_target_pairs={{0,4},{1,5},{2,6},{3,7},{4,0},{5,1},{6,2},{7,3},{8,12},{9,13},{10,... | collective-permute-start | bytes 245768 | tf_op jit(solution)/shard_map/ppermute | solution.py:30
  16.2 44.0 %collective-permute-start.3 = (bf16[64,4,16,128]{3,2,1,0:T(8,128)(2,1)}, bf16[64,4,16,128]{3,2,1,0:T(8,128)(2,1)S(1)}, u32[]{:S(2)}, u32[]{:S(2)}) collective-permute-start(bf16[64,4,16,128]{3,2,1,0:T(8,128)(2,1)} %get-tuple-element.31.own), channel_id=1, source_target_pairs={{0,1},{1,0},{2,3},{3,2},{4,5},{5,4},{6,7},{7,6},{8,9},{9,8},{10,11... | collective-permute-start | bytes 3145736 | tf_op jit(solution)/shard_map/ppermute | solution.py:30
  18.9 41.3 %collective-permute-start.4 = (bf16[64,4,16,128]{3,2,1,0:T(8,128)(2,1)}, bf16[64,4,16,128]{3,2,1,0:T(8,128)(2,1)S(1)}, u32[]{:S(2)}, u32[]{:S(2)}) collective-permute-start(bf16[64,4,16,128]{3,2,1,0:T(8,128)(2,1)} %get-tuple-element.31.own), channel_id=1, source_target_pairs={{1,2},{3,4},{5,6},{2,1},{4,3},{6,5},{9,10},{11,12},{13,14},{10,9},... | collective-permute-start | bytes 3145736 | tf_op jit(solution)/shard_map/ppermute | solution.py:476
  20.4 2.2 %copy-start = (bf16[1,64,16,16,128]{4,3,2,1,0:T(8,128)(2,1)S(1)}, bf16[1,64,16,16,128]{4,3,2,1,0:T(8,128)(2,1)}, u32[]{:S(2)}) copy-start(bf16[1,64,16,16,128]{4,3,2,1,0:T(8,128)(2,1)} %param.10) | copy-start | bytes 12582916
  22.6 37.6 %copy-start.1 = (bf16[64,4,16,128]{3,2,1,0:T(8,128)(2,1)S(1)}, bf16[64,4,16,128]{3,2,1,0:T(8,128)(2,1)}, u32[]{:S(2)}) copy-start(bf16[64,4,16,128]{3,2,1,0:T(8,128)(2,1)} %get-tuple-element.31.own) | copy-start | bytes 3145732
  22.6 37.6 %copy-start.2 = (bf16[64,4,16,128]{3,2,1,0:T(8,128)(2,1)S(1)}, bf16[64,4,16,128]{3,2,1,0:T(8,128)(2,1)}, u32[]{:S(2)}) copy-start(bf16[64,4,16,128]{3,2,1,0:T(8,128)(2,1)} %get-tuple-element.32.inner) | copy-start | bytes 3145732
  62.2 7.2 %collective-permute-start.5 = (f32[4,136,128]{2,1,0:T(8,128)S(1)}, f32[4,136,128]{2,1,0:T(8,128)S(1)}, u32[]{:S(2)}, u32[]{:S(2)}) collective-permute-start(f32[4,136,128]{2,1,0:T(8,128)S(1)} %slice.57), channel_id=1, source_target_pairs={{0,8},{8,0},{16,24},{24,16},{1,9},{9,1},{17,25},{25,17},{2,10},{10... | collective-permute-start | bytes 835592 | tf_op jit(solution)/shard_map/ppermute | solution.py:30
  69.4 8.6 %collective-permute-start.6 = (f32[2,136,128]{2,1,0:T(8,128)S(1)}, f32[2,136,128]{2,1,0:T(8,128)S(1)}, u32[]{:S(2)}, u32[]{:S(2)}) collective-permute-start(f32[2,136,128]{2,1,0:T(8,128)S(1)} %slice.75), channel_id=1, source_target_pairs={{0,16},{8,24},{16,0},{24,8},{1,17},{9,25},{17,1},{25,9},{2,18},{10... | collective-permute-start | bytes 417800 | tf_op jit(solution)/shard_map/ppermute | solution.py:30
  78.0 5.9 %collective-permute-start.7 = (f32[264,128]{1,0:T(8,128)S(1)}, f32[264,128]{1,0:T(8,128)S(1)}, u32[]{:S(2)}, u32[]{:S(2)}) collective-permute-start(f32[264,128]{1,0:T(8,128)S(1)} %pad_maximum_fusion.2), channel_id=1, source_target_pairs={{0,1},{1,0},{2,3},{3,2},{4,5},{5,4},{6,7},{7,6},{8,9},{9,8},{10,11... | collective-permute-start | bytes 405512 | tf_op jit(solution)/shard_map/ppermute | solution.py:30
  84.0 7.2 %collective-permute-start.8 = (f32[200,128]{1,0:T(8,128)S(1)}, f32[200,128]{1,0:T(8,128)S(1)}, u32[]{:S(2)}, u32[]{:S(2)}) collective-permute-start(f32[200,128]{1,0:T(8,128)S(1)} %pad_maximum_fusion.3), channel_id=1, source_target_pairs={{0,2},{1,3},{2,0},{3,1},{4,6},{5,7},{6,4},{7,5},{8,10},{9,11},{10,... | collective-permute-start | bytes 307208 | tf_op jit(solution)/shard_map/ppermute | solution.py:30
  91.3 5.4 %collective-permute-start.9 = (f32[168,128]{1,0:T(8,128)S(1)}, f32[168,128]{1,0:T(8,128)S(1)}, u32[]{:S(2)}, u32[]{:S(2)}) collective-permute-start(f32[168,128]{1,0:T(8,128)S(1)} %pad_maximum_fusion.4), channel_id=1, source_target_pairs={{0,4},{1,5},{2,6},{3,7},{4,0},{5,1},{6,2},{7,3},{8,12},{9,13},{10,... | collective-permute-start | bytes 258056 | tf_op jit(solution)/shard_map/ppermute | solution.py:30
  96.8 4.4 %collective-permute-start.10 = (f32[1,136,128]{2,1,0:T(8,128)S(1)}, f32[1,136,128]{2,1,0:T(8,128)S(1)}, u32[]{:S(2)}, u32[]{:S(2)}) collective-permute-start(f32[1,136,128]{2,1,0:T(8,128)S(1)} %fusion), channel_id=1, source_target_pairs={{0,1},{1,0},{2,3},{3,2},{4,5},{5,4},{6,7},{7,6},{8,9},{9,8},{10,11... | collective-permute-start | bytes 208904 | tf_op jit(solution)/shard_map/ppermute | solution.py:30
  101.2 5.1 %collective-permute-start.11 = (f32[2,136,128]{2,1,0:T(8,128)S(1)}, f32[2,136,128]{2,1,0:T(8,128)S(1)}, u32[]{:S(2)}, u32[]{:S(2)}) collective-permute-start(f32[2,136,128]{2,1,0:T(8,128)S(1)} %pad_maximum_fusion.1), channel_id=1, source_target_pairs={{0,16},{8,24},{16,0},{24,8},{1,17},{9,25},{17,1},{25,9},{2,18},{10... | collective-permute-start | bytes 417800 | tf_op jit(solution)/shard_map/ppermute | solution.py:30
  106.3 1.6 %collective-permute-start.12 = (f32[4,136,128]{2,1,0:T(8,128)S(1)}, f32[4,136,128]{2,1,0:T(8,128)S(1)}, u32[]{:S(2)}, u32[]{:S(2)}) collective-permute-start(f32[4,136,128]{2,1,0:T(8,128)S(1)} %pad_maximum_fusion.near), channel_id=1, source_target_pairs={{0,8},{8,0},{16,24},{24,16},{1,9},{9,1},{17,25},{25,17},{2,10},{10... | collective-permute-start | bytes 835592 | tf_op jit(solution)/shard_map/ppermute | solution.py:30

commit v7 on v6

--- a/solution.py
+++ b/solution.py
@@ -17,7 +17,7 @@
 SMALL_ROWS = 8
 STRIP_TILES = 8
 VMEM_BYTES = 32 * 1024 * 1024
-STRIP_BYTES = 54 * 1024 * 1024
+STRIP_BYTES = 49 * 1024 * 1024
 INNER_BYTES = 48 * 1024 * 1024
 
 

time: 111 us -> 110 us (level)
  Pallas kernels: 9.8 us -> 41.7 us
  waiting for transfers between devices: 61.6 us -> 39.4 us
  starting transfers between devices: 31.8 us -> 20.5 us
  local copies, waits for them, and re-layouts: 3.01 us -> 4.51 us
    pallas_call x1, Pallas kernels: 2.08 us -> 26 us  [local(): pl.pallas_call(functools.partial(inner_kernel, peers, work), in_specs=[sm...]
    ppermute x12, waiting for transfers between devices: 61.6 us -> 39.4 us  [swap(): return lax.ppermute(value, axis, [(i, i ^ bit) for i in range(count)])]
    ppermute x12, starting transfers between devices: 31.1 us -> 18.8 us  [swap(): return lax.ppermute(value, axis, [(i, i ^ bit) for i in range(count)])]
    pallas_call x1, Pallas kernels: 1.91 us -> 11.2 us  [local(): pl.pallas_call(functools.partial(border_kernel, peers, work, parts), in_s...]
    unnamed x20 -> x18, local copies, waits for them, and re-layouts: 2.22 us -> 3.73 us
    pallas_call x1, Pallas kernels: 4.39 us -> 3.08 us  [border_strips(): pl.pallas_call(strip_kernel, in_specs=[pl.BlockSpec(memory_space=pltpu.HB...]
  transfers between devices with their start and end apart: 13 -> 13, of which waited for: 11 -> 11; matrix products, arithmetic and copies ran while one was open for 1% -> 1% of each run, Pallas kernels for 6% -> 27%
where the time goes in v7:
time: 110 us; the launch traced here: 109 us
  Pallas kernels  41.7 us (38%)
  waiting for transfers between devices  39.4 us (36%)
  starting transfers between devices  20.5 us (19%)
  local copies, waits for them, and re-layouts  4.51 us (4%)
  between operations  2.22 us (2%)
    ppermute x12, waiting for transfers between devices, swap(): return lax.ppermute(value, axis, [(i, i ^ bit) for i in range(count)])  39.4 us
    pallas_call x1, Pallas kernels, local(): pl.pallas_call(functools.partial(inner_kernel, peers, work), in_specs=[sm...  26 us
    ppermute x12, starting transfers between devices, swap(): return lax.ppermute(value, axis, [(i, i ^ bit) for i in range(count)])  18.8 us
    pallas_call x1, Pallas kernels, local(): pl.pallas_call(functools.partial(border_kernel, peers, work, parts), in_s...  11.2 us
    unnamed x18, local copies, waits for them, and re-layouts  3.73 us
    pallas_call x1, Pallas kernels, border_strips(): pl.pallas_call(strip_kernel, in_specs=[pl.BlockSpec(memory_space=pltpu.HB...  3.08 us
  transfers between devices with their start and end apart: 13, of which 11 were waited for; matrix products, arithmetic and copies ran while one was open for 1% of the time, Pallas kernels for 27%

profile of v7, /device:TPU:0, one launch (start us, length us, event | category | flops | bytes accessed | tf_op | source)
XLA Modules:
  0.0 109.2 jit_solution(18115739103620147792)
XLA Ops:
  0.6 0.0 copy-start.2
  0.6 0.0 copy-start.1
  0.7 0.0 copy-start.5
  0.7 0.0 copy-start.8
  0.7 0.0 copy-start.7
  1.4 0.7 pad_bitcast_fusion
  2.1 3.0 %collective-permute-start = (f32[1,40,128]{2,1,0:T(8,128)S(1)}, f32[1,40,128]{2,1,0:T(8,128)S(1)}, u32[]{:S(2)}, u32[]{:S(2)}) collective-permute-start(f32[1,40,128]{2,1,0:T(8,128)S(1)} %pad_bitcast_fusion), channel_id=1, source_target_pairs={{0,1},{1,0},{2,3},{3,2},{4,5},{5,4},{6,7},{7,6},{8,9},{9,8},{10,11... | collective-permute-start | bytes 61448 | tf_op jit(solution)/shard_map/ppermute | solution.py:30
  5.1 3.1 %shard_map.137 = (bf16[64,4,16,128]{3,2,1,0:T(8,128)(2,1)S(1)}, bf16[64,4,16,128]{3,2,1,0:T(8,128)(2,1)S(1)}, f32[64,128]{1,0:T(8,128)S(1)}) custom-call(bf16[64,16,16,128]{3,2,1,0:T(8,128)(2,1)} %bitcast.51), custom_call_target="tpu_custom_call" | custom-call | tf_op jit(solution)/shard_map/pallas_call | solution.py:75
  8.2 0.0 collective-permute-done
  8.2 1.6 %collective-permute-start.1 = (f32[2,40,128]{2,1,0:T(8,128)S(1)}, f32[2,40,128]{2,1,0:T(8,128)S(1)}, u32[]{:S(2)}, u32[]{:S(2)}) collective-permute-start(f32[2,40,128]{2,1,0:T(8,128)S(1)} %pad_maximum_fusion.6), channel_id=1, source_target_pairs={{0,2},{1,3},{2,0},{3,1},{4,6},{5,7},{6,4},{7,5},{8,10},{9,11},{10,... | collective-permute-start | bytes 122888 | tf_op jit(solution)/shard_map/ppermute | solution.py:30
  9.8 2.4 %collective-permute-done.1 = f32[2,40,128]{2,1,0:T(8,128)S(1)} collective-permute-done((f32[2,40,128]{2,1,0:T(8,128)S(1)}, f32[2,40,128]{2,1,0:T(8,128)S(1)}, u32[]{:S(2)}, u32[]{:S(2)}) %collective-permute-start.1) | collective-permute-done | bytes 40992 | tf_op jit(solution)/shard_map/ppermute | solution.py:30
  12.3 2.6 %collective-permute-start.2 = (f32[4,40,128]{2,1,0:T(8,128)S(1)}, f32[4,40,128]{2,1,0:T(8,128)S(1)}, u32[]{:S(2)}, u32[]{:S(2)}) collective-permute-start(f32[4,40,128]{2,1,0:T(8,128)S(1)} %pad_maximum_fusion.5), channel_id=1, source_target_pairs={{0,4},{1,5},{2,6},{3,7},{4,0},{5,1},{6,2},{7,3},{8,12},{9,13},{10,... | collective-permute-start | bytes 245768 | tf_op jit(solution)/shard_map/ppermute | solution.py:30
  14.8 0.6 collective-permute-start.3
  15.5 2.1 %collective-permute-done.2 = f32[4,40,128]{2,1,0:T(8,128)S(1)} collective-permute-done((f32[4,40,128]{2,1,0:T(8,128)S(1)}, f32[4,40,128]{2,1,0:T(8,128)S(1)}, u32[]{:S(2)}, u32[]{:S(2)}) %collective-permute-start.2) | collective-permute-done | bytes 81952 | tf_op jit(solution)/shard_map/ppermute | solution.py:30
  17.6 0.6 copy-done.3
  18.2 1.7 %collective-permute-start.4 = (bf16[64,4,16,128]{3,2,1,0:T(8,128)(2,1)S(1)}, bf16[64,4,16,128]{3,2,1,0:T(8,128)(2,1)}, u32[]{:S(2)}, u32[]{:S(2)}) collective-permute-start(bf16[64,4,16,128]{3,2,1,0:T(8,128)(2,1)S(1)} %get-tuple-element.31.own), channel_id=1, source_target_pairs={{1,2},{3,4},{5,6},{2,1},{4,3},{6,5},{9,10},{11,12},{13,14},{10,9},... | collective-permute-start | bytes 3145736 | tf_op jit(solution)/shard_map/ppermute | solution.py:476
  20.6 0.1 pad_add_fusion.meta
  20.6 0.0 copy-done.2
  20.6 0.0 copy-done.1
  20.7 0.0 copy-done.5
  20.7 0.0 copy-done.8
  20.7 0.0 copy-done.7
  20.7 0.0 copy-start
  20.7 2.2 %copy-done = bf16[1,64,16,16,128]{4,3,2,1,0:T(8,128)(2,1)S(1)} copy-done((bf16[1,64,16,16,128]{4,3,2,1,0:T(8,128)(2,1)S(1)}, bf16[1,64,16,16,128]{4,3,2,1,0:T(8,128)(2,1)}, u32[]{:S(2)}) %copy-start) | copy-done | bytes 4194328
  22.9 0.9 copy-done.4
  23.8 26.0 %shard_map.138 = (f32[64,512]{1,0:T(8,128)S(1)}, f32[64,128]{1,0:T(8,128)S(1)}, f32[64,512]{1,0:T(8,128)S(1)}, f32[72,128]{1,0:T(8,128)S(1)}, f32[8,128]{1,0:T(8...) custom-call(s32[4]{0:T(128)S(1)} %pad_add_fusion.meta, s32[8]{0:T(128)S(1)} %bitcast.57, ...), custom_call_target="tpu_custom_call" | custom-call | tf_op jit(solution)/shard_map/pallas_call | solution.py:491
  49.7 8.8 %collective-permute-done.3.halo_pair = bf16[64,4,16,128]{3,2,1,0:T(8,128)(2,1)S(1)} collective-permute-done((bf16[64,4,16,128]{3,2,1,0:T(8,128)(2,1)S(1)}, bf16[64,4,16,128]{3,2,1,0:T(8,128)(2,1)S(1)}, u32[]{:S(2)}, u32[]{:S(2)}) %collective-permute-start.3) | collective-permute-done | bytes 1048608 | tf_op jit(solution)/shard_map/ppermute | solution.py:30
  58.5 0.0 collective-permute-done.4.halo_cross
  58.5 0.0 copy-done.6
  58.5 11.2 %shard_map.139 = (f32[256,128]{1,0:T(8,128)S(1)}, f32[8,136,128]{2,1,0:T(8,128)S(1)}) custom-call(s32[4]{0:T(128)S(1)} %pad_add_fusion.meta, s32[1]{0:T(128)} %get-tuple-element.30.begin_in, s32[8]{0:T(128)S(1)} %bitcast.58, s32[8,64]{1,0:T(8,128)S(1)} %bitcast.56, bf16[64,4,16,128]{3,2,1,0:T(8,128)(2,1)S(1)} %get-tuple-element.31.own, ...), custom_call_target="tpu_custom_call" | custom-call | tf_op jit(solution)/shard_map/pallas_call | solution.py:525
  69.8 0.1 collective-permute-start.5
  69.9 1.5 %collective-permute-done.5 = f32[4,136,128]{2,1,0:T(8,128)S(1)} collective-permute-done((f32[4,136,128]{2,1,0:T(8,128)S(1)}, f32[4,136,128]{2,1,0:T(8,128)S(1)}, u32[]{:S(2)}, u32[]{:S(2)}) %collective-permute-start.5) | collective-permute-done | bytes 278560 | tf_op jit(solution)/shard_map/ppermute | solution.py:30
  71.5 1.4 %collective-permute-start.6 = (f32[2,136,128]{2,1,0:T(8,128)S(1)}, f32[2,136,128]{2,1,0:T(8,128)S(1)}, u32[]{:S(2)}, u32[]{:S(2)}) collective-permute-start(f32[2,136,128]{2,1,0:T(8,128)S(1)} %slice.75), channel_id=1, source_target_pairs={{0,16},{8,24},{16,0},{24,8},{1,17},{9,25},{17,1},{25,9},{2,18},{10... | collective-permute-start | bytes 417800 | tf_op jit(solution)/shard_map/ppermute | solution.py:30
  72.9 4.4 %collective-permute-done.6 = f32[2,136,128]{2,1,0:T(8,128)S(1)} collective-permute-done((f32[2,136,128]{2,1,0:T(8,128)S(1)}, f32[2,136,128]{2,1,0:T(8,128)S(1)}, u32[]{:S(2)}, u32[]{:S(2)}) %collective-permute-start.6) | collective-permute-done | bytes 139296 | tf_op jit(solution)/shard_map/ppermute | solution.py:30
  77.3 5.3 %collective-permute-start.7 = (f32[264,128]{1,0:T(8,128)S(1)}, f32[264,128]{1,0:T(8,128)S(1)}, u32[]{:S(2)}, u32[]{:S(2)}) collective-permute-start(f32[264,128]{1,0:T(8,128)S(1)} %pad_maximum_fusion.2), channel_id=1, source_target_pairs={{0,1},{1,0},{2,3},{3,2},{4,5},{5,4},{6,7},{7,6},{8,9},{9,8},{10,11... | collective-permute-start | bytes 405512 | tf_op jit(solution)/shard_map/ppermute | solution.py:30
  82.7 3.1 %collective-permute-done.7 = f32[264,128]{1,0:T(8,128)S(1)} collective-permute-done((f32[264,128]{1,0:T(8,128)S(1)}, f32[264,128]{1,0:T(8,128)S(1)}, u32[]{:S(2)}, u32[]{:S(2)}) %collective-permute-start.7) | collective-permute-done | bytes 135200 | tf_op jit(solution)/shard_map/ppermute | solution.py:30
  85.8 0.3 collective-permute-start.8
  86.0 4.5 %collective-permute-done.8 = f32[200,128]{1,0:T(8,128)S(1)} collective-permute-done((f32[200,128]{1,0:T(8,128)S(1)}, f32[200,128]{1,0:T(8,128)S(1)}, u32[]{:S(2)}, u32[]{:S(2)}) %collective-permute-start.8) | collective-permute-done | bytes 102432 | tf_op jit(solution)/shard_map/ppermute | solution.py:30
  90.6 0.5 collective-permute-start.9
  91.0 5.5 %collective-permute-done.9 = f32[168,128]{1,0:T(8,128)S(1)} collective-permute-done((f32[168,128]{1,0:T(8,128)S(1)}, f32[168,128]{1,0:T(8,128)S(1)}, u32[]{:S(2)}, u32[]{:S(2)}) %collective-permute-start.9) | collective-permute-done | bytes 86048 | tf_op jit(solution)/shard_map/ppermute | solution.py:30
  96.6 1.8 %collective-permute-start.10 = (f32[1,136,128]{2,1,0:T(8,128)S(1)}, f32[1,136,128]{2,1,0:T(8,128)S(1)}, u32[]{:S(2)}, u32[]{:S(2)}) collective-permute-start(f32[1,136,128]{2,1,0:T(8,128)S(1)} %fusion), channel_id=1, source_target_pairs={{0,1},{1,0},{2,3},{3,2},{4,5},{5,4},{6,7},{7,6},{8,9},{9,8},{10,11... | collective-permute-start | bytes 208904 | tf_op jit(solution)/shard_map/ppermute | solution.py:30
  98.4 2.5 %collective-permute-done.10 = f32[1,136,128]{2,1,0:T(8,128)S(1)} collective-permute-done((f32[1,136,128]{2,1,0:T(8,128)S(1)}, f32[1,136,128]{2,1,0:T(8,128)S(1)}, u32[]{:S(2)}, u32[]{:S(2)}) %collective-permute-start.10) | collective-permute-done | bytes 69664 | tf_op jit(solution)/shard_map/ppermute | solution.py:30
  101.0 1.6 %collective-permute-start.11 = (f32[2,136,128]{2,1,0:T(8,128)S(1)}, f32[2,136,128]{2,1,0:T(8,128)S(1)}, u32[]{:S(2)}, u32[]{:S(2)}) collective-permute-start(f32[2,136,128]{2,1,0:T(8,128)S(1)} %pad_maximum_fusion.1), channel_id=1, source_target_pairs={{0,16},{8,24},{16,0},{24,8},{1,17},{9,25},{17,1},{25,9},{2,18},{10... | collective-permute-start | bytes 417800 | tf_op jit(solution)/shard_map/ppermute | solution.py:30
  102.6 3.5 %collective-permute-done.11 = f32[2,136,128]{2,1,0:T(8,128)S(1)} collective-permute-done((f32[2,136,128]{2,1,0:T(8,128)S(1)}, f32[2,136,128]{2,1,0:T(8,128)S(1)}, u32[]{:S(2)}, u32[]{:S(2)}) %collective-permute-start.11) | collective-permute-done | bytes 139296 | tf_op jit(solution)/shard_map/ppermute | solution.py:30
  106.1 0.1 collective-permute-start.12
  106.2 0.6 fusion.2
  106.8 0.9 collective-permute-done.12.far
  107.7 1.4 %shard_map.140 = (f32[9,128]{1,0:T(8,128)}, f32[1,128]{1,0:T(1,128)}, f32[128,512]{1,0:T(8,128)}, f32[512,128]{1,0:T(8,128)}) custom-call(s32[4]{0:T(128)S(1)} %pad_add_fusion.meta, f32[4,136,128]{2,1,0:T(8,128)S(1)} %pad_maximum_fusion.near, f32[4,136,128]{2,1,0:T(8,128)S(1)} %collective-permute-done.12.far), custom_call_target="tpu_custom_call" | custom-call | tf_op jit(solution)/shard_map/pallas_call | solution.py:584
  (25 shorter events, 0.3 us)
Async XLA Ops:
  0.6 20.0 %copy-start.2 = (bf16[512,128]{1,0:T(8,128)(2,1)S(1)}, bf16[512,128]{1,0:T(8,128)(2,1)}, u32[]{:S(2)}) copy-start(bf16[512,128]{1,0:T(8,128)(2,1)} %w_out.1) | copy-start | bytes 393220
  0.6 20.0 %copy-start.1 = (bf16[128,512]{1,0:T(8,128)(2,1)S(1)}, bf16[128,512]{1,0:T(8,128)(2,1)}, u32[]{:S(2)}) copy-start(bf16[128,512]{1,0:T(8,128)(2,1)} %w_in.3) | copy-start | bytes 393220
  0.7 20.0 %copy-start.5 = (bf16[9,128]{1,0:T(8,128)(2,1)S(1)}, bf16[9,128]{1,0:T(8,128)(2,1)}, u32[]{:S(2)}) copy-start(bf16[9,128]{1,0:T(8,128)(2,1)} %kern.3) | copy-start | bytes 6916
  0.7 20.0 %copy-start.8 = (f32[128]{0:T(128)S(1)}, f32[128]{0:T(128)}, u32[]{:S(2)}) copy-start(f32[128]{0:T(128)} %param.16) | copy-start | bytes 1540
  0.7 20.0 %copy-start.7 = (s32[1,8]{1,0:T(1,128)S(1)}, s32[1,8]{1,0:T(1,128)}, u32[]{:S(2)}) copy-start(s32[1,8]{1,0:T(1,128)} %param.13) | copy-start | bytes 100
  2.1 6.1 %collective-permute-start = (f32[1,40,128]{2,1,0:T(8,128)S(1)}, f32[1,40,128]{2,1,0:T(8,128)S(1)}, u32[]{:S(2)}, u32[]{:S(2)}) collective-permute-start(f32[1,40,128]{2,1,0:T(8,128)S(1)} %pad_bitcast_fusion), channel_id=1, source_target_pairs={{0,1},{1,0},{2,3},{3,2},{4,5},{5,4},{6,7},{7,6},{8,9},{9,8},{10,11... | collective-permute-start | bytes 61448 | tf_op jit(solution)/shard_map/ppermute | solution.py:30
  5.1 53.5 %copy-start.6 = (s32[1,64,8]{1,2,0:T(8,128)S(1)}, s32[1,64,8]{1,2,0:T(8,128)}, u32[]{:S(2)}) copy-start(s32[1,64,8]{1,2,0:T(8,128)} %param.12) | copy-start | bytes 6148
  8.2 4.1 %collective-permute-start.1 = (f32[2,40,128]{2,1,0:T(8,128)S(1)}, f32[2,40,128]{2,1,0:T(8,128)S(1)}, u32[]{:S(2)}, u32[]{:S(2)}) collective-permute-start(f32[2,40,128]{2,1,0:T(8,128)S(1)} %pad_maximum_fusion.6), channel_id=1, source_target_pairs={{0,2},{1,3},{2,0},{3,1},{4,6},{5,7},{6,4},{7,5},{8,10},{9,11},{10,... | collective-permute-start | bytes 122888 | tf_op jit(solution)/shard_map/ppermute | solution.py:30
  12.3 5.3 %collective-permute-start.2 = (f32[4,40,128]{2,1,0:T(8,128)S(1)}, f32[4,40,128]{2,1,0:T(8,128)S(1)}, u32[]{:S(2)}, u32[]{:S(2)}) collective-permute-start(f32[4,40,128]{2,1,0:T(8,128)S(1)} %pad_maximum_fusion.5), channel_id=1, source_target_pairs={{0,4},{1,5},{2,6},{3,7},{4,0},{5,1},{6,2},{7,3},{8,12},{9,13},{10,... | collective-permute-start | bytes 245768 | tf_op jit(solution)/shard_map/ppermute | solution.py:30
  14.8 43.7 %collective-permute-start.3 = (bf16[64,4,16,128]{3,2,1,0:T(8,128)(2,1)S(1)}, bf16[64,4,16,128]{3,2,1,0:T(8,128)(2,1)S(1)}, u32[]{:S(2)}, u32[]{:S(2)}) collective-permute-start(bf16[64,4,16,128]{3,2,1,0:T(8,128)(2,1)S(1)} %get-tuple-element.31.own), channel_id=1, source_target_pairs={{0,1},{1,0},{2,3},{3,2},{4,5},{5,4},{6,7},{7,6},{8,9},{9,8},{10,11... | collective-permute-start | bytes 3145736 | tf_op jit(solution)/shard_map/ppermute | solution.py:30
  17.6 0.6 copy-start.3
  18.2 40.3 %collective-permute-start.4 = (bf16[64,4,16,128]{3,2,1,0:T(8,128)(2,1)S(1)}, bf16[64,4,16,128]{3,2,1,0:T(8,128)(2,1)}, u32[]{:S(2)}, u32[]{:S(2)}) collective-permute-start(bf16[64,4,16,128]{3,2,1,0:T(8,128)(2,1)S(1)} %get-tuple-element.31.own), channel_id=1, source_target_pairs={{1,2},{3,4},{5,6},{2,1},{4,3},{6,5},{9,10},{11,12},{13,14},{10,9},... | collective-permute-start | bytes 3145736 | tf_op jit(solution)/shard_map/ppermute | solution.py:476
  20.7 2.2 %copy-start = (bf16[1,64,16,16,128]{4,3,2,1,0:T(8,128)(2,1)S(1)}, bf16[1,64,16,16,128]{4,3,2,1,0:T(8,128)(2,1)}, u32[]{:S(2)}) copy-start(bf16[1,64,16,16,128]{4,3,2,1,0:T(8,128)(2,1)} %param.10) | copy-start | bytes 12582916
  22.9 0.9 copy-start.4
  69.8 1.6 %collective-permute-start.5 = (f32[4,136,128]{2,1,0:T(8,128)S(1)}, f32[4,136,128]{2,1,0:T(8,128)S(1)}, u32[]{:S(2)}, u32[]{:S(2)}) collective-permute-start(f32[4,136,128]{2,1,0:T(8,128)S(1)} %slice.57), channel_id=1, source_target_pairs={{0,8},{8,0},{16,24},{24,16},{1,9},{9,1},{17,25},{25,17},{2,10},{10... | collective-permute-start | bytes 835592 | tf_op jit(solution)/shard_map/ppermute | solution.py:30
  71.5 5.8 %collective-permute-start.6 = (f32[2,136,128]{2,1,0:T(8,128)S(1)}, f32[2,136,128]{2,1,0:T(8,128)S(1)}, u32[]{:S(2)}, u32[]{:S(2)}) collective-permute-start(f32[2,136,128]{2,1,0:T(8,128)S(1)} %slice.75), channel_id=1, source_target_pairs={{0,16},{8,24},{16,0},{24,8},{1,17},{9,25},{17,1},{25,9},{2,18},{10... | collective-permute-start | bytes 417800 | tf_op jit(solution)/shard_map/ppermute | solution.py:30
  77.3 8.4 %collective-permute-start.7 = (f32[264,128]{1,0:T(8,128)S(1)}, f32[264,128]{1,0:T(8,128)S(1)}, u32[]{:S(2)}, u32[]{:S(2)}) collective-permute-start(f32[264,128]{1,0:T(8,128)S(1)} %pad_maximum_fusion.2), channel_id=1, source_target_pairs={{0,1},{1,0},{2,3},{3,2},{4,5},{5,4},{6,7},{7,6},{8,9},{9,8},{10,11... | collective-permute-start | bytes 405512 | tf_op jit(solution)/shard_map/ppermute | solution.py:30
  85.8 4.7 %collective-permute-start.8 = (f32[200,128]{1,0:T(8,128)S(1)}, f32[200,128]{1,0:T(8,128)S(1)}, u32[]{:S(2)}, u32[]{:S(2)}) collective-permute-start(f32[200,128]{1,0:T(8,128)S(1)} %pad_maximum_fusion.3), channel_id=1, source_target_pairs={{0,2},{1,3},{2,0},{3,1},{4,6},{5,7},{6,4},{7,5},{8,10},{9,11},{10,... | collective-permute-start | bytes 307208 | tf_op jit(solution)/shard_map/ppermute | solution.py:30
  90.6 6.0 %collective-permute-start.9 = (f32[168,128]{1,0:T(8,128)S(1)}, f32[168,128]{1,0:T(8,128)S(1)}, u32[]{:S(2)}, u32[]{:S(2)}) collective-permute-start(f32[168,128]{1,0:T(8,128)S(1)} %pad_maximum_fusion.4), channel_id=1, source_target_pairs={{0,4},{1,5},{2,6},{3,7},{4,0},{5,1},{6,2},{7,3},{8,12},{9,13},{10,... | collective-permute-start | bytes 258056 | tf_op jit(solution)/shard_map/ppermute | solution.py:30
  96.6 4.4 %collective-permute-start.10 = (f32[1,136,128]{2,1,0:T(8,128)S(1)}, f32[1,136,128]{2,1,0:T(8,128)S(1)}, u32[]{:S(2)}, u32[]{:S(2)}) collective-permute-start(f32[1,136,128]{2,1,0:T(8,128)S(1)} %fusion), channel_id=1, source_target_pairs={{0,1},{1,0},{2,3},{3,2},{4,5},{5,4},{6,7},{7,6},{8,9},{9,8},{10,11... | collective-permute-start | bytes 208904 | tf_op jit(solution)/shard_map/ppermute | solution.py:30
  101.0 5.1 %collective-permute-start.11 = (f32[2,136,128]{2,1,0:T(8,128)S(1)}, f32[2,136,128]{2,1,0:T(8,128)S(1)}, u32[]{:S(2)}, u32[]{:S(2)}) collective-permute-start(f32[2,136,128]{2,1,0:T(8,128)S(1)} %pad_maximum_fusion.1), channel_id=1, source_target_pairs={{0,16},{8,24},{16,0},{24,8},{1,17},{9,25},{17,1},{25,9},{2,18},{10... | collective-permute-start | bytes 417800 | tf_op jit(solution)/shard_map/ppermute | solution.py:30
  106.1 1.6 %collective-permute-start.12 = (f32[4,136,128]{2,1,0:T(8,128)S(1)}, f32[4,136,128]{2,1,0:T(8,128)S(1)}, u32[]{:S(2)}, u32[]{:S(2)}) collective-permute-start(f32[4,136,128]{2,1,0:T(8,128)S(1)} %pad_maximum_fusion.near), channel_id=1, source_target_pairs={{0,8},{8,0},{16,24},{24,16},{1,9},{9,1},{17,25},{25,17},{2,10},{10... | collective-permute-start | bytes 835592 | tf_op jit(solution)/shard_map/ppermute | solution.py:30
